TPU v7x, 32 devices: a whole 2x2x4 slice. The times are simulated.
32 devices in a mesh: leaf: 16 (over z, y, core), blk: 2 (over x).
Axes of the slice: x: 2, y: 2, z: 4, core: 2. Of those that a mesh axis runs over, the one named last changes fastest.
Arguments:
- sample: float32 [3, 28672, 512], P(None, ('leaf', 'blk')), may hold values from -6 to 6
- probes: float32 [3, 28672, 512], P(None, ('leaf', 'blk')), may hold values from -0.09375 to 0.09375
- skeleton_rows: int32 [14, 128], replicated, may hold values from 0 to 14335, as said below
Outputs:
- interpolants: float32 [3, 28672, 128], P(None, ('leaf', 'blk'))
- coupling: float32 [3, 16, 128, 128], P(None, 'leaf')
Inputs may be any that keep to these rules, and one draw needn't show every extreme that they name: `skeleton_rows`: list 2^(l+1) - 2 + j belongs to node j of level l; it holds 128 distinct row indices counted from the node's first row, below 28672 / 2^(l+1); its first entry is always 0 and its last entry is always the node's last row.
All inputs are finite; a program needn't handle non-finite values.
Results may differ from a plain program's by a relative error of at most 0.0003.
Values sent between devices are 32-bit elements; how exact they have to be, the bound alone decides.
No kernel may reach another device: no remote copies, remote signals or barrier semaphores. Data moves between devices by JAX's collectives and lax.ppermute only.
A program may use at most 128 MiB of HBM per device.

v0:
```python
import functools
import math

import jax
import jax.numpy as jnp
from jax import lax
from jax.experimental import pallas as pl
from jax.experimental.pallas import tpu as pltpu
from jax.sharding import PartitionSpec as P

ridge_term = 0.05
AXES = ("n0", "n1", "n2", "mid", "core", "blk")
TILE = 8
WIDTH = 128
VMEM = pl.BlockSpec(memory_space=pltpu.VMEM)
SMEM = pl.BlockSpec(memory_space=pltpu.SMEM)
ANY = pl.BlockSpec(memory_space=pltpu.HBM)
BIG = pltpu.CompilerParams(vmem_limit_bytes=49 * 1024 * 1024)


def arr(*shape):
    return jax.ShapeDtypeStruct(shape, jnp.float32)


def cost(flops, bytes_accessed):
    return pl.CostEstimate(flops=flops, bytes_accessed=bytes_accessed, transcendentals=0)


def split(block):
    high = block.astype(jnp.bfloat16)
    low = (block - high.astype(jnp.float32)).astype(jnp.bfloat16)
    return high, low


def plain_dot(left_side, right_side, left_dim, right_dim):
    return lax.dot_general(
        left_side, right_side, (((left_dim,), (right_dim,)), ((), ())), preferred_element_type=jnp.float32
    )


def dot3(left_side, right_side, left_dim=1, right_dim=0):
    left_high, left_low = split(left_side)
    right_high, right_low = split(right_side)
    return (
        plain_dot(left_high, right_high, left_dim, right_dim)
        + plain_dot(left_high, right_low, left_dim, right_dim)
        + plain_dot(left_low, right_high, left_dim, right_dim)
    )


def dot6(left_side, right_side, left_dim=1, right_dim=0):
    return lax.dot_general(
        left_side,
        right_side,
        (((left_dim,), (right_dim,)), ((), ())),
        precision=lax.Precision.HIGHEST,
        preferred_element_type=jnp.float32,
    )


def inverse_of(matrix):
    size = matrix.shape[0]
    count = size // TILE
    wide = 4
    shape = (TILE, size)
    lane = lax.broadcasted_iota(jnp.int32, shape, 1)
    sub = lax.broadcasted_iota(jnp.int32, shape, 0)

    def over_lanes(block, at):
        return jnp.broadcast_to(block[:, at:at + 1], shape)

    def over_subs(block, at):
        return jnp.broadcast_to(block[at:at + 1, :], shape)

    rows = [matrix[TILE * i:TILE * (i + 1), :] for i in range(count)]
    diagonal = [jnp.where(lane - TILE * i == sub, rows[i], 0.0) for i in range(count)]
    along = jnp.broadcast_to(lax.rsqrt(sum(diagonal).sum(axis=0, keepdims=True)), shape)
    down = [jnp.broadcast_to(lax.rsqrt(block.sum(axis=1, keepdims=True)), shape) for block in diagonal]
    rows = [rows[i] * down[i] * along for i in range(count)]
    for panel_at in range(0, count, wide):
        inside = range(panel_at, panel_at + wide)
        for k in inside:
            first = TILE * k
            in_block = (lane >= first) & (lane < first + TILE)
            cols = [over_lanes(rows[k], first + j) for j in range(TILE)]
            panel = jnp.where(in_block, jnp.where(lane - first == sub, 1.0, 0.0), rows[k])
            for j in range(0, TILE, 2):
                one, two = cols[j], cols[j + 1]
                a, b = over_subs(one, j), over_subs(two, j)
                c, d = over_subs(one, j + 1), over_subs(two, j + 1)
                factor = 1.0 / (a * d - b * c)

                def step(block):
                    top, bottom = over_subs(block, j), over_subs(block, j + 1)
                    new_top = d * top - b * bottom
                    new_bottom = a * bottom - c * top
                    others = one * new_top + two * new_bottom
                    kept = jnp.where((sub == j) | (sub == j + 1), 0.0, block)
                    change = jnp.where(sub == j, -new_top, jnp.where(sub == j + 1, -new_bottom, others))
                    return kept - change * factor

                panel = step(panel)
                for m in range(j + 2, TILE):
                    cols[m] = step(cols[m])
            spread_rows = [over_subs(panel, j) for j in range(TILE)]
            for i in inside:
                if i != k:
                    block = rows[i]
                    total = jnp.where(in_block, 0.0, block)
                    for j in range(TILE):
                        total = total - over_lanes(block, first + j) * spread_rows[j]
                    rows[i] = total
            rows[k] = panel
        first, last = TILE * panel_at, TILE * (panel_at + wide)
        in_panel = (lane >= first) & (lane < last)
        zero = jnp.zeros(shape, jnp.float32)
        solved = jnp.concatenate([rows[i] if i in inside else zero for i in range(count)], axis=0)
        ahead = [(panel_at + wide + i) % count for i in range(wide)]
        later = [i for i in range(count) if i not in inside and i not in ahead]
        for chosen in (ahead, later):
            factors = jnp.concatenate([jnp.where(in_panel, rows[i], 0.0) for i in chosen], axis=0)
            change = dot6(factors, solved)
            for at, i in enumerate(chosen):
                rows[i] = jnp.where(in_panel, 0.0, rows[i]) - change[TILE * at:TILE * (at + 1), :]
    return jnp.concatenate([rows[i] * down[i] * along for i in range(count)], axis=0)


def invert_kernel(a_ref, o_ref):
    o_ref[...] = inverse_of(a_ref[...])


def invert(matrix):
    size = matrix.shape[0]
    return pl.pallas_call(
        invert_kernel,
        out_shape=arr(size, size),
        in_specs=[VMEM],
        out_specs=VMEM,
        cost_estimate=cost(4 * 10 ** 9, 8 * size ** 2),
    )(matrix)


def ridge(matrix):
    size = matrix.shape[0]
    row = lax.broadcasted_iota(jnp.int32, (size, size), 0)
    col = lax.broadcasted_iota(jnp.int32, (size, size), 1)
    return matrix + jnp.where(row == col, ridge_term, 0.0)


def split3(block):
    high = block.astype(jnp.bfloat16)
    rest = block - high.astype(jnp.float32)
    middle = rest.astype(jnp.bfloat16)
    return high, middle, (rest - middle.astype(jnp.float32)).astype(jnp.bfloat16)


def marks(list_ref, level, sizes, row_count):
    place = [lax.axis_index(axis) for axis in AXES]
    device = 0
    for index, size in zip(place, sizes):
        device = device * size + index
    node = 0
    for index in place[:level + 1]:
        node = node * 2 + index
    row_total = row_count * math.prod(sizes)
    shift = node * (row_total >> level + 1) - device * row_count
    listed = list_ref[pl.ds(node + (2 ** (level + 1) - 2), 1), :] + shift
    row_ids = lax.broadcasted_iota(jnp.int32, (row_count, listed.shape[1]), 0)
    return jnp.where(row_ids == listed, 1.0, 0.0).astype(jnp.bfloat16)


def taken(mark, parts):
    return sum(plain_dot(mark, part, 0, 0) for part in reversed(parts))


def pick_kernel(wanted, sizes, list_hbm, s_hbm, kept_ref, sent_ref, list_ref, s_buf, sems):
    levels = sorted({level for level, _ in wanted})
    sources = sorted({source for _, source in wanted})
    running = copies(
        [(list_hbm, list_ref)] + [(s_hbm.at[source], s_buf.at[at]) for at, source in enumerate(sources)], sems
    )
    half = kept_ref.shape[1]
    here = lax.axis_index("core") == 0
    running[0].wait()
    mark = {level: marks(list_ref, level, sizes, s_buf.shape[1]) for level in levels}
    for at, source in enumerate(sources):
        running[1 + at].wait()
        parts = split3(s_buf[at])
        for slot, (level, from_source) in enumerate(wanted):
            if from_source == source:
                rows = taken(mark[level], parts)
                kept_ref[slot] = jnp.where(here, rows[:half], rows[half:])
                sent_ref[slot] = jnp.where(here, rows[half:], rows[:half])


def pick(skeleton_rows, sample, wanted, sizes):
    _, row_count, samples = sample.shape
    skel = skeleton_rows.shape[1]
    count = len(wanted)
    sources = len({source for _, source in wanted})
    return pl.pallas_call(
        functools.partial(pick_kernel, wanted, sizes),
        out_shape=[arr(count, skel // 2, samples)] * 2,
        in_specs=[ANY, ANY],
        out_specs=[VMEM] * 2,
        scratch_shapes=[
            pltpu.VMEM(skeleton_rows.shape, jnp.int32),
            pltpu.VMEM((sources, row_count, samples), jnp.float32),
            pltpu.SemaphoreType.DMA((1 + sources,)),
        ],
        compiler_params=BIG,
        cost_estimate=cost(10 ** 9 * count, sources * row_count * samples * 4),
    )(skeleton_rows, sample)


def project(sample_block, skeleton, samples, earlier):
    high, low = split(sample_block)
    total = dot3_halves(high, low, skeleton, 1)
    for basis, tilt in earlier:
        total = total - dot3(basis, tilt)
    return total * (1.0 / samples)


def dot3_halves(high, low, skeleton, right_dim):
    width = skeleton.shape[0]
    right_high, right_low = split(skeleton)
    both = plain_dot(high, jnp.concatenate([right_high, right_low], axis=0), 1, right_dim)
    return both[:, :width] + both[:, width:] + plain_dot(low, right_high, 1, right_dim)


def store_terms(kept_ref, sent_ref, kind, term):
    here = lax.axis_index("core") == 0
    half, width = kept_ref.shape[0], term.shape[0]
    turned = term.T
    lanes = pl.ds(kind * width, width)
    kept_ref[:, lanes] = jnp.where(here, turned[:half], turned[half:])
    sent_ref[:, lanes] = jnp.where(here, turned[half:], turned[:half])


def moments(projected, tests):
    high, low = split(projected)
    test_high, test_low = split(tests)
    return plain_dot(high, test_high, 0, 0) + plain_dot(high, test_low, 0, 0) + plain_dot(low, test_high, 0, 0)


def copies(pairs, sems):
    started = []
    for at, (source, target) in enumerate(pairs):
        copy = pltpu.make_async_copy(source, target, sems.at[at])
        copy.start()
        started.append(copy)
    return started


def ordered(mine_ref, other_ref):
    here = lax.axis_index("core") == 0
    low = jnp.where(here, mine_ref[...], other_ref[...])
    high = jnp.where(here, other_ref[...], mine_ref[...])
    return low, high


def joined(low, high, kind):
    return jnp.concatenate([half[:, kind * WIDTH:(kind + 1) * WIDTH] for half in (low, high)], axis=0)


def whole(mine_ref, other_ref):
    return jnp.concatenate(ordered(mine_ref, other_ref), axis=0)


def whole_rows(low, high, slot):
    return jnp.concatenate([low[slot], high[slot]], axis=0)


def couple(skeleton, moment_t):
    spread = ridge(dot6(moment_t, moment_t, 0, 0))
    cross = dot3(skeleton, moment_t)
    return dot3(cross, inverse_of(spread))


def gram_of(skeleton, samples):
    return ridge(dot6(skeleton, skeleton, 1, 1) * (1.0 / samples))


def first_kernel(mine_ref, other_ref, s_hbm, t_hbm, skel_ref, gram_ref, p_ref, kept_ref, sent_ref, s_buf, t_buf, sems):
    samples = mine_ref.shape[1]
    levels = t_buf.shape[0]
    running = copies([(s_hbm.at[0], s_buf)] + [(t_hbm.at[l], t_buf.at[l]) for l in range(levels)], sems)
    skeleton = whole(mine_ref, other_ref)
    skel_ref[...] = skeleton
    gram_ref[...] = gram_of(skeleton, samples)
    running[0].wait()
    projected = project(s_buf[...], skeleton, samples, [])
    p_ref[...] = projected
    for level in range(levels):
        running[1 + level].wait()
        store_terms(kept_ref, sent_ref, level, moments(projected, t_buf[level]))


def second_kernel(mine_ref, other_ref, ours_ref, rows_mine, rows_other, skel0_ref, p0_ref, s_hbm, t_hbm,
                  c0_ref, e02_ref, skel_ref, tilt_ref, gram_ref, p_ref, kept_ref, sent_ref, s_buf, t_buf, sems):
    samples = skel0_ref.shape[1]
    running = copies([(s_hbm.at[1], s_buf), (t_hbm.at[1], t_buf.at[0]), (t_hbm.at[2], t_buf.at[1])], sems)
    low, high = ordered(mine_ref, other_ref)
    rows_low, rows_high = ordered(rows_mine, rows_other)
    skeleton_0 = skel0_ref[...]
    low_0 = dot3(whole_rows(rows_low, rows_high, 0), skeleton_0, 1, 1) * (1.0 / samples)
    coupling = couple(skeleton_0, joined(low, high, 0))
    c0_ref[...] = coupling
    back = dot3(ours_ref[...], coupling)
    e01 = dot3(back, joined(low, high, 1), 1, 1)
    e02_ref[...] = dot3(back, joined(low, high, 2), 1, 1)
    skeleton = whole_rows(rows_low, rows_high, 1) - dot3(low_0, e01)
    skel_ref[...] = skeleton
    gram_ref[...] = gram_of(skeleton, samples)
    tilt = dot3(e01, skeleton, 1, 1)
    tilt_ref[...] = tilt
    running[0].wait()
    projected = project(s_buf[...], skeleton, samples, [(p0_ref[...], tilt)])
    p_ref[...] = projected
    for kind in range(2):
        running[1 + kind].wait()
        store_terms(kept_ref, sent_ref, kind, moments(projected, t_buf[kind]))


def third_kernel(mine_ref, other_ref, ours_ref, rows_mine, rows_other, skel0_ref, skel1_ref, tilt_in_ref, e02_ref,
                 p0_ref, p1_ref, s_hbm, t_hbm, c1_ref, skel_ref, gram_ref, p_ref, kept_ref, sent_ref, s_buf, t_buf, sems):
    samples = skel1_ref.shape[1]
    share = 1.0 / samples
    running = copies([(s_hbm.at[2], s_buf), (t_hbm.at[2], t_buf)], sems)
    low, high = ordered(mine_ref, other_ref)
    rows_low, rows_high = ordered(rows_mine, rows_other)
    skeleton_1 = skel1_ref[...]
    e02 = e02_ref[...]
    low_0 = dot3(whole_rows(rows_low, rows_high, 0), skel0_ref[...], 1, 1) * share
    low_1 = (dot3(whole_rows(rows_low, rows_high, 1), skeleton_1, 1, 1) - dot3(low_0, tilt_in_ref[...])) * share
    rows = whole_rows(rows_low, rows_high, 2) - dot3(low_0, e02)
    coupling = couple(skeleton_1, joined(low, high, 0))
    c1_ref[...] = coupling
    e12 = dot3(dot3(ours_ref[...], coupling), joined(low, high, 1), 1, 1)
    skeleton = rows - dot3(low_1, e12)
    skel_ref[...] = skeleton
    gram_ref[...] = gram_of(skeleton, samples)
    tilt_0 = dot3(e02, skeleton, 1, 1)
    tilt_1 = dot3(e12, skeleton, 1, 1)
    running[0].wait()
    projected = project(s_buf[...], skeleton, samples, [(p0_ref[...], tilt_0), (p1_ref[...], tilt_1)])
    p_ref[...] = projected
    running[1].wait()
    store_terms(kept_ref, sent_ref, 0, moments(projected, t_buf[...]))


def bases_kernel(*refs):
    levels = len(refs) // 2
    for level in range(levels):
        refs[-1][level] = dot3(refs[level][...], refs[levels + level][...])


def last_kernel(mine_ref, other_ref, skel_ref, c0_ref, c1_ref, out_ref):
    low, high = ordered(mine_ref, other_ref)
    out_ref[0, 0] = c0_ref[...]
    out_ref[1, 0] = c1_ref[...]
    out_ref[2, 0] = couple(skel_ref[...], joined(low, high, 0))


def level_call(kernel, specs, outs, scratch, flops, operands):
    return pl.pallas_call(
        kernel,
        out_shape=outs,
        in_specs=specs,
        out_specs=[VMEM] * len(outs),
        scratch_shapes=scratch,
        compiler_params=BIG,
        cost_estimate=cost(flops, 4 * 10 ** 6),
    )(*operands)


def swap(block, axis):
    return lax.ppermute(block, axis, [(0, 1), (1, 0)])


def chips_of(axes):
    return math.prod(lax.axis_size(axis) for axis in axes)


def to_chunks(stack, count):
    rows, width = stack.shape
    return stack.reshape(count, rows // count, width)


def exchange(pieces, axes):
    return lax.all_to_all(pieces, axes, 0, 0, tiled=True)


def total_over(stack, axes):
    for axis in axes:
        count = lax.axis_size(axis)
        if count == 2:
            stack = stack + swap(stack, axis)
        elif count > 2:
            stack = lax.psum(stack, axis)
    return stack


def held(first, *others):
    return lax.optimization_barrier((first,) + others)


def combine_kernel(plan, pieces_ref, inverse_ref, out_ref):
    inverse = inverse_ref[...]
    for at, (kind, places) in enumerate(plan):
        lanes = slice(kind * WIDTH, (kind + 1) * WIDTH)
        out_ref[at] = dot3(sum(pieces_ref[place, :, lanes] for place in places), inverse)


def combine(pieces, inverse, plan):
    rows = pieces.shape[1]
    return pl.pallas_call(
        functools.partial(combine_kernel, plan),
        out_shape=arr(len(plan), rows, WIDTH),
        in_specs=[VMEM, VMEM],
        out_specs=VMEM,
        cost_estimate=cost(10 ** 8, 10 ** 6),
    )(pieces, inverse)


def fan_kernel(plan, sums_ref, out_ref):
    for place, wanted in enumerate(plan):
        for kind, at in enumerate(wanted):
            out_ref[place, :, kind * WIDTH:(kind + 1) * WIDTH] = sums_ref[at]


def fan_out(sums, plan):
    rows = sums.shape[1]
    return pl.pallas_call(
        functools.partial(fan_kernel, plan),
        out_shape=arr(len(plan), rows, WIDTH * len(plan[0])),
        in_specs=[VMEM],
        out_specs=VMEM,
        cost_estimate=cost(10 ** 6, 10 ** 6),
    )(sums)


def local(sample, probes, skeleton_rows):
    levels, row_count, samples = sample.shape
    skel = skeleton_rows.shape[1]
    sizes = [lax.axis_size(axis) for axis in AXES]
    s_buf = pltpu.VMEM((row_count, samples), jnp.float32)
    square, wide, tall = arr(skel, skel), arr(skel, samples), arr(row_count, skel)

    def t_buf(count):
        return pltpu.VMEM((count, row_count, samples), jnp.float32)

    def sems(count):
        return pltpu.SemaphoreType.DMA((count,))

    def outgoing(kinds):
        return [arr(samples // 2, kinds * skel)] * 2

    chips = [("n1", "n2", "mid", "blk"), ("n2", "mid", "blk"), ("mid", "blk")]
    kept, sent = pick(skeleton_rows, sample, ((0, 0),), sizes)
    half = kept[0] + swap(sent[0], "core")
    half, lists = held(half, skeleton_rows)
    half = total_over(half, ("mid", "blk"))
    rest_kept, rest_sent = pick(lists, sample, ((1, 0), (1, 1)), sizes)
    half = total_over(half, ("n2", "n1"))
    rest = rest_kept + swap(rest_sent, "core")
    rest = total_over(rest, ("mid", "blk"))

    skeleton_0, gram, projected_0, kept, sent = level_call(
        first_kernel,
        [VMEM] * 2 + [ANY, ANY],
        [wide, square, tall] + outgoing(levels),
        [s_buf, t_buf(levels), sems(1 + levels)],
        3 * 10 ** 9,
        (half, swap(half, "core"), sample, probes),
    )
    sent, rest = held(sent, rest)
    terms = kept + swap(sent, "core")
    inverse_0 = invert(gram)
    rows_one = total_over(rest, ("n2",))
    pieces = exchange(to_chunks(terms, chips_of(chips[0])), chips[0])
    pieces, inverse_0 = held(pieces, inverse_0)
    inner = chips_of(chips[2])
    places = [(one, two) for one in range(2) for two in range(2) for _ in range(inner)]
    every = range(len(places))
    plan = [(0, list(every))]
    plan += [(1, [at for at in every if places[at][0] == one]) for one in range(2)]
    plan += [(2, [at for at in every if places[at][1] == two]) for two in range(2)]
    sums = swap(combine(pieces, inverse_0, plan), "n0")
    sums, lists, rows_one = held(sums, skeleton_rows, rows_one)
    rest_kept, rest_sent = pick(lists, sample, ((2, 0), (2, 1), (2, 2)), sizes)
    mine = exchange(fan_out(sums, [(0, 2 - one, 4 - two) for one, two in places]), chips[0])
    mine = mine.reshape(samples // 2, levels * skel)
    mine, rest_kept, rest_sent = held(mine, rest_kept, rest_sent)
    other = swap(mine, "core")
    rest = rest_kept + swap(rest_sent, "core")

    coupling_0, e02, skeleton_1, tilt, gram, projected_1, kept, sent = level_call(
        second_kernel,
        [VMEM] * 7 + [ANY, ANY],
        [square, wide, wide, square, square, tall] + outgoing(2),
        [s_buf, t_buf(2), sems(3)],
        8 * 10 ** 9,
        (mine, other, inverse_0, rows_one, swap(rows_one, "core"), skeleton_0, projected_0, sample, probes),
    )
    sent, rest = held(sent, rest)
    terms = kept + swap(sent, "core")
    inverse_1 = invert(gram)
    pieces = exchange(to_chunks(terms, chips_of(chips[1])), chips[1])
    rows_two = total_over(rest, ("mid", "blk"))
    pieces, inverse_1, rows_two = held(pieces, inverse_1, rows_two)
    places = [two for two in range(2) for _ in range(inner)]
    every = range(len(places))
    plan = [(0, list(every))] + [(1, [at for at in every if places[at] == two]) for two in range(2)]
    sums = swap(combine(pieces, inverse_1, plan), "n1")
    mine = exchange(fan_out(sums, [(0, 2 - two) for two in places]), chips[1])
    mine = mine.reshape(samples // 2, 2 * skel)
    other = swap(mine, "core")

    coupling_1, skeleton_2, gram, projected_2, kept, sent = level_call(
        third_kernel,
        [VMEM] * 11 + [ANY, ANY],
        [square, wide, square, tall] + outgoing(1),
        [s_buf, pltpu.VMEM((row_count, samples), jnp.float32), sems(2)],
        8 * 10 ** 9,
        (mine, other, inverse_1, rows_two, swap(rows_two, "core"), skeleton_0, skeleton_1, tilt, e02,
         projected_0, projected_1, sample, probes),
    )
    terms = kept + swap(sent, "core")
    terms = total_over(terms, chips[2])
    inverse_2 = invert(gram)
    terms, inverse_2 = held(terms, inverse_2)
    mine = swap(combine(terms[None], inverse_2, [(0, [0])])[0], "n2")
    bases, = level_call(
        bases_kernel, [VMEM] * 6, [arr(levels, row_count, skel)], [], 4 * 10 ** 9,
        (projected_0, projected_1, projected_2, inverse_0, inverse_1, inverse_2),
    )
    mine, bases = held(mine, bases)
    other = swap(mine, "core")
    couplings, = level_call(
        last_kernel, [VMEM] * 5, [arr(levels, 1, skel, skel)], [], 5 * 10 ** 9,
        (mine, other, skeleton_2, coupling_0, coupling_1),
    )
    return bases, couplings


def solution(mesh):
    leaves, blocks = mesh.shape["leaf"], mesh.shape["blk"]
    fine = jax.sharding.Mesh(mesh.devices.reshape(2, 2, 2, leaves // 16, 2, blocks), AXES)
    rows = P(None, AXES, None)
    return jax.shard_map(
        local,
        mesh=fine,
        in_specs=(rows, rows, P()),
        out_specs=(rows, P(None, AXES[:-1], None, None)),
        check_vma=False,
    )
```

profile of v0, /device:TPU:0, one launch (start us, length us, event | category | flops | bytes accessed | tf_op | source)
XLA Modules:
  0.0 146.1 jit_solution(4492364874694933195)
XLA Ops:
  1.3 2.3 %shard_map.50 = (f32[1,64,512]{2,1,0:T(8,128)S(1)}, f32[1,64,512]{2,1,0:T(8,128)S(1)}) custom-call(s32[14,128]{1,0:T(8,128)S(1)} %copy-done.3, f32[3,896,512]{2,1,0:T(8,128)} %s_hbm.11), custom_call_target="tpu_custom_call" | custom-call | flops 1000000000 | bytes 1835008 | tf_op jit(solution)/shard_map/pallas_call | solution.py:201
  5.1 2.9 %collective-permute-start.1 = (f32[64,512]{1,0:T(8,128)S(1)}, f32[64,512]{1,0:T(8,128)S(1)}, u32[]{:S(2)}, u32[]{:S(2)}) collective-permute-start(f32[64,512]{1,0:T(8,128)S(1)} %bitcast_add_fusion), channel_id=1, source_target_pairs={{0,1},{1,0},{2,3},{3,2},{4,5},{5,4},{6,7},{7,6},{8,9},{9,8},{10,11... | collective-permute-start | bytes 393224 | tf_op jit(solution)/shard_map/ppermute | solution.py:378
  8.1 3.0 %shard_map.52 = (f32[2,64,512]{2,1,0:T(8,128)S(1)}, f32[2,64,512]{2,1,0:T(8,128)S(1)}) custom-call(s32[14,128]{1,0:T(8,128)S(1)} %copy-done.3, f32[3,896,512]{2,1,0:T(8,128)} %s_hbm.11), custom_call_target="tpu_custom_call" | custom-call | flops 2000000000 | bytes 3670016 | tf_op jit(solution)/shard_map/pallas_call | solution.py:201
  13.7 3.5 %collective-permute-done.2 = f32[64,512]{1,0:T(8,128)S(1)} collective-permute-done((f32[64,512]{1,0:T(8,128)S(1)}, f32[64,512]{1,0:T(8,128)S(1)}, u32[]{:S(2)}, u32[]{:S(2)}) %collective-permute-start.2) | collective-permute-done | bytes 131104 | tf_op jit(solution)/shard_map/ppermute | solution.py:378
  22.3 3.0 %collective-permute-done.6 = f32[2,64,512]{2,1,0:T(8,128)S(1)} collective-permute-done((f32[2,64,512]{2,1,0:T(8,128)S(1)}, f32[2,64,512]{2,1,0:T(8,128)S(1)}, u32[]{:S(2)}, u32[]{:S(2)}) %collective-permute-start.6) | collective-permute-done | bytes 262176 | tf_op jit(solution)/shard_map/ppermute | solution.py:378
  25.4 4.9 %shard_map.51 = (f32[128,512]{1,0:T(8,128)S(1)}, f32[128,128]{1,0:T(8,128)S(1)}, f32[896,128]{1,0:T(8,128)S(1)}, f32[256,384]{1,0:T(8,128)S(1)}, f32[256,384]{1,0:T(8,128)S(1)}) custom-call(f32[64,512]{1,0:T(8,128)S(1)} %add.42.mine_ref, f32[64,512]{1,0:T(8,128)S(1)} %collective-permute-done.4.other_ref, f32[3,896,512]{2,1,0:T(8,128)} %s_hbm.11, ...), custom_call_target="tpu_custom_call" | custom-call | flops 3000000000 | bytes 4000000 | tf_op jit(solution)/shard_map/pallas_call | solution.py:366
  32.9 3.7 %all-to-all-start = ((f32[8,32,384]{2,1,0:T(8,128)}), f32[8,32,384]{2,1,0:T(8,128)S(1)}, u32[]{:S(2)}, u32[]{:S(2)}) async-start(f32[8,32,384]{2,1,0:T(8,128)} %bitcast.2), calls=%async_computation | async-start | bytes 786432 | tf_op jit(solution)/shard_map/all_to_all | solution.py:391
  38.6 5.6 %shard_map.53.inverse_ref.ours_ref.refs_3_ = f32[128,128]{1,0:T(8,128)} custom-call(f32[128,128]{1,0:T(8,128)} %copy-done.5), custom_call_target="tpu_custom_call" | custom-call | flops 4000000000 | bytes 131072 | tf_op jit(solution)/shard_map/pallas_call | solution.py:134
  47.4 2.6 %collective-permute-start.8 = (f32[5,32,128]{2,1,0:T(8,128)}, f32[5,32,128]{2,1,0:T(8,128)S(1)}, u32[]{:S(2)}, u32[]{:S(2)}) collective-permute-start(f32[5,32,128]{2,1,0:T(8,128)} %shard_map.54), channel_id=1, source_target_pairs={{0,16},{16,0},{1,17},{17,1},{2,18},{18,2},{3,19},{19,3},{4,20},{20... | collective-permute-start | bytes 245768 | tf_op jit(solution)/shard_map/ppermute | solution.py:378
  50.1 3.8 %collective-permute-done.8.sums_ref = f32[5,32,128]{2,1,0:T(8,128)S(1)} collective-permute-done((f32[5,32,128]{2,1,0:T(8,128)}, f32[5,32,128]{2,1,0:T(8,128)S(1)}, u32[]{:S(2)}, u32[]{:S(2)}) %collective-permute-start.8) | collective-permute-done | bytes 81952 | tf_op jit(solution)/shard_map/ppermute | solution.py:378
  56.1 3.6 %all-to-all-start.1 = ((f32[8,32,384]{2,1,0:T(8,128)}), f32[8,32,384]{2,1,0:T(8,128)S(1)}, u32[]{:S(2)}, u32[]{:S(2)}) async-start(f32[8,32,384]{2,1,0:T(8,128)} %shard_map.55), calls=%async_computation.1 | async-start | bytes 786432 | tf_op jit(solution)/shard_map/all_to_all | solution.py:391
  59.8 3.8 %shard_map.56 = (f32[3,64,512]{2,1,0:T(8,128)S(1)}, f32[3,64,512]{2,1,0:T(8,128)S(1)}) custom-call(s32[14,128]{1,0:T(8,128)S(1)} %copy-done.4, f32[3,896,512]{2,1,0:T(8,128)} %s_hbm.11), custom_call_target="tpu_custom_call" | custom-call | flops 3000000000 | bytes 5505024 | tf_op jit(solution)/shard_map/pallas_call | solution.py:201
  63.7 3.0 %all-to-all-done.1 = f32[8,32,384]{2,1,0:T(8,128)S(1)} async-done(((f32[8,32,384]{2,1,0:T(8,128)}), f32[8,32,384]{2,1,0:T(8,128)S(1)}, u32[]{:S(2)}, u32[]{:S(2)}) %all-to-all-start.1) | async-done | bytes 393248 | tf_op jit(solution)/shard_map/all_to_all | solution.py:391
  69.4 10.0 %shard_map.57 = (f32[128,128]{1,0:T(8,128)S(1)}, f32[128,512]{1,0:T(8,128)S(1)}, f32[128,512]{1,0:T(8,128)S(1)}, f32[128,128]{1,0:T(8,128)S(1)}, f32[128,128]{1,...) custom-call(f32[256,384]{1,0:T(8,128)S(1)} %bitcast.10, ...), custom_call_target="tpu_custom_call" | custom-call | flops 8000000000 | bytes 4000000 | tf_op jit(solution)/shard_map/pallas_call | solution.py:366
  81.8 3.4 %all-to-all-start.2 = ((f32[4,64,256]{2,1,0:T(8,128)}), f32[4,64,256]{2,1,0:T(8,128)S(1)}, u32[]{:S(2)}, u32[]{:S(2)}) async-start(f32[4,64,256]{2,1,0:T(8,128)} %bitcast.4), calls=%async_computation.2 | async-start | bytes 524288 | tf_op jit(solution)/shard_map/all_to_all | solution.py:391
  85.2 5.6 %shard_map.58.inverse_ref.ours_ref.refs_4_ = f32[128,128]{1,0:T(8,128)} custom-call(f32[128,128]{1,0:T(8,128)} %copy-done.9), custom_call_target="tpu_custom_call" | custom-call | flops 4000000000 | bytes 131072 | tf_op jit(solution)/shard_map/pallas_call | solution.py:134
  91.6 2.2 %all-to-all-done.2.pieces_ref = f32[4,64,256]{2,1,0:T(8,128)S(1)} async-done(((f32[4,64,256]{2,1,0:T(8,128)}), f32[4,64,256]{2,1,0:T(8,128)S(1)}, u32[]{:S(2)}, u32[]{:S(2)}) %all-to-all-start.2) | async-done | bytes 262176 | tf_op jit(solution)/shard_map/all_to_all | solution.py:391
  97.4 3.8 %collective-permute-done.15.sums_ref = f32[3,64,128]{2,1,0:T(8,128)S(1)} collective-permute-done((f32[3,64,128]{2,1,0:T(8,128)}, f32[3,64,128]{2,1,0:T(8,128)S(1)}, u32[]{:S(2)}, u32[]{:S(2)}) %collective-permute-start.15) | collective-permute-done | bytes 98336 | tf_op jit(solution)/shard_map/ppermute | solution.py:378
  103.4 3.6 %all-to-all-start.3 = ((f32[4,64,256]{2,1,0:T(8,128)}), f32[4,64,256]{2,1,0:T(8,128)S(1)}, u32[]{:S(2)}, u32[]{:S(2)}) async-start(f32[4,64,256]{2,1,0:T(8,128)} %shard_map.60), calls=%async_computation.3 | async-start | bytes 524288 | tf_op jit(solution)/shard_map/all_to_all | solution.py:391
  107.1 5.0 %all-to-all-done.3 = f32[4,64,256]{2,1,0:T(8,128)S(1)} async-done(((f32[4,64,256]{2,1,0:T(8,128)}), f32[4,64,256]{2,1,0:T(8,128)S(1)}, u32[]{:S(2)}, u32[]{:S(2)}) %all-to-all-start.3) | async-done | bytes 262176 | tf_op jit(solution)/shard_map/all_to_all | solution.py:391
  114.5 8.5 %shard_map.61 = (f32[128,128]{1,0:T(8,128)S(1)}, f32[128,512]{1,0:T(8,128)S(1)}, f32[128,128]{1,0:T(8,128)S(1)}, f32[896,128]{1,0:T(8,128)S(1)}, f32[256,128]{1,0:T(8,128)S(1)}, /*index=5*/f32[256,128]{1,0:T(8,128)S(1)}) custom-call(f32[256,256]{1,0:T(8,128)S(1)} %bitcast.12, f32[256,256]{1,0:T(8,128)S(1)} %collective-permute-done.16.other_ref, ...), custom_call_target="tpu_custom_call" | custom-call | flops 8000000000 | bytes 4000000 | tf_op jit(solution)/shard_map/pallas_call | solution.py:366
  125.8 5.6 %shard_map.62.inverse_ref.refs_5_ = f32[128,128]{1,0:T(8,128)} custom-call(f32[128,128]{1,0:T(8,128)} %copy-done.10), custom_call_target="tpu_custom_call" | custom-call | flops 4000000000 | bytes 131072 | tf_op jit(solution)/shard_map/pallas_call | solution.py:134
  137.0 2.3 %collective-permute-done.20.mine_ref = f32[256,128]{1,0:T(8,128)S(1)} collective-permute-done((f32[256,128]{1,0:T(8,128)}, f32[256,128]{1,0:T(8,128)S(1)}, u32[]{:S(2)}, u32[]{:S(2)}) %collective-permute-start.20) | collective-permute-done | bytes 131104 | tf_op jit(solution)/shard_map/ppermute | solution.py:378
  140.7 5.4 %shard_map.65 = f32[3,1,128,128]{3,2,1,0:T(8,128)} custom-call(f32[256,128]{1,0:T(8,128)S(1)} %collective-permute-done.20.mine_ref, f32[256,128]{1,0:T(8,128)S(1)} %collective-permute-done.21.other_ref, f32[128,512]{1,0:T(8,128)S(1)} %copy-done.8, f32[128,128]{1,0:T(8,128)S(1)} %copy-done.12, f32[128,128]{1,0:T(8,128)S(1)} %get-tuple-element.93.c1_ref), custom_call_target="tpu_custom_call" | custom-call | flops 5000000000 | bytes 4000000 | tf_op jit(solution)/shard_map/pallas_call | solution.py:366
  (91 shorter events, 44.0 us)
Async XLA Ops:
  3.6 1.5 %collective-permute-start = (f32[64,512]{1,0:T(8,128)S(1)}, f32[64,512]{1,0:T(8,128)S(1)}, u32[]{:S(2)}, u32[]{:S(2)}) collective-permute-start(f32[64,512]{1,0:T(8,128)S(1)} %bitcast.13), channel_id=1, source_target_pairs={{0,2},{2,0},{1,3},{3,1},{4,6},{6,4},{5,7},{7,5},{8,10},{10,8},{9,1... | collective-permute-start | bytes 393224 | tf_op jit(solution)/shard_map/ppermute | solution.py:378
  5.1 6.7 %collective-permute-start.1 = (f32[64,512]{1,0:T(8,128)S(1)}, f32[64,512]{1,0:T(8,128)S(1)}, u32[]{:S(2)}, u32[]{:S(2)}) collective-permute-start(f32[64,512]{1,0:T(8,128)S(1)} %bitcast_add_fusion), channel_id=1, source_target_pairs={{0,1},{1,0},{2,3},{3,2},{4,5},{5,4},{6,7},{7,6},{8,9},{9,8},{10,11... | collective-permute-start | bytes 393224 | tf_op jit(solution)/shard_map/ppermute | solution.py:378
  11.1 7.7 %collective-permute-start.5 = (f32[2,64,512]{2,1,0:T(8,128)S(1)}, f32[2,64,512]{2,1,0:T(8,128)S(1)}, u32[]{:S(2)}, u32[]{:S(2)}) collective-permute-start(f32[2,64,512]{2,1,0:T(8,128)S(1)} %get-tuple-element.55), channel_id=1, source_target_pairs={{0,2},{2,0},{1,3},{3,1},{4,6},{6,4},{5,7},{7,5},{8,10},{10,8},{9,1... | collective-permute-start | bytes 786440 | tf_op jit(solution)/shard_map/ppermute | solution.py:378
  11.9 5.3 %collective-permute-start.2 = (f32[64,512]{1,0:T(8,128)S(1)}, f32[64,512]{1,0:T(8,128)S(1)}, u32[]{:S(2)}, u32[]{:S(2)}) collective-permute-start(f32[64,512]{1,0:T(8,128)S(1)} %add.40), channel_id=1, source_target_pairs={{0,4},{4,0},{1,5},{5,1},{2,6},{6,2},{3,7},{7,3},{8,12},{12,8},{9,1... | collective-permute-start | bytes 393224 | tf_op jit(solution)/shard_map/ppermute | solution.py:378
  17.2 5.0 %collective-permute-start.3 = (f32[64,512]{1,0:T(8,128)S(1)}, f32[64,512]{1,0:T(8,128)S(1)}, u32[]{:S(2)}, u32[]{:S(2)}) collective-permute-start(f32[64,512]{1,0:T(8,128)S(1)} %add.41), channel_id=1, source_target_pairs={{0,8},{8,0},{1,9},{9,1},{2,10},{10,2},{3,11},{11,3},{4,12},{12,4},... | collective-permute-start | bytes 393224 | tf_op jit(solution)/shard_map/ppermute | solution.py:378
  18.9 6.4 %collective-permute-start.6 = (f32[2,64,512]{2,1,0:T(8,128)S(1)}, f32[2,64,512]{2,1,0:T(8,128)S(1)}, u32[]{:S(2)}, u32[]{:S(2)}) collective-permute-start(f32[2,64,512]{2,1,0:T(8,128)S(1)} %add.43), channel_id=1, source_target_pairs={{0,1},{1,0},{2,3},{3,2},{4,5},{5,4},{6,7},{7,6},{8,9},{9,8},{10,11... | collective-permute-start | bytes 786440 | tf_op jit(solution)/shard_map/ppermute | solution.py:378
  22.3 3.1 %collective-permute-start.4 = (f32[64,512]{1,0:T(8,128)S(1)}, f32[64,512]{1,0:T(8,128)S(1)}, u32[]{:S(2)}, u32[]{:S(2)}) collective-permute-start(f32[64,512]{1,0:T(8,128)S(1)} %add.42.mine_ref), channel_id=1, source_target_pairs={{0,2},{2,0},{1,3},{3,1},{4,6},{6,4},{5,7},{7,5},{8,10},{10,8},{9,1... | collective-permute-start | bytes 393224 | tf_op jit(solution)/shard_map/ppermute | solution.py:378
  30.3 1.8 %collective-permute-start.7 = (f32[256,384]{1,0:T(8,128)S(1)}, f32[256,384]{1,0:T(8,128)S(1)}, u32[]{:S(2)}, u32[]{:S(2)}) collective-permute-start(f32[256,384]{1,0:T(8,128)S(1)} %get-tuple-element.56), channel_id=1, source_target_pairs={{0,2},{2,0},{1,3},{3,1},{4,6},{6,4},{5,7},{7,5},{8,10},{10,8},{9,1... | collective-permute-start | bytes 1179656 | tf_op jit(solution)/shard_map/ppermute | solution.py:378
  32.9 11.9 %all-to-all-start = ((f32[8,32,384]{2,1,0:T(8,128)}), f32[8,32,384]{2,1,0:T(8,128)S(1)}, u32[]{:S(2)}, u32[]{:S(2)}) async-start(f32[8,32,384]{2,1,0:T(8,128)} %bitcast.2), calls=%async_computation | async-start | bytes 786432 | tf_op jit(solution)/shard_map/all_to_all | solution.py:391
  36.6 13.4 %collective-permute-start.9 = (f32[2,64,512]{2,1,0:T(8,128)S(1)}, f32[2,64,512]{2,1,0:T(8,128)S(1)}, u32[]{:S(2)}, u32[]{:S(2)}) collective-permute-start(f32[2,64,512]{2,1,0:T(8,128)S(1)} %add.44), channel_id=1, source_target_pairs={{0,4},{4,0},{1,5},{5,1},{2,6},{6,2},{3,7},{7,3},{8,12},{12,8},{9,1... | collective-permute-start | bytes 786440 | tf_op jit(solution)/shard_map/ppermute | solution.py:378
  47.4 6.4 %collective-permute-start.8 = (f32[5,32,128]{2,1,0:T(8,128)}, f32[5,32,128]{2,1,0:T(8,128)S(1)}, u32[]{:S(2)}, u32[]{:S(2)}) collective-permute-start(f32[5,32,128]{2,1,0:T(8,128)} %shard_map.54), channel_id=1, source_target_pairs={{0,16},{16,0},{1,17},{17,1},{2,18},{18,2},{3,19},{19,3},{4,20},{20... | collective-permute-start | bytes 245768 | tf_op jit(solution)/shard_map/ppermute | solution.py:378
  56.1 10.5 %all-to-all-start.1 = ((f32[8,32,384]{2,1,0:T(8,128)}), f32[8,32,384]{2,1,0:T(8,128)S(1)}, u32[]{:S(2)}, u32[]{:S(2)}) async-start(f32[8,32,384]{2,1,0:T(8,128)} %shard_map.55), calls=%async_computation.1 | async-start | bytes 786432 | tf_op jit(solution)/shard_map/all_to_all | solution.py:391
  66.7 1.7 %collective-permute-start.12 = (f32[3,64,512]{2,1,0:T(8,128)S(1)}, f32[3,64,512]{2,1,0:T(8,128)S(1)}, u32[]{:S(2)}, u32[]{:S(2)}) collective-permute-start(f32[3,64,512]{2,1,0:T(8,128)S(1)} %get-tuple-element.72), channel_id=1, source_target_pairs={{0,2},{2,0},{1,3},{3,1},{4,6},{6,4},{5,7},{7,5},{8,10},{10,8},{9,1... | collective-permute-start | bytes 1179656 | tf_op jit(solution)/shard_map/ppermute | solution.py:378
  66.7 2.7 %collective-permute-start.10 = (f32[256,384]{1,0:T(8,128)S(1)}, f32[256,384]{1,0:T(8,128)S(1)}, u32[]{:S(2)}, u32[]{:S(2)}) collective-permute-start(f32[256,384]{1,0:T(8,128)S(1)} %bitcast.9), channel_id=1, source_target_pairs={{0,2},{2,0},{1,3},{3,1},{4,6},{6,4},{5,7},{7,5},{8,10},{10,8},{9,1... | collective-permute-start | bytes 1179656 | tf_op jit(solution)/shard_map/ppermute | solution.py:378
  67.2 2.1 %collective-permute-start.11 = (f32[2,64,512]{2,1,0:T(8,128)S(1)}, f32[2,64,512]{2,1,0:T(8,128)S(1)}, u32[]{:S(2)}, u32[]{:S(2)}) collective-permute-start(f32[2,64,512]{2,1,0:T(8,128)S(1)} %add.46.rows_mine), channel_id=1, source_target_pairs={{0,2},{2,0},{1,3},{3,1},{4,6},{6,4},{5,7},{7,5},{8,10},{10,8},{9,1... | collective-permute-start | bytes 786440 | tf_op jit(solution)/shard_map/ppermute | solution.py:378
  79.4 1.6 %collective-permute-start.13 = (f32[256,256]{1,0:T(8,128)S(1)}, f32[256,256]{1,0:T(8,128)S(1)}, u32[]{:S(2)}, u32[]{:S(2)}) collective-permute-start(f32[256,256]{1,0:T(8,128)S(1)} %get-tuple-element.73), channel_id=1, source_target_pairs={{0,2},{2,0},{1,3},{3,1},{4,6},{6,4},{5,7},{7,5},{8,10},{10,8},{9,1... | collective-permute-start | bytes 786440 | tf_op jit(solution)/shard_map/ppermute | solution.py:378
  79.6 11.9 %collective-permute-start.14 = (f32[3,64,512]{2,1,0:T(8,128)S(1)}, f32[3,64,512]{2,1,0:T(8,128)S(1)}, u32[]{:S(2)}, u32[]{:S(2)}) collective-permute-start(f32[3,64,512]{2,1,0:T(8,128)S(1)} %add.47), channel_id=1, source_target_pairs={{0,1},{1,0},{2,3},{3,2},{4,5},{5,4},{6,7},{7,6},{8,9},{9,8},{10,11... | collective-permute-start | bytes 1179656 | tf_op jit(solution)/shard_map/ppermute | solution.py:378
  81.8 12.1 %all-to-all-start.2 = ((f32[4,64,256]{2,1,0:T(8,128)}), f32[4,64,256]{2,1,0:T(8,128)S(1)}, u32[]{:S(2)}, u32[]{:S(2)}) async-start(f32[4,64,256]{2,1,0:T(8,128)} %bitcast.4), calls=%async_computation.2 | async-start | bytes 524288 | tf_op jit(solution)/shard_map/all_to_all | solution.py:391
  96.3 4.8 %collective-permute-start.15 = (f32[3,64,128]{2,1,0:T(8,128)}, f32[3,64,128]{2,1,0:T(8,128)S(1)}, u32[]{:S(2)}, u32[]{:S(2)}) collective-permute-start(f32[3,64,128]{2,1,0:T(8,128)} %shard_map.59), channel_id=1, source_target_pairs={{0,8},{8,0},{1,9},{9,1},{2,10},{10,2},{3,11},{11,3},{4,12},{12,4},... | collective-permute-start | bytes 294920 | tf_op jit(solution)/shard_map/ppermute | solution.py:378
  103.4 8.8 %all-to-all-start.3 = ((f32[4,64,256]{2,1,0:T(8,128)}), f32[4,64,256]{2,1,0:T(8,128)S(1)}, u32[]{:S(2)}, u32[]{:S(2)}) async-start(f32[4,64,256]{2,1,0:T(8,128)} %shard_map.60), calls=%async_computation.3 | async-start | bytes 524288 | tf_op jit(solution)/shard_map/all_to_all | solution.py:391
  107.1 5.1 %collective-permute-start.17 = (f32[3,64,512]{2,1,0:T(8,128)S(1)}, f32[3,64,512]{2,1,0:T(8,128)S(1)}, u32[]{:S(2)}, u32[]{:S(2)}) collective-permute-start(f32[3,64,512]{2,1,0:T(8,128)S(1)} %add.49.rows_mine), channel_id=1, source_target_pairs={{0,2},{2,0},{1,3},{3,1},{4,6},{6,4},{5,7},{7,5},{8,10},{10,8},{9,1... | collective-permute-start | bytes 1179656 | tf_op jit(solution)/shard_map/ppermute | solution.py:378
  112.2 1.5 %collective-permute-start.16 = (f32[256,256]{1,0:T(8,128)S(1)}, f32[256,256]{1,0:T(8,128)S(1)}, u32[]{:S(2)}, u32[]{:S(2)}) collective-permute-start(f32[256,256]{1,0:T(8,128)S(1)} %bitcast.11), channel_id=1, source_target_pairs={{0,2},{2,0},{1,3},{3,1},{4,6},{6,4},{5,7},{7,5},{8,10},{10,8},{9,1... | collective-permute-start | bytes 786440 | tf_op jit(solution)/shard_map/ppermute | solution.py:378
  124.5 6.9 %collective-permute-start.19 = (f32[256,128]{1,0:T(8,128)S(1)}, f32[256,128]{1,0:T(8,128)S(1)}, u32[]{:S(2)}, u32[]{:S(2)}) collective-permute-start(f32[256,128]{1,0:T(8,128)S(1)} %add.50), channel_id=1, source_target_pairs={{0,1},{1,0},{2,3},{3,2},{4,5},{5,4},{6,7},{7,6},{8,9},{9,8},{10,11... | collective-permute-start | bytes 393224 | tf_op jit(solution)/shard_map/ppermute | solution.py:378
  133.9 5.5 %collective-permute-start.20 = (f32[256,128]{1,0:T(8,128)}, f32[256,128]{1,0:T(8,128)S(1)}, u32[]{:S(2)}, u32[]{:S(2)}) collective-permute-start(f32[256,128]{1,0:T(8,128)} %bitcast.15), channel_id=1, source_target_pairs={{0,4},{4,0},{1,5},{5,1},{2,6},{6,2},{3,7},{7,3},{8,12},{12,8},{9,1... | collective-permute-start | bytes 393224 | tf_op jit(solution)/shard_map/ppermute | solution.py:378
  (19 other events, 89.1 us)
where the time goes:
time: 147 us; the launch traced here: 146 us
  Pallas kernels  65.2 us (44%)
  waiting for transfers between devices  40.6 us (28%)
  starting transfers between devices  31.8 us (22%)
  local copies, waits for them, and re-layouts  5.14 us (3%)
  other arithmetic  2.5 us (2%)
    pallas_call x5, Pallas kernels, level_call(): pl.pallas_call(kernel, out_shape=outs, in_specs=specs, out_specs=[VMEM] *...  30.6 us
    ppermute x22, waiting for transfers between devices, swap(): return lax.ppermute(block, axis, [(0, 1), (1, 0)])  29.7 us
    ppermute x22, starting transfers between devices, swap(): return lax.ppermute(block, axis, [(0, 1), (1, 0)])  17.4 us
    pallas_call x3, Pallas kernels, invert(): pl.pallas_call(invert_kernel, out_shape=arr(size, size), in_specs=[VMEM],...  16.8 us
    all_to_all x4, starting transfers between devices, exchange(): return lax.all_to_all(pieces, axes, 0, 0, tiled=True)  14.4 us
    all_to_all x4, waiting for transfers between devices, exchange(): return lax.all_to_all(pieces, axes, 0, 0, tiled=True)  10.9 us
    pallas_call x3, Pallas kernels, pick(): pl.pallas_call(functools.partial(pick_kernel, wanted, sizes), out_shape=[...  9.16 us
    pallas_call x3, Pallas kernels, combine(): pl.pallas_call(functools.partial(combine_kernel, plan), out_shape=arr(len...  5.45 us
  transfers between devices with their start and end apart: 26, of which 20 were waited for; matrix products, arithmetic and copies ran while one was open for 1% of the time, Pallas kernels for 19%

commit v1 on v0

--- a/solution.py
+++ b/solution.py
@@ -11,11 +11,13 @@
 ridge_term = 0.05
 AXES = ("n0", "n1", "n2", "mid", "core", "blk")
 TILE = 8
+PANEL = 4
 WIDTH = 128
 VMEM = pl.BlockSpec(memory_space=pltpu.VMEM)
 SMEM = pl.BlockSpec(memory_space=pltpu.SMEM)
 ANY = pl.BlockSpec(memory_space=pltpu.HBM)
 BIG = pltpu.CompilerParams(vmem_limit_bytes=49 * 1024 * 1024)
+SMALL = pltpu.CompilerParams(vmem_limit_bytes=4 * 1024 * 1024)
 
 
 def arr(*shape):
@@ -58,10 +60,26 @@
     )
 
 
+def scales_of(matrix):
+    size = matrix.shape[0]
+    row = lax.broadcasted_iota(jnp.int32, (size, size), 0)
+    col = lax.broadcasted_iota(jnp.int32, (size, size), 1)
+    diagonal = jnp.where(row == col, matrix, 0.0)
+    along = lax.rsqrt(diagonal.sum(axis=0, keepdims=True))
+    down = lax.rsqrt(diagonal.sum(axis=1, keepdims=True))
+    return jnp.broadcast_to(down, matrix.shape) * jnp.broadcast_to(along, matrix.shape)
+
+
 def inverse_of(matrix):
+    scales = scales_of(matrix)
+    panels = matrix.shape[0] // TILE // PANEL
+    return eliminate(matrix * scales, range(panels)) * scales
+
+
+def eliminate(matrix, panels):
     size = matrix.shape[0]
     count = size // TILE
-    wide = 4
+    wide = PANEL
     shape = (TILE, size)
     lane = lax.broadcasted_iota(jnp.int32, shape, 1)
     sub = lax.broadcasted_iota(jnp.int32, shape, 0)
@@ -73,11 +91,7 @@
         return jnp.broadcast_to(block[at:at + 1, :], shape)
 
     rows = [matrix[TILE * i:TILE * (i + 1), :] for i in range(count)]
-    diagonal = [jnp.where(lane - TILE * i == sub, rows[i], 0.0) for i in range(count)]
-    along = jnp.broadcast_to(lax.rsqrt(sum(diagonal).sum(axis=0, keepdims=True)), shape)
-    down = [jnp.broadcast_to(lax.rsqrt(block.sum(axis=1, keepdims=True)), shape) for block in diagonal]
-    rows = [rows[i] * down[i] * along for i in range(count)]
-    for panel_at in range(0, count, wide):
+    for panel_at in [wide * panel for panel in panels]:
         inside = range(panel_at, panel_at + wide)
         for k in inside:
             first = TILE * k
@@ -122,22 +136,31 @@
             change = dot6(factors, solved)
             for at, i in enumerate(chosen):
                 rows[i] = jnp.where(in_panel, 0.0, rows[i]) - change[TILE * at:TILE * (at + 1), :]
-    return jnp.concatenate([rows[i] * down[i] * along for i in range(count)], axis=0)
-
-
-def invert_kernel(a_ref, o_ref):
-    o_ref[...] = inverse_of(a_ref[...])
+    return jnp.concatenate(rows, axis=0)
+
+
+def first_half_kernel(a_ref, o_ref, scales_ref):
+    scales = scales_of(a_ref[...])
+    scales_ref[...] = scales
+    o_ref[...] = eliminate(a_ref[...] * scales, (0, 1))
+
+
+def second_half_kernel(a_ref, scales_ref, o_ref):
+    o_ref[...] = eliminate(a_ref[...], (2, 3)) * scales_ref[...]
 
 
 def invert(matrix):
     size = matrix.shape[0]
+    half = cost(2 * 10 ** 9, 8 * size ** 2)
+    square = arr(size, size)
+    state, scales = pl.pallas_call(
+        first_half_kernel, out_shape=[square] * 2, in_specs=[VMEM], out_specs=[VMEM] * 2,
+        compiler_params=SMALL, cost_estimate=half,
+    )(matrix)
     return pl.pallas_call(
-        invert_kernel,
-        out_shape=arr(size, size),
-        in_specs=[VMEM],
-        out_specs=VMEM,
-        cost_estimate=cost(4 * 10 ** 9, 8 * size ** 2),
-    )(matrix)
+        second_half_kernel, out_shape=square, in_specs=[VMEM] * 2, out_specs=VMEM,
+        compiler_params=SMALL, cost_estimate=half,
+    )(state, scales)
 
 
 def ridge(matrix):
@@ -281,7 +304,8 @@
     return ridge(dot6(skeleton, skeleton, 1, 1) * (1.0 / samples))
 
 
-def first_kernel(mine_ref, other_ref, s_hbm, t_hbm, skel_ref, gram_ref, p_ref, kept_ref, sent_ref, s_buf, t_buf, sems):
+def first_kernel(mine_ref, other_ref, s_hbm, t_hbm, skel_ref, gram_ref, p_hbm, kept_ref, sent_ref,
+                 s_buf, t_buf, p_ref, sems):
     samples = mine_ref.shape[1]
     levels = t_buf.shape[0]
     running = copies([(s_hbm.at[0], s_buf)] + [(t_hbm.at[l], t_buf.at[l]) for l in range(levels)], sems)
@@ -291,15 +315,18 @@
     running[0].wait()
     projected = project(s_buf[...], skeleton, samples, [])
     p_ref[...] = projected
+    leaving = copies([(p_ref, p_hbm)], sems.at[pl.ds(1 + levels, 1)])
     for level in range(levels):
         running[1 + level].wait()
         store_terms(kept_ref, sent_ref, level, moments(projected, t_buf[level]))
-
-
-def second_kernel(mine_ref, other_ref, ours_ref, rows_mine, rows_other, skel0_ref, p0_ref, s_hbm, t_hbm,
-                  c0_ref, e02_ref, skel_ref, tilt_ref, gram_ref, p_ref, kept_ref, sent_ref, s_buf, t_buf, sems):
+    leaving[0].wait()
+
+
+def second_kernel(mine_ref, other_ref, ours_ref, rows_mine, rows_other, skel0_ref, p0_hbm, s_hbm, t_hbm,
+                  c0_ref, e02_ref, skel_ref, tilt_ref, gram_ref, p_hbm, kept_ref, sent_ref,
+                  s_buf, t_buf, p_ref, p0_ref, sems):
     samples = skel0_ref.shape[1]
-    running = copies([(s_hbm.at[1], s_buf), (t_hbm.at[1], t_buf.at[0]), (t_hbm.at[2], t_buf.at[1])], sems)
+    running = copies([(s_hbm.at[1], s_buf), (p0_hbm, p0_ref), (t_hbm.at[1], t_buf.at[0]), (t_hbm.at[2], t_buf.at[1])], sems)
     low, high = ordered(mine_ref, other_ref)
     rows_low, rows_high = ordered(rows_mine, rows_other)
     skeleton_0 = skel0_ref[...]
@@ -315,19 +342,34 @@
     tilt = dot3(e01, skeleton, 1, 1)
     tilt_ref[...] = tilt
     running[0].wait()
+    running[1].wait()
     projected = project(s_buf[...], skeleton, samples, [(p0_ref[...], tilt)])
     p_ref[...] = projected
+    leaving = copies([(p_ref, p_hbm)], sems.at[pl.ds(4, 1)])
     for kind in range(2):
-        running[1 + kind].wait()
+        running[2 + kind].wait()
         store_terms(kept_ref, sent_ref, kind, moments(projected, t_buf[kind]))
-
-
-def third_kernel(mine_ref, other_ref, ours_ref, rows_mine, rows_other, skel0_ref, skel1_ref, tilt_in_ref, e02_ref,
-                 p0_ref, p1_ref, s_hbm, t_hbm, c1_ref, skel_ref, gram_ref, p_ref, kept_ref, sent_ref, s_buf, t_buf, sems):
+    leaving[0].wait()
+
+
+def third_kernel(pieces, *refs):
+    parts, refs = refs[:pieces], refs[pieces:]
+    (ours_ref, rows_mine, rows_other, skel0_ref, skel1_ref, tilt_in_ref, e02_ref, p0_hbm, p1_hbm, s_hbm, t_hbm,
+     c1_ref, skel_ref, gram_ref, p_hbm, kept_ref, sent_ref, s_buf, t_buf, p_ref, p0_ref, p1_ref, sems) = refs
     samples = skel1_ref.shape[1]
     share = 1.0 / samples
-    running = copies([(s_hbm.at[2], s_buf), (t_hbm.at[2], t_buf)], sems)
-    low, high = ordered(mine_ref, other_ref)
+    running = copies([(s_hbm.at[2], s_buf), (p0_hbm, p0_ref), (p1_hbm, p1_ref), (t_hbm.at[2], t_buf)], sems)
+    if pieces == 2:
+        low, high = ordered(*parts)
+    else:
+        first = lax.axis_index("blk") == 0
+        both = [
+            jnp.concatenate([jnp.where(first, one, two), jnp.where(first, two, one)], axis=0)
+            for one, two in ((parts[0][...], parts[1][...]), (parts[2][...], parts[3][...]))
+        ]
+        here = lax.axis_index("core") == 0
+        low = jnp.where(here, both[0], both[1])
+        high = jnp.where(here, both[1], both[0])
     rows_low, rows_high = ordered(rows_mine, rows_other)
     skeleton_1 = skel1_ref[...]
     e02 = e02_ref[...]
@@ -342,17 +384,21 @@
     gram_ref[...] = gram_of(skeleton, samples)
     tilt_0 = dot3(e02, skeleton, 1, 1)
     tilt_1 = dot3(e12, skeleton, 1, 1)
-    running[0].wait()
+    for copy in running[:3]:
+        copy.wait()
     projected = project(s_buf[...], skeleton, samples, [(p0_ref[...], tilt_0), (p1_ref[...], tilt_1)])
     p_ref[...] = projected
-    running[1].wait()
+    leaving = copies([(p_ref, p_hbm)], sems.at[pl.ds(4, 1)])
+    running[3].wait()
     store_terms(kept_ref, sent_ref, 0, moments(projected, t_buf[...]))
-
-
-def bases_kernel(*refs):
-    levels = len(refs) // 2
-    for level in range(levels):
-        refs[-1][level] = dot3(refs[level][...], refs[levels + level][...])
+    leaving[0].wait()
+
+
+def bases_kernel(p0_hbm, p1_hbm, p2_hbm, inverse_0, inverse_1, inverse_2, out_ref, p_buf, sems):
+    running = copies([(source, p_buf.at[at]) for at, source in enumerate((p0_hbm, p1_hbm, p2_hbm))], sems)
+    for level, inverse in enumerate((inverse_0, inverse_1, inverse_2)):
+        running[level].wait()
+        out_ref[level] = dot3(p_buf[level], inverse[...])
 
 
 def last_kernel(mine_ref, other_ref, skel_ref, c0_ref, c1_ref, out_ref):
@@ -362,12 +408,12 @@
     out_ref[2, 0] = couple(skel_ref[...], joined(low, high, 0))
 
 
-def level_call(kernel, specs, outs, scratch, flops, operands):
+def level_call(kernel, specs, outs, scratch, flops, operands, in_hbm=None):
     return pl.pallas_call(
         kernel,
         out_shape=outs,
         in_specs=specs,
-        out_specs=[VMEM] * len(outs),
+        out_specs=[ANY if at == in_hbm else VMEM for at in range(len(outs))],
         scratch_shapes=scratch,
         compiler_params=BIG,
         cost_estimate=cost(flops, 4 * 10 ** 6),
@@ -405,22 +451,45 @@
     return lax.optimization_barrier((first,) + others)
 
 
-def combine_kernel(plan, pieces_ref, inverse_ref, out_ref):
+def combine_kernel(plan, *refs):
+    pieces_refs, inverse_ref, out_ref = refs[:-2], refs[-2], refs[-1]
     inverse = inverse_ref[...]
     for at, (kind, places) in enumerate(plan):
         lanes = slice(kind * WIDTH, (kind + 1) * WIDTH)
-        out_ref[at] = dot3(sum(pieces_ref[place, :, lanes] for place in places), inverse)
+        total = sum(pieces_refs[which][place, :, lanes] for which, place in places)
+        out_ref[at] = dot3(total, inverse)
 
 
 def combine(pieces, inverse, plan):
-    rows = pieces.shape[1]
+    rows = pieces[0].shape[1]
     return pl.pallas_call(
         functools.partial(combine_kernel, plan),
         out_shape=arr(len(plan), rows, WIDTH),
-        in_specs=[VMEM, VMEM],
+        in_specs=[VMEM] * (len(pieces) + 1),
         out_specs=VMEM,
+        compiler_params=SMALL,
         cost_estimate=cost(10 ** 8, 10 ** 6),
-    )(pieces, inverse)
+    )(*pieces, inverse)
+
+
+def add_split_kernel(axis, one_ref, two_ref, kept_ref, sent_ref):
+    total = one_ref[...] + two_ref[...]
+    half = kept_ref.shape[0]
+    first = lax.axis_index(axis) == 0
+    kept_ref[...] = jnp.where(first, total[:half], total[half:])
+    sent_ref[...] = jnp.where(first, total[half:], total[:half])
+
+
+def add_split(one, two, axis):
+    rows, width = one.shape
+    return pl.pallas_call(
+        functools.partial(add_split_kernel, axis),
+        out_shape=[arr(rows // 2, width)] * 2,
+        in_specs=[VMEM] * 2,
+        out_specs=[VMEM] * 2,
+        compiler_params=SMALL,
+        cost_estimate=cost(10 ** 6, 10 ** 6),
+    )(one, two)
 
 
 def fan_kernel(plan, sums_ref, out_ref):
@@ -436,6 +505,7 @@
         out_shape=arr(len(plan), rows, WIDTH * len(plan[0])),
         in_specs=[VMEM],
         out_specs=VMEM,
+        compiler_params=SMALL,
         cost_estimate=cost(10 ** 6, 10 ** 6),
     )(sums)
 
@@ -445,6 +515,7 @@
     skel = skeleton_rows.shape[1]
     sizes = [lax.axis_size(axis) for axis in AXES]
     s_buf = pltpu.VMEM((row_count, samples), jnp.float32)
+    p_buf = pltpu.VMEM((row_count, skel), jnp.float32)
     square, wide, tall = arr(skel, skel), arr(skel, samples), arr(row_count, skel)
 
     def t_buf(count):
@@ -464,18 +535,20 @@
     rest_kept, rest_sent = pick(lists, sample, ((1, 0), (1, 1)), sizes)
     half = total_over(half, ("n2", "n1"))
     rest = rest_kept + swap(rest_sent, "core")
+    half, rest = held(half, rest)
     rest = total_over(rest, ("mid", "blk"))
 
     skeleton_0, gram, projected_0, kept, sent = level_call(
         first_kernel,
         [VMEM] * 2 + [ANY, ANY],
         [wide, square, tall] + outgoing(levels),
-        [s_buf, t_buf(levels), sems(1 + levels)],
+        [s_buf, t_buf(levels), p_buf, sems(2 + levels)],
         3 * 10 ** 9,
         (half, swap(half, "core"), sample, probes),
-    )
-    sent, rest = held(sent, rest)
+        in_hbm=2,
+    )
     terms = kept + swap(sent, "core")
+    terms, rest = held(terms, rest)
     inverse_0 = invert(gram)
     rows_one = total_over(rest, ("n2",))
     pieces = exchange(to_chunks(terms, chips_of(chips[0])), chips[0])
@@ -483,10 +556,10 @@
     inner = chips_of(chips[2])
     places = [(one, two) for one in range(2) for two in range(2) for _ in range(inner)]
     every = range(len(places))
-    plan = [(0, list(every))]
-    plan += [(1, [at for at in every if places[at][0] == one]) for one in range(2)]
-    plan += [(2, [at for at in every if places[at][1] == two]) for two in range(2)]
-    sums = swap(combine(pieces, inverse_0, plan), "n0")
+    plan = [(0, [(0, at) for at in every])]
+    plan += [(1, [(0, at) for at in every if places[at][0] == one]) for one in range(2)]
+    plan += [(2, [(0, at) for at in every if places[at][1] == two]) for two in range(2)]
+    sums = swap(combine([pieces], inverse_0, plan), "n0")
     sums, lists, rows_one = held(sums, skeleton_rows, rows_one)
     rest_kept, rest_sent = pick(lists, sample, ((2, 0), (2, 1), (2, 2)), sizes)
     mine = exchange(fan_out(sums, [(0, 2 - one, 4 - two) for one, two in places]), chips[0])
@@ -494,45 +567,67 @@
     mine, rest_kept, rest_sent = held(mine, rest_kept, rest_sent)
     other = swap(mine, "core")
     rest = rest_kept + swap(rest_sent, "core")
+    mine, other, rest = held(mine, other, rest)
+    rest = total_over(rest, ("mid", "blk"))
 
     coupling_0, e02, skeleton_1, tilt, gram, projected_1, kept, sent = level_call(
         second_kernel,
-        [VMEM] * 7 + [ANY, ANY],
+        [VMEM] * 6 + [ANY] * 3,
         [square, wide, wide, square, square, tall] + outgoing(2),
-        [s_buf, t_buf(2), sems(3)],
+        [s_buf, t_buf(2), p_buf, p_buf, sems(5)],
         8 * 10 ** 9,
         (mine, other, inverse_0, rows_one, swap(rows_one, "core"), skeleton_0, projected_0, sample, probes),
+        in_hbm=5,
     )
     sent, rest = held(sent, rest)
+    sent, rows_two = held(sent, rest)
+    inverse_1 = invert(gram)
+    if chips_of(chips[2]) == 2:
+        kept, sent = add_split(kept, swap(sent, "core"), "blk")
+        terms = kept + swap(sent, "blk")
+        arrived = swap(terms, "n2")
+        arrived, inverse_1 = held(arrived, inverse_1)
+        plan = [(0, [(0, 0), (1, 0)]), (1, [(1, 0)])]
+        sums = swap(combine([terms[None], arrived[None]], inverse_1, plan), "n1")
+        mine = fan_out(sums, [(0, 1)])[0]
+        beside = swap(mine, "blk")
+        parts = (mine, beside, swap(mine, "core"), swap(beside, "core"))
+    else:
+        terms = kept + swap(sent, "core")
+        pieces = exchange(to_chunks(terms, chips_of(chips[1])), chips[1])
+        pieces, inverse_1 = held(pieces, inverse_1)
+        places = [two for two in range(2) for _ in range(inner)]
+        every = range(len(places))
+        plan = [(0, [(0, at) for at in every])]
+        plan += [(1, [(0, at) for at in every if places[at] == two]) for two in range(2)]
+        sums = swap(combine([pieces], inverse_1, plan), "n1")
+        mine = exchange(fan_out(sums, [(0, 2 - two) for two in places]), chips[1])
+        mine = mine.reshape(samples // 2, 2 * skel)
+        parts = (mine, swap(mine, "core"))
+
+    coupling_1, skeleton_2, gram, projected_2, kept, sent = level_call(
+        functools.partial(third_kernel, len(parts)),
+        [VMEM] * (len(parts) + 7) + [ANY] * 4,
+        [square, wide, square, tall] + outgoing(1),
+        [s_buf, pltpu.VMEM((row_count, samples), jnp.float32), p_buf, p_buf, p_buf, sems(5)],
+        8 * 10 ** 9,
+        parts + (inverse_1, rows_two, swap(rows_two, "core"), skeleton_0, skeleton_1, tilt, e02,
+                 projected_0, projected_1, sample, probes),
+        in_hbm=3,
+    )
+    inverse_2 = invert(gram)
     terms = kept + swap(sent, "core")
-    inverse_1 = invert(gram)
-    pieces = exchange(to_chunks(terms, chips_of(chips[1])), chips[1])
-    rows_two = total_over(rest, ("mid", "blk"))
-    pieces, inverse_1, rows_two = held(pieces, inverse_1, rows_two)
-    places = [two for two in range(2) for _ in range(inner)]
-    every = range(len(places))
-    plan = [(0, list(every))] + [(1, [at for at in every if places[at] == two]) for two in range(2)]
-    sums = swap(combine(pieces, inverse_1, plan), "n1")
-    mine = exchange(fan_out(sums, [(0, 2 - two) for two in places]), chips[1])
-    mine = mine.reshape(samples // 2, 2 * skel)
-    other = swap(mine, "core")
-
-    coupling_1, skeleton_2, gram, projected_2, kept, sent = level_call(
-        third_kernel,
-        [VMEM] * 11 + [ANY, ANY],
-        [square, wide, square, tall] + outgoing(1),
-        [s_buf, pltpu.VMEM((row_count, samples), jnp.float32), sems(2)],
-        8 * 10 ** 9,
-        (mine, other, inverse_1, rows_two, swap(rows_two, "core"), skeleton_0, skeleton_1, tilt, e02,
-         projected_0, projected_1, sample, probes),
-    )
-    terms = kept + swap(sent, "core")
-    terms = total_over(terms, chips[2])
-    inverse_2 = invert(gram)
-    terms, inverse_2 = held(terms, inverse_2)
-    mine = swap(combine(terms[None], inverse_2, [(0, [0])])[0], "n2")
+    if chips_of(chips[2]) == 2:
+        arrived = swap(terms, "blk")
+        arrived, inverse_2 = held(arrived, inverse_2)
+        mine = combine([terms[None], arrived[None]], inverse_2, [(0, [(0, 0), (1, 0)])])
+    else:
+        terms, inverse_2 = held(total_over(terms, chips[2]), inverse_2)
+        mine = combine([terms[None]], inverse_2, [(0, [(0, 0)])])
+    mine = swap(mine[0], "n2")
     bases, = level_call(
-        bases_kernel, [VMEM] * 6, [arr(levels, row_count, skel)], [], 4 * 10 ** 9,
+        bases_kernel, [ANY] * 3 + [VMEM] * 3, [arr(levels, row_count, skel)],
+        [pltpu.VMEM((levels, row_count, skel), jnp.float32), sems(levels)], 4 * 10 ** 9,
         (projected_0, projected_1, projected_2, inverse_0, inverse_1, inverse_2),
     )
     mine, bases = held(mine, bases)

time: 147 us -> 136 us (0.925)
  Pallas kernels: 65.2 us -> 55.9 us
  waiting for transfers between devices: 40.6 us -> 49.9 us
  starting transfers between devices: 31.8 us -> 27.1 us
  local copies, waits for them, and re-layouts: 5.14 us -> 0.7 us
    ppermute x22 -> x26, waiting for transfers between devices: 29.7 us -> 45.3 us  [swap(): return lax.ppermute(block, axis, [(0, 1), (1, 0)])]
    all_to_all x4 -> x2, waiting for transfers between devices: 10.9 us -> 4.56 us  [exchange(): return lax.all_to_all(pieces, axes, 0, 0, tiled=True)]
    all_to_all x4 -> x2, starting transfers between devices: 14.4 us -> 8.36 us  [exchange(): return lax.all_to_all(pieces, axes, 0, 0, tiled=True)]
    pallas_call x3, Pallas kernels: 5.45 us -> 0.65 us  [combine(): pl.pallas_call(functools.partial(combine_kernel, plan), out_shape=arr(len...]
    unnamed x34 -> x4, local copies, waits for them, and re-layouts: 5.14 us -> 0.7 us
    pallas_call x2, Pallas kernels: 3.27 us -> 0.78 us  [fan_out(): pl.pallas_call(functools.partial(fan_kernel, plan), out_shape=arr(len(pla...]
    pallas_call x8 -> x12, Pallas kernels: 47.3 us -> 45.4 us  [the longest x5 33.1 us: level_call(): pl.pallas_call(kernel, out_shape=outs, in_specs=specs, out_specs=[ANY if...]
    ppermute x22 -> x26, starting transfers between devices: 17.4 us -> 18.8 us  [swap(): return lax.ppermute(block, axis, [(0, 1), (1, 0)])]
  transfers between devices with their start and end apart: 26 -> 28, of which waited for: 20 -> 23; matrix products, arithmetic and copies ran while one was open for 1% -> 0% of each run, Pallas kernels for 19% -> 24%
where the time goes in v1:
time: 136 us
  Pallas kernels  55.9 us (41%)
  waiting for transfers between devices  49.9 us (37%)
  starting transfers between devices  27.1 us (20%)
    ppermute x26, waiting for transfers between devices, swap(): return lax.ppermute(block, axis, [(0, 1), (1, 0)])  45.3 us
    pallas_call x5, Pallas kernels, level_call(): pl.pallas_call(kernel, out_shape=outs, in_specs=specs, out_specs=[ANY if...  33.1 us
    ppermute x26, starting transfers between devices, swap(): return lax.ppermute(block, axis, [(0, 1), (1, 0)])  18.8 us
    pallas_call x3, Pallas kernels, pick(): pl.pallas_call(functools.partial(pick_kernel, wanted, sizes), out_shape=[...  9.13 us
    all_to_all x2, starting transfers between devices, exchange(): return lax.all_to_all(pieces, axes, 0, 0, tiled=True)  8.36 us
    pallas_call x3, Pallas kernels, invert(): pl.pallas_call(first_half_kernel, out_shape=[square] * 2, in_specs=[VMEM]...  6.35 us
    pallas_call x3, Pallas kernels, invert(): pl.pallas_call(second_half_kernel, out_shape=square, in_specs=[VMEM] * 2,...  5.88 us
    all_to_all x2, waiting for transfers between devices, exchange(): return lax.all_to_all(pieces, axes, 0, 0, tiled=True)  4.56 us
  transfers between devices with their start and end apart: 28, of which 23 were waited for; matrix products, arithmetic and copies ran while one was open for 0% of the time, Pallas kernels for 24%

profile of v1, /device:TPU:0, one launch (start us, length us, event | category | flops | bytes accessed | tf_op | source)
XLA Modules:
  0.0 135.7 jit_solution(17498494361700989587)
XLA Ops:
  1.3 2.3 %shard_map.50 = (f32[1,64,512]{2,1,0:T(8,128)S(1)}, f32[1,64,512]{2,1,0:T(8,128)S(1)}) custom-call(s32[14,128]{1,0:T(8,128)S(1)} %copy-done, f32[3,896,512]{2,1,0:T(8,128)} %refs_13_.1), custom_call_target="tpu_custom_call" | custom-call | flops 1000000000 | bytes 1835008 | tf_op jit(solution)/shard_map/pallas_call | solution.py:224
  5.1 2.9 %collective-permute-start.1 = (f32[64,512]{1,0:T(8,128)S(1)}, f32[64,512]{1,0:T(8,128)S(1)}, u32[]{:S(2)}, u32[]{:S(2)}) collective-permute-start(f32[64,512]{1,0:T(8,128)S(1)} %bitcast_add_fusion), channel_id=1, source_target_pairs={{0,1},{1,0},{2,3},{3,2},{4,5},{5,4},{6,7},{7,6},{8,9},{9,8},{10,11... | collective-permute-start | bytes 393224 | tf_op jit(solution)/shard_map/ppermute | solution.py:424
  8.1 3.0 %shard_map.51 = (f32[2,64,512]{2,1,0:T(8,128)S(1)}, f32[2,64,512]{2,1,0:T(8,128)S(1)}) custom-call(s32[14,128]{1,0:T(8,128)S(1)} %copy-done, f32[3,896,512]{2,1,0:T(8,128)} %refs_13_.1), custom_call_target="tpu_custom_call" | custom-call | flops 2000000000 | bytes 3670016 | tf_op jit(solution)/shard_map/pallas_call | solution.py:224
  13.7 3.5 %collective-permute-done.2 = f32[64,512]{1,0:T(8,128)S(1)} collective-permute-done((f32[64,512]{1,0:T(8,128)S(1)}, f32[64,512]{1,0:T(8,128)S(1)}, u32[]{:S(2)}, u32[]{:S(2)}) %collective-permute-start.2) | collective-permute-done | bytes 131104 | tf_op jit(solution)/shard_map/ppermute | solution.py:424
  18.9 3.3 %collective-permute-done.3 = f32[64,512]{1,0:T(8,128)S(1)} collective-permute-done((f32[64,512]{1,0:T(8,128)S(1)}, f32[64,512]{1,0:T(8,128)S(1)}, u32[]{:S(2)}, u32[]{:S(2)}) %collective-permute-start.3) | collective-permute-done | bytes 131104 | tf_op jit(solution)/shard_map/ppermute | solution.py:424
  23.7 5.2 %shard_map.52 = (f32[128,512]{1,0:T(8,128)S(1)}, f32[128,128]{1,0:T(8,128)S(1)}, f32[896,128]{1,0:T(8,128)S(1)}, f32[256,384]{1,0:T(8,128)S(1)}, f32[256,384]{1,0:T(8,128)S(1)}) custom-call(f32[64,512]{1,0:T(8,128)S(1)} %add.39.mine_ref, f32[64,512]{1,0:T(8,128)S(1)} %collective-permute-done.5.other_ref, f32[3,896,512]{2,1,0:T(8,128)} %refs_13_.1, ...), custom_call_target="tpu_custom_call" | custom-call | flops 3000000000 | bytes 4000000 | tf_op jit(solution)/shard_map/pallas_call | solution.py:412
  30.6 7.1 %collective-permute-done.7 = f32[2,64,512]{2,1,0:T(8,128)S(1)} collective-permute-done((f32[2,64,512]{2,1,0:T(8,128)S(1)}, f32[2,64,512]{2,1,0:T(8,128)S(1)}, u32[]{:S(2)}, u32[]{:S(2)}) %collective-permute-start.7) | collective-permute-done | bytes 262176 | tf_op jit(solution)/shard_map/ppermute | solution.py:424
  38.5 4.7 %all-to-all-start = ((f32[8,32,384]{2,1,0:T(8,128)}), f32[8,32,384]{2,1,0:T(8,128)S(1)}, u32[]{:S(2)}, u32[]{:S(2)}) async-start(f32[8,32,384]{2,1,0:T(8,128)} %bitcast.2), calls=%async_computation | async-start | bytes 786432 | tf_op jit(solution)/shard_map/all_to_all | solution.py:437
  51.1 2.6 %collective-permute-start.8 = (f32[5,32,128]{2,1,0:T(8,128)S(1)}, f32[5,32,128]{2,1,0:T(8,128)S(1)}, u32[]{:S(2)}, u32[]{:S(2)}) collective-permute-start(f32[5,32,128]{2,1,0:T(8,128)S(1)} %shard_map.55), channel_id=1, source_target_pairs={{0,16},{16,0},{1,17},{17,1},{2,18},{18,2},{3,19},{19,3},{4,20},{20... | collective-permute-start | bytes 245768 | tf_op jit(solution)/shard_map/ppermute | solution.py:424
  53.8 2.3 %collective-permute-done.9 = f32[2,64,512]{2,1,0:T(8,128)S(1)} collective-permute-done((f32[2,64,512]{2,1,0:T(8,128)S(1)}, f32[2,64,512]{2,1,0:T(8,128)S(1)}, u32[]{:S(2)}, u32[]{:S(2)}) %collective-permute-start.9) | collective-permute-done | bytes 262176 | tf_op jit(solution)/shard_map/ppermute | solution.py:424
  58.2 3.6 %all-to-all-start.1 = ((f32[8,32,384]{2,1,0:T(8,128)}), f32[8,32,384]{2,1,0:T(8,128)S(1)}, u32[]{:S(2)}, u32[]{:S(2)}) async-start(f32[8,32,384]{2,1,0:T(8,128)} %shard_map.56), calls=%async_computation.1 | async-start | bytes 786432 | tf_op jit(solution)/shard_map/all_to_all | solution.py:437
  61.8 3.8 %shard_map.57 = (f32[3,64,512]{2,1,0:T(8,128)S(1)}, f32[3,64,512]{2,1,0:T(8,128)S(1)}) custom-call(s32[14,128]{1,0:T(8,128)S(1)} %copy-done.1, f32[3,896,512]{2,1,0:T(8,128)} %refs_13_.1), custom_call_target="tpu_custom_call" | custom-call | flops 3000000000 | bytes 5505024 | tf_op jit(solution)/shard_map/pallas_call | solution.py:224
  65.6 3.1 %all-to-all-done.1 = f32[8,32,384]{2,1,0:T(8,128)S(1)} async-done(((f32[8,32,384]{2,1,0:T(8,128)}), f32[8,32,384]{2,1,0:T(8,128)S(1)}, u32[]{:S(2)}, u32[]{:S(2)}) %all-to-all-start.1) | async-done | bytes 393248 | tf_op jit(solution)/shard_map/all_to_all | solution.py:437
  71.4 9.7 %shard_map.58 = (f32[128,128]{1,0:T(8,128)S(1)}, f32[128,512]{1,0:T(8,128)S(1)}, f32[128,512]{1,0:T(8,128)S(1)}, f32[128,128]{1,0:T(8,128)S(1)}, f32[128,128]{1,...) custom-call(f32[256,384]{1,0:T(8,128)S(1)} %bitcast.14, ...), custom_call_target="tpu_custom_call" | custom-call | flops 8000000000 | bytes 4000000 | tf_op jit(solution)/shard_map/pallas_call | solution.py:412
  84.5 2.1 %shard_map.60 = (f32[128,128]{1,0:T(8,128)S(1)}, f32[128,128]{1,0:T(8,128)S(1)}) custom-call(f32[128,128]{1,0:T(8,128)S(1)} %get-tuple-element.95.a_ref), custom_call_target="tpu_custom_call" | custom-call | flops 2000000000 | bytes 131072 | tf_op jit(solution)/shard_map/pallas_call | solution.py:156
  86.6 2.8 %collective-permute-done.15 = f32[128,256]{1,0:T(8,128)S(1)} collective-permute-done((f32[128,256]{1,0:T(8,128)S(1)}, f32[128,256]{1,0:T(8,128)S(1)}, u32[]{:S(2)}, u32[]{:S(2)}) %collective-permute-start.15) | collective-permute-done | bytes 131104 | tf_op jit(solution)/shard_map/ppermute | solution.py:424
  92.0 2.5 %collective-permute-done.16 = f32[128,256]{1,0:T(8,128)S(1)} collective-permute-done((f32[128,256]{1,0:T(8,128)S(1)}, f32[128,256]{1,0:T(8,128)S(1)}, u32[]{:S(2)}, u32[]{:S(2)}) %collective-permute-start.16) | collective-permute-done | bytes 131104 | tf_op jit(solution)/shard_map/ppermute | solution.py:424
  95.8 3.9 %collective-permute-done.17.sums_ref = f32[2,128,128]{2,1,0:T(8,128)S(1)} collective-permute-done((f32[2,128,128]{2,1,0:T(8,128)S(1)}, f32[2,128,128]{2,1,0:T(8,128)S(1)}, u32[]{:S(2)}, u32[]{:S(2)}) %collective-permute-start.17) | collective-permute-done | bytes 131104 | tf_op jit(solution)/shard_map/ppermute | solution.py:424
  100.4 4.4 %collective-permute-done.18.refs_1_ = f32[128,256]{1,0:T(8,128)S(1)} collective-permute-done((f32[128,256]{1,0:T(8,128)S(1)}, f32[128,256]{1,0:T(8,128)S(1)}, u32[]{:S(2)}, u32[]{:S(2)}) %collective-permute-start.18) | collective-permute-done | bytes 131104 | tf_op jit(solution)/shard_map/ppermute | solution.py:424
  106.1 9.4 %shard_map.64 = (f32[128,128]{1,0:T(8,128)S(1)}, f32[128,512]{1,0:T(8,128)S(1)}, f32[128,128]{1,0:T(8,128)S(1)}, f32[896,128]{1,0:T(8,128)S(1)}, f32[256,128]{1,0:T(8,128)S(1)}, /*index=5*/f32[256,128]{1,0:T(8,128)S(1)}) custom-call(f32[128,256]{1,0:T(8,128)S(1)} %bitcast.20, f32[128,256]{1,0:T(8,128)S(1)} %collective-permute-done.18.refs_1_, ...), custom_call_target="tpu_custom_call" | custom-call | flops 8000000000 | bytes 4000000 | tf_op jit(solution)/shard_map/pallas_call | solution.py:412
  115.7 2.1 %shard_map.65 = (f32[128,128]{1,0:T(8,128)S(1)}, f32[128,128]{1,0:T(8,128)S(1)}) custom-call(f32[128,128]{1,0:T(8,128)S(1)} %get-tuple-element.107.a_ref), custom_call_target="tpu_custom_call" | custom-call | flops 2000000000 | bytes 131072 | tf_op jit(solution)/shard_map/pallas_call | solution.py:156
  120.5 3.2 %collective-permute-done.23 = f32[256,128]{1,0:T(8,128)S(1)} collective-permute-done((f32[256,128]{1,0:T(8,128)S(1)}, f32[256,128]{1,0:T(8,128)S(1)}, u32[]{:S(2)}, u32[]{:S(2)}) %collective-permute-start.23) | collective-permute-done | bytes 131104 | tf_op jit(solution)/shard_map/ppermute | solution.py:424
  124.5 3.5 %shard_map.68 = f32[3,896,128]{2,1,0:T(8,128)} custom-call(f32[896,128]{1,0:T(8,128)S(1)} %get-tuple-element.88.p0_hbm.refs_11_, f32[896,128]{1,0:T(8,128)S(1)} %get-tuple-element.104.refs_12_.p1_hbm, f32[896,128]{1,0:T(8,128)S(1)} %get-tuple-element.112.p2_hbm, f32[128,128]{1,0:T(8,128)S(1)} %shard_map.54.refs_1_.ours_ref.inverse_0, ...), custom_call_target="tpu_custom_call" | custom-call | flops 4000000000 | bytes 4000000 | tf_op jit(solution)/shard_map/pallas_call | solution.py:412
  130.3 5.4 %shard_map.69 = f32[3,1,128,128]{3,2,1,0:T(8,128)} custom-call(f32[256,128]{1,0:T(8,128)S(1)} %collective-permute-done.24.mine_ref, f32[256,128]{1,0:T(8,128)S(1)} %collective-permute-done.25.other_ref, f32[128,512]{1,0:T(8,128)S(1)} %get-tuple-element.115.skel_ref, f32[128,128]{1,0:T(8,128)S(1)} %get-tuple-element.116.c0_ref, ...), custom_call_target="tpu_custom_call" | custom-call | flops 5000000000 | bytes 4000000 | tf_op jit(solution)/shard_map/pallas_call | solution.py:412
  (68 shorter events, 38.5 us)
Async XLA Ops:
  5.1 6.7 %collective-permute-start.1 = (f32[64,512]{1,0:T(8,128)S(1)}, f32[64,512]{1,0:T(8,128)S(1)}, u32[]{:S(2)}, u32[]{:S(2)}) collective-permute-start(f32[64,512]{1,0:T(8,128)S(1)} %bitcast_add_fusion), channel_id=1, source_target_pairs={{0,1},{1,0},{2,3},{3,2},{4,5},{5,4},{6,7},{7,6},{8,9},{9,8},{10,11... | collective-permute-start | bytes 393224 | tf_op jit(solution)/shard_map/ppermute | solution.py:424
  11.1 7.7 %collective-permute-start.4 = (f32[2,64,512]{2,1,0:T(8,128)S(1)}, f32[2,64,512]{2,1,0:T(8,128)S(1)}, u32[]{:S(2)}, u32[]{:S(2)}) collective-permute-start(f32[2,64,512]{2,1,0:T(8,128)S(1)} %get-tuple-element.65), channel_id=1, source_target_pairs={{0,2},{2,0},{1,3},{3,1},{4,6},{6,4},{5,7},{7,5},{8,10},{10,8},{9,1... | collective-permute-start | bytes 786440 | tf_op jit(solution)/shard_map/ppermute | solution.py:424
  11.9 5.3 %collective-permute-start.2 = (f32[64,512]{1,0:T(8,128)S(1)}, f32[64,512]{1,0:T(8,128)S(1)}, u32[]{:S(2)}, u32[]{:S(2)}) collective-permute-start(f32[64,512]{1,0:T(8,128)S(1)} %add.37), channel_id=1, source_target_pairs={{0,4},{4,0},{1,5},{5,1},{2,6},{6,2},{3,7},{7,3},{8,12},{12,8},{9,1... | collective-permute-start | bytes 393224 | tf_op jit(solution)/shard_map/ppermute | solution.py:424
  17.2 5.0 %collective-permute-start.3 = (f32[64,512]{1,0:T(8,128)S(1)}, f32[64,512]{1,0:T(8,128)S(1)}, u32[]{:S(2)}, u32[]{:S(2)}) collective-permute-start(f32[64,512]{1,0:T(8,128)S(1)} %add.38), channel_id=1, source_target_pairs={{0,8},{8,0},{1,9},{9,1},{2,10},{10,2},{3,11},{11,3},{4,12},{12,4},... | collective-permute-start | bytes 393224 | tf_op jit(solution)/shard_map/ppermute | solution.py:424
  28.9 8.8 %collective-permute-start.6 = (f32[256,384]{1,0:T(8,128)S(1)}, f32[256,384]{1,0:T(8,128)S(1)}, u32[]{:S(2)}, u32[]{:S(2)}) collective-permute-start(f32[256,384]{1,0:T(8,128)S(1)} %get-tuple-element.68), channel_id=1, source_target_pairs={{0,2},{2,0},{1,3},{3,1},{4,6},{6,4},{5,7},{7,5},{8,10},{10,8},{9,1... | collective-permute-start | bytes 1179656 | tf_op jit(solution)/shard_map/ppermute | solution.py:424
  29.1 8.6 %collective-permute-start.7 = (f32[2,64,512]{2,1,0:T(8,128)S(1)}, f32[2,64,512]{2,1,0:T(8,128)S(1)}, u32[]{:S(2)}, u32[]{:S(2)}) collective-permute-start(f32[2,64,512]{2,1,0:T(8,128)S(1)} %add.40), channel_id=1, source_target_pairs={{0,1},{1,0},{2,3},{3,2},{4,5},{5,4},{6,7},{7,6},{8,9},{9,8},{10,11... | collective-permute-start | bytes 786440 | tf_op jit(solution)/shard_map/ppermute | solution.py:424
  38.5 12.4 %all-to-all-start = ((f32[8,32,384]{2,1,0:T(8,128)}), f32[8,32,384]{2,1,0:T(8,128)S(1)}, u32[]{:S(2)}, u32[]{:S(2)}) async-start(f32[8,32,384]{2,1,0:T(8,128)} %bitcast.2), calls=%async_computation | async-start | bytes 786432 | tf_op jit(solution)/shard_map/all_to_all | solution.py:437
  45.4 10.7 %collective-permute-start.9 = (f32[2,64,512]{2,1,0:T(8,128)S(1)}, f32[2,64,512]{2,1,0:T(8,128)S(1)}, u32[]{:S(2)}, u32[]{:S(2)}) collective-permute-start(f32[2,64,512]{2,1,0:T(8,128)S(1)} %add.42), channel_id=1, source_target_pairs={{0,4},{4,0},{1,5},{5,1},{2,6},{6,2},{3,7},{7,3},{8,12},{12,8},{9,1... | collective-permute-start | bytes 786440 | tf_op jit(solution)/shard_map/ppermute | solution.py:424
  51.1 6.2 %collective-permute-start.8 = (f32[5,32,128]{2,1,0:T(8,128)S(1)}, f32[5,32,128]{2,1,0:T(8,128)S(1)}, u32[]{:S(2)}, u32[]{:S(2)}) collective-permute-start(f32[5,32,128]{2,1,0:T(8,128)S(1)} %shard_map.55), channel_id=1, source_target_pairs={{0,16},{16,0},{1,17},{17,1},{2,18},{18,2},{3,19},{19,3},{4,20},{20... | collective-permute-start | bytes 245768 | tf_op jit(solution)/shard_map/ppermute | solution.py:424
  58.2 10.5 %all-to-all-start.1 = ((f32[8,32,384]{2,1,0:T(8,128)}), f32[8,32,384]{2,1,0:T(8,128)S(1)}, u32[]{:S(2)}, u32[]{:S(2)}) async-start(f32[8,32,384]{2,1,0:T(8,128)} %shard_map.56), calls=%async_computation.1 | async-start | bytes 786432 | tf_op jit(solution)/shard_map/all_to_all | solution.py:437
  68.7 1.7 %collective-permute-start.11 = (f32[3,64,512]{2,1,0:T(8,128)S(1)}, f32[3,64,512]{2,1,0:T(8,128)S(1)}, u32[]{:S(2)}, u32[]{:S(2)}) collective-permute-start(f32[3,64,512]{2,1,0:T(8,128)S(1)} %get-tuple-element.83), channel_id=1, source_target_pairs={{0,2},{2,0},{1,3},{3,1},{4,6},{6,4},{5,7},{7,5},{8,10},{10,8},{9,1... | collective-permute-start | bytes 1179656 | tf_op jit(solution)/shard_map/ppermute | solution.py:424
  68.7 2.3 %collective-permute-start.10 = (f32[256,384]{1,0:T(8,128)S(1)}, f32[256,384]{1,0:T(8,128)S(1)}, u32[]{:S(2)}, u32[]{:S(2)}) collective-permute-start(f32[256,384]{1,0:T(8,128)S(1)} %bitcast.13), channel_id=1, source_target_pairs={{0,2},{2,0},{1,3},{3,1},{4,6},{6,4},{5,7},{7,5},{8,10},{10,8},{9,1... | collective-permute-start | bytes 1179656 | tf_op jit(solution)/shard_map/ppermute | solution.py:424
  69.2 2.1 %collective-permute-start.12 = (f32[2,64,512]{2,1,0:T(8,128)S(1)}, f32[2,64,512]{2,1,0:T(8,128)S(1)}, u32[]{:S(2)}, u32[]{:S(2)}) collective-permute-start(f32[2,64,512]{2,1,0:T(8,128)S(1)} %add.43.rows_mine), channel_id=1, source_target_pairs={{0,2},{2,0},{1,3},{3,1},{4,6},{6,4},{5,7},{7,5},{8,10},{10,8},{9,1... | collective-permute-start | bytes 786440 | tf_op jit(solution)/shard_map/ppermute | solution.py:424
  71.0 11.2 %collective-permute-start.13 = (f32[3,64,512]{2,1,0:T(8,128)S(1)}, f32[3,64,512]{2,1,0:T(8,128)S(1)}, u32[]{:S(2)}, u32[]{:S(2)}) collective-permute-start(f32[3,64,512]{2,1,0:T(8,128)S(1)} %add.44), channel_id=1, source_target_pairs={{0,1},{1,0},{2,3},{3,2},{4,5},{5,4},{6,7},{7,6},{8,9},{9,8},{10,11... | collective-permute-start | bytes 1179656 | tf_op jit(solution)/shard_map/ppermute | solution.py:424
  82.2 1.6 %collective-permute-start.14 = (f32[256,256]{1,0:T(8,128)S(1)}, f32[256,256]{1,0:T(8,128)S(1)}, u32[]{:S(2)}, u32[]{:S(2)}) collective-permute-start(f32[256,256]{1,0:T(8,128)S(1)} %get-tuple-element.92), channel_id=1, source_target_pairs={{0,2},{2,0},{1,3},{3,1},{4,6},{6,4},{5,7},{7,5},{8,10},{10,8},{9,1... | collective-permute-start | bytes 786440 | tf_op jit(solution)/shard_map/ppermute | solution.py:424
  83.8 5.6 %collective-permute-start.15 = (f32[128,256]{1,0:T(8,128)S(1)}, f32[128,256]{1,0:T(8,128)S(1)}, u32[]{:S(2)}, u32[]{:S(2)}) collective-permute-start(f32[128,256]{1,0:T(8,128)S(1)} %get-tuple-element.94), channel_id=1, source_target_pairs={{0,1},{1,0},{2,3},{3,2},{4,5},{5,4},{6,7},{7,6},{8,9},{9,8},{10,11... | collective-permute-start | bytes 393224 | tf_op jit(solution)/shard_map/ppermute | solution.py:424
  89.5 5.0 %collective-permute-start.16 = (f32[128,256]{1,0:T(8,128)S(1)}, f32[128,256]{1,0:T(8,128)S(1)}, u32[]{:S(2)}, u32[]{:S(2)}) collective-permute-start(f32[128,256]{1,0:T(8,128)S(1)} %add.46), channel_id=1, source_target_pairs={{0,4},{4,0},{1,5},{5,1},{2,6},{6,2},{3,7},{7,3},{8,12},{12,8},{9,1... | collective-permute-start | bytes 393224 | tf_op jit(solution)/shard_map/ppermute | solution.py:424
  94.7 5.0 %collective-permute-start.17 = (f32[2,128,128]{2,1,0:T(8,128)S(1)}, f32[2,128,128]{2,1,0:T(8,128)S(1)}, u32[]{:S(2)}, u32[]{:S(2)}) collective-permute-start(f32[2,128,128]{2,1,0:T(8,128)S(1)} %shard_map.62), channel_id=1, source_target_pairs={{0,8},{8,0},{1,9},{9,1},{2,10},{10,2},{3,11},{11,3},{4,12},{12,4},... | collective-permute-start | bytes 393224 | tf_op jit(solution)/shard_map/ppermute | solution.py:424
  95.8 9.0 %collective-permute-start.21 = (f32[3,64,512]{2,1,0:T(8,128)S(1)}, f32[3,64,512]{2,1,0:T(8,128)S(1)}, u32[]{:S(2)}, u32[]{:S(2)}) collective-permute-start(f32[3,64,512]{2,1,0:T(8,128)S(1)} %add.45.refs_5_), channel_id=1, source_target_pairs={{0,2},{2,0},{1,3},{3,1},{4,6},{6,4},{5,7},{7,5},{8,10},{10,8},{9,1... | collective-permute-start | bytes 1179656 | tf_op jit(solution)/shard_map/ppermute | solution.py:424
  99.7 5.0 %collective-permute-start.18 = (f32[128,256]{1,0:T(8,128)S(1)}, f32[128,256]{1,0:T(8,128)S(1)}, u32[]{:S(2)}, u32[]{:S(2)}) collective-permute-start(f32[128,256]{1,0:T(8,128)S(1)} %bitcast.18), channel_id=1, source_target_pairs={{0,1},{1,0},{2,3},{3,2},{4,5},{5,4},{6,7},{7,6},{8,9},{9,8},{10,11... | collective-permute-start | bytes 393224 | tf_op jit(solution)/shard_map/ppermute | solution.py:424
  100.4 4.4 %collective-permute-start.19 = (f32[128,256]{1,0:T(8,128)S(1)}, f32[128,256]{1,0:T(8,128)S(1)}, u32[]{:S(2)}, u32[]{:S(2)}) collective-permute-start(f32[128,256]{1,0:T(8,128)S(1)} %bitcast.19), channel_id=1, source_target_pairs={{0,2},{2,0},{1,3},{3,1},{4,6},{6,4},{5,7},{7,5},{8,10},{10,8},{9,1... | collective-permute-start | bytes 393224 | tf_op jit(solution)/shard_map/ppermute | solution.py:424
  115.5 2.3 %collective-permute-start.22 = (f32[256,128]{1,0:T(8,128)S(1)}, f32[256,128]{1,0:T(8,128)S(1)}, u32[]{:S(2)}, u32[]{:S(2)}) collective-permute-start(f32[256,128]{1,0:T(8,128)S(1)} %get-tuple-element.106), channel_id=1, source_target_pairs={{0,2},{2,0},{1,3},{3,1},{4,6},{6,4},{5,7},{7,5},{8,10},{10,8},{9,1... | collective-permute-start | bytes 393224 | tf_op jit(solution)/shard_map/ppermute | solution.py:424
  117.9 5.8 %collective-permute-start.23 = (f32[256,128]{1,0:T(8,128)S(1)}, f32[256,128]{1,0:T(8,128)S(1)}, u32[]{:S(2)}, u32[]{:S(2)}) collective-permute-start(f32[256,128]{1,0:T(8,128)S(1)} %add.47), channel_id=1, source_target_pairs={{0,1},{1,0},{2,3},{3,2},{4,5},{5,4},{6,7},{7,6},{8,9},{9,8},{10,11... | collective-permute-start | bytes 393224 | tf_op jit(solution)/shard_map/ppermute | solution.py:424
  123.9 5.0 %collective-permute-start.24 = (f32[256,128]{1,0:T(8,128)S(1)}, f32[256,128]{1,0:T(8,128)S(1)}, u32[]{:S(2)}, u32[]{:S(2)}) collective-permute-start(f32[256,128]{1,0:T(8,128)S(1)} %bitcast.15), channel_id=1, source_target_pairs={{0,4},{4,0},{1,5},{5,1},{2,6},{6,2},{3,7},{7,3},{8,12},{12,8},{9,1... | collective-permute-start | bytes 393224 | tf_op jit(solution)/shard_map/ppermute | solution.py:424
  (6 other events, 22.8 us)

commit v2 on v1

--- a/solution.py
+++ b/solution.py
@@ -17,6 +17,7 @@
 SMEM = pl.BlockSpec(memory_space=pltpu.SMEM)
 ANY = pl.BlockSpec(memory_space=pltpu.HBM)
 BIG = pltpu.CompilerParams(vmem_limit_bytes=49 * 1024 * 1024)
+MIDDLE = pltpu.CompilerParams(vmem_limit_bytes=10 * 1024 * 1024)
 SMALL = pltpu.CompilerParams(vmem_limit_bytes=4 * 1024 * 1024)
 
 
@@ -40,24 +41,32 @@
     )
 
 
+def split3(block):
+    high = block.astype(jnp.bfloat16)
+    rest = block - high.astype(jnp.float32)
+    middle = rest.astype(jnp.bfloat16)
+    return high, middle, (rest - middle.astype(jnp.float32)).astype(jnp.bfloat16)
+
+
+def stacked_dot(left_parts, right_parts, left_dim, right_dim):
+    count = len(left_parts)
+    rows = left_parts[0].shape[1 - left_dim]
+    total = None
+    for at in reversed(range(count)):
+        stack = jnp.concatenate(left_parts[:count - at], axis=1 - left_dim)
+        block = plain_dot(stack, right_parts[at], left_dim, right_dim)
+        for part in reversed(range(count - at)):
+            term = block[part * rows:(part + 1) * rows]
+            total = term if total is None else total + term
+    return total
+
+
 def dot3(left_side, right_side, left_dim=1, right_dim=0):
-    left_high, left_low = split(left_side)
-    right_high, right_low = split(right_side)
-    return (
-        plain_dot(left_high, right_high, left_dim, right_dim)
-        + plain_dot(left_high, right_low, left_dim, right_dim)
-        + plain_dot(left_low, right_high, left_dim, right_dim)
-    )
+    return stacked_dot(split(left_side), split(right_side), left_dim, right_dim)
 
 
 def dot6(left_side, right_side, left_dim=1, right_dim=0):
-    return lax.dot_general(
-        left_side,
-        right_side,
-        (((left_dim,), (right_dim,)), ((), ())),
-        precision=lax.Precision.HIGHEST,
-        preferred_element_type=jnp.float32,
-    )
+    return stacked_dot(split3(left_side), split3(right_side), left_dim, right_dim)
 
 
 def scales_of(matrix):
@@ -139,28 +148,34 @@
     return jnp.concatenate(rows, axis=0)
 
 
-def first_half_kernel(a_ref, o_ref, scales_ref):
-    scales = scales_of(a_ref[...])
+def first_half_kernel(skel_ref, o_ref, scales_ref):
+    gram = gram_of(skel_ref[...], skel_ref.shape[1])
+    scales = scales_of(gram)
     scales_ref[...] = scales
-    o_ref[...] = eliminate(a_ref[...] * scales, (0, 1))
+    o_ref[...] = eliminate(gram * scales, (0, 1))
 
 
 def second_half_kernel(a_ref, scales_ref, o_ref):
     o_ref[...] = eliminate(a_ref[...], (2, 3)) * scales_ref[...]
 
 
-def invert(matrix):
-    size = matrix.shape[0]
-    half = cost(2 * 10 ** 9, 8 * size ** 2)
-    square = arr(size, size)
-    state, scales = pl.pallas_call(
+def invert_first(skeleton):
+    square = arr(skeleton.shape[0], skeleton.shape[0])
+    return pl.pallas_call(
         first_half_kernel, out_shape=[square] * 2, in_specs=[VMEM], out_specs=[VMEM] * 2,
-        compiler_params=SMALL, cost_estimate=half,
-    )(matrix)
-    return pl.pallas_call(
-        second_half_kernel, out_shape=square, in_specs=[VMEM] * 2, out_specs=VMEM,
-        compiler_params=SMALL, cost_estimate=half,
+        compiler_params=SMALL, cost_estimate=cost(2 * 10 ** 9, 10 ** 5),
+    )(skeleton)
+
+
+def invert_second(state, scales):
+    return pl.pallas_call(
+        second_half_kernel, out_shape=arr(*state.shape), in_specs=[VMEM] * 2, out_specs=VMEM,
+        compiler_params=SMALL, cost_estimate=cost(2 * 10 ** 9, 10 ** 5),
     )(state, scales)
+
+
+def invert(skeleton):
+    return invert_second(*invert_first(skeleton))
 
 
 def ridge(matrix):
@@ -168,13 +183,6 @@
     row = lax.broadcasted_iota(jnp.int32, (size, size), 0)
     col = lax.broadcasted_iota(jnp.int32, (size, size), 1)
     return matrix + jnp.where(row == col, ridge_term, 0.0)
-
-
-def split3(block):
-    high = block.astype(jnp.bfloat16)
-    rest = block - high.astype(jnp.float32)
-    middle = rest.astype(jnp.bfloat16)
-    return high, middle, (rest - middle.astype(jnp.float32)).astype(jnp.bfloat16)
 
 
 def marks(list_ref, level, sizes, row_count):
@@ -187,7 +195,16 @@
         node = node * 2 + index
     row_total = row_count * math.prod(sizes)
     shift = node * (row_total >> level + 1) - device * row_count
-    listed = list_ref[pl.ds(node + (2 ** (level + 1) - 2), 1), :] + shift
+    at = node + (2 ** (level + 1) - 2)
+    skel = list_ref.shape[1]
+    lane = lax.broadcasted_iota(jnp.int32, (TILE, skel), 1)
+    parts = []
+    for first in range(0, skel, 16):
+        part = jnp.zeros((TILE, skel), jnp.int32)
+        for i in range(first, first + 16):
+            part = jnp.where(lane == i, list_ref[at, i], part)
+        parts.append(part)
+    listed = sum(parts)[:1] + shift
     row_ids = lax.broadcasted_iota(jnp.int32, (row_count, listed.shape[1]), 0)
     return jnp.where(row_ids == listed, 1.0, 0.0).astype(jnp.bfloat16)
 
@@ -196,44 +213,32 @@
     return sum(plain_dot(mark, part, 0, 0) for part in reversed(parts))
 
 
-def pick_kernel(wanted, sizes, list_hbm, s_hbm, kept_ref, sent_ref, list_ref, s_buf, sems):
-    levels = sorted({level for level, _ in wanted})
-    sources = sorted({source for _, source in wanted})
-    running = copies(
-        [(list_hbm, list_ref)] + [(s_hbm.at[source], s_buf.at[at]) for at, source in enumerate(sources)], sems
-    )
+def pick_kernel(wanted, sizes, list_ref, *refs):
+    sources, (kept_ref, sent_ref) = refs[:-2], refs[-2:]
     half = kept_ref.shape[1]
     here = lax.axis_index("core") == 0
-    running[0].wait()
-    mark = {level: marks(list_ref, level, sizes, s_buf.shape[1]) for level in levels}
-    for at, source in enumerate(sources):
-        running[1 + at].wait()
-        parts = split3(s_buf[at])
-        for slot, (level, from_source) in enumerate(wanted):
-            if from_source == source:
-                rows = taken(mark[level], parts)
-                kept_ref[slot] = jnp.where(here, rows[:half], rows[half:])
-                sent_ref[slot] = jnp.where(here, rows[half:], rows[:half])
+    mark = marks(list_ref, wanted[0][0], sizes, sources[0].shape[0])
+    for slot, source_ref in enumerate(sources):
+        rows = taken(mark, split3(source_ref[...]))
+        kept_ref[slot] = jnp.where(here, rows[:half], rows[half:])
+        sent_ref[slot] = jnp.where(here, rows[half:], rows[:half])
 
 
 def pick(skeleton_rows, sample, wanted, sizes):
     _, row_count, samples = sample.shape
     skel = skeleton_rows.shape[1]
     count = len(wanted)
-    sources = len({source for _, source in wanted})
+    block = (None, row_count, samples)
+    specs = [pl.BlockSpec(block, functools.partial(lambda source, step: (source, 0, 0), source)) for _, source in wanted]
     return pl.pallas_call(
         functools.partial(pick_kernel, wanted, sizes),
         out_shape=[arr(count, skel // 2, samples)] * 2,
-        in_specs=[ANY, ANY],
+        grid=(1,),
+        in_specs=[SMEM] + specs,
         out_specs=[VMEM] * 2,
-        scratch_shapes=[
-            pltpu.VMEM(skeleton_rows.shape, jnp.int32),
-            pltpu.VMEM((sources, row_count, samples), jnp.float32),
-            pltpu.SemaphoreType.DMA((1 + sources,)),
-        ],
         compiler_params=BIG,
-        cost_estimate=cost(10 ** 9 * count, sources * row_count * samples * 4),
-    )(skeleton_rows, sample)
+        cost_estimate=cost(10 ** 9 * count, count * row_count * samples * 4),
+    )(skeleton_rows, *([sample] * count))
 
 
 def project(sample_block, skeleton, samples, earlier):
@@ -261,9 +266,7 @@
 
 
 def moments(projected, tests):
-    high, low = split(projected)
-    test_high, test_low = split(tests)
-    return plain_dot(high, test_high, 0, 0) + plain_dot(high, test_low, 0, 0) + plain_dot(low, test_high, 0, 0)
+    return dot3(projected, tests, 0, 0)
 
 
 def copies(pairs, sems):
@@ -304,14 +307,13 @@
     return ridge(dot6(skeleton, skeleton, 1, 1) * (1.0 / samples))
 
 
-def first_kernel(mine_ref, other_ref, s_hbm, t_hbm, skel_ref, gram_ref, p_hbm, kept_ref, sent_ref,
+def first_kernel(mine_ref, other_ref, s_hbm, t_hbm, skel_ref, p_hbm, kept_ref, sent_ref,
                  s_buf, t_buf, p_ref, sems):
     samples = mine_ref.shape[1]
     levels = t_buf.shape[0]
     running = copies([(s_hbm.at[0], s_buf)] + [(t_hbm.at[l], t_buf.at[l]) for l in range(levels)], sems)
     skeleton = whole(mine_ref, other_ref)
     skel_ref[...] = skeleton
-    gram_ref[...] = gram_of(skeleton, samples)
     running[0].wait()
     projected = project(s_buf[...], skeleton, samples, [])
     p_ref[...] = projected
@@ -322,23 +324,25 @@
     leaving[0].wait()
 
 
-def second_kernel(mine_ref, other_ref, ours_ref, rows_mine, rows_other, skel0_ref, p0_hbm, s_hbm, t_hbm,
-                  c0_ref, e02_ref, skel_ref, tilt_ref, gram_ref, p_hbm, kept_ref, sent_ref,
-                  s_buf, t_buf, p_ref, p0_ref, sems):
+def second_rows_kernel(rows_mine, rows_other, skel0_ref, low_ref, rows_ref):
+    rows_low, rows_high = ordered(rows_mine, rows_other)
+    samples = skel0_ref.shape[1]
+    low_ref[...] = dot3(whole_rows(rows_low, rows_high, 0), skel0_ref[...], 1, 1) * (1.0 / samples)
+    rows_ref[...] = whole_rows(rows_low, rows_high, 1)
+
+
+def second_kernel(mine_ref, other_ref, ours_ref, low_ref, rows_ref, skel0_ref, p0_hbm, s_hbm, t_hbm,
+                  c0_ref, back_ref, skel_ref, tilt_ref, p_hbm, kept_ref, sent_ref, s_buf, t_buf, p_ref, p0_ref, sems):
     samples = skel0_ref.shape[1]
     running = copies([(s_hbm.at[1], s_buf), (p0_hbm, p0_ref), (t_hbm.at[1], t_buf.at[0]), (t_hbm.at[2], t_buf.at[1])], sems)
     low, high = ordered(mine_ref, other_ref)
-    rows_low, rows_high = ordered(rows_mine, rows_other)
-    skeleton_0 = skel0_ref[...]
-    low_0 = dot3(whole_rows(rows_low, rows_high, 0), skeleton_0, 1, 1) * (1.0 / samples)
-    coupling = couple(skeleton_0, joined(low, high, 0))
+    coupling = couple(skel0_ref[...], joined(low, high, 0))
     c0_ref[...] = coupling
     back = dot3(ours_ref[...], coupling)
+    back_ref[...] = back
     e01 = dot3(back, joined(low, high, 1), 1, 1)
-    e02_ref[...] = dot3(back, joined(low, high, 2), 1, 1)
-    skeleton = whole_rows(rows_low, rows_high, 1) - dot3(low_0, e01)
+    skeleton = rows_ref[...] - dot3(low_ref[...], e01)
     skel_ref[...] = skeleton
-    gram_ref[...] = gram_of(skeleton, samples)
     tilt = dot3(e01, skeleton, 1, 1)
     tilt_ref[...] = tilt
     running[0].wait()
@@ -352,12 +356,25 @@
     leaving[0].wait()
 
 
+def third_rows_kernel(mine_ref, other_ref, back_ref, rows_mine, rows_other, skel0_ref, skel1_ref, tilt_ref,
+                      e02_ref, low_ref, rows_ref):
+    share = 1.0 / skel0_ref.shape[1]
+    low, high = ordered(mine_ref, other_ref)
+    rows_low, rows_high = ordered(rows_mine, rows_other)
+    e02 = dot3(back_ref[...], joined(low, high, 2), 1, 1)
+    e02_ref[...] = e02
+    low_0 = dot3(whole_rows(rows_low, rows_high, 0), skel0_ref[...], 1, 1) * share
+    low_ref[...] = (
+        dot3(whole_rows(rows_low, rows_high, 1), skel1_ref[...], 1, 1) - dot3(low_0, tilt_ref[...])
+    ) * share
+    rows_ref[...] = whole_rows(rows_low, rows_high, 2) - dot3(low_0, e02)
+
+
 def third_kernel(pieces, *refs):
     parts, refs = refs[:pieces], refs[pieces:]
-    (ours_ref, rows_mine, rows_other, skel0_ref, skel1_ref, tilt_in_ref, e02_ref, p0_hbm, p1_hbm, s_hbm, t_hbm,
-     c1_ref, skel_ref, gram_ref, p_hbm, kept_ref, sent_ref, s_buf, t_buf, p_ref, p0_ref, p1_ref, sems) = refs
+    (ours_ref, rows_ref, low_ref, e02_ref, skel1_ref, p0_hbm, p1_hbm, s_hbm, t_hbm,
+     c1_ref, skel_ref, p_hbm, kept_ref, sent_ref, s_buf, t_buf, p_ref, p0_ref, p1_ref, sems) = refs
     samples = skel1_ref.shape[1]
-    share = 1.0 / samples
     running = copies([(s_hbm.at[2], s_buf), (p0_hbm, p0_ref), (p1_hbm, p1_ref), (t_hbm.at[2], t_buf)], sems)
     if pieces == 2:
         low, high = ordered(*parts)
@@ -370,18 +387,12 @@
         here = lax.axis_index("core") == 0
         low = jnp.where(here, both[0], both[1])
         high = jnp.where(here, both[1], both[0])
-    rows_low, rows_high = ordered(rows_mine, rows_other)
-    skeleton_1 = skel1_ref[...]
     e02 = e02_ref[...]
-    low_0 = dot3(whole_rows(rows_low, rows_high, 0), skel0_ref[...], 1, 1) * share
-    low_1 = (dot3(whole_rows(rows_low, rows_high, 1), skeleton_1, 1, 1) - dot3(low_0, tilt_in_ref[...])) * share
-    rows = whole_rows(rows_low, rows_high, 2) - dot3(low_0, e02)
-    coupling = couple(skeleton_1, joined(low, high, 0))
+    coupling = couple(skel1_ref[...], joined(low, high, 0))
     c1_ref[...] = coupling
     e12 = dot3(dot3(ours_ref[...], coupling), joined(low, high, 1), 1, 1)
-    skeleton = rows - dot3(low_1, e12)
+    skeleton = rows_ref[...] - dot3(low_ref[...], e12)
     skel_ref[...] = skeleton
-    gram_ref[...] = gram_of(skeleton, samples)
     tilt_0 = dot3(e02, skeleton, 1, 1)
     tilt_1 = dot3(e12, skeleton, 1, 1)
     for copy in running[:3]:
@@ -420,8 +431,23 @@
     )(*operands)
 
 
+def small_call(kernel, outs, operands):
+    return pl.pallas_call(
+        kernel,
+        out_shape=outs,
+        in_specs=[VMEM] * len(operands),
+        out_specs=[VMEM] * len(outs),
+        compiler_params=MIDDLE,
+        cost_estimate=cost(10 ** 9, 10 ** 6),
+    )(*operands)
+
+
 def swap(block, axis):
     return lax.ppermute(block, axis, [(0, 1), (1, 0)])
+
+
+def cross_swap(block):
+    return lax.ppermute(block, ("n1", "n2"), [(0, 3), (1, 2), (2, 1), (3, 0)])
 
 
 def chips_of(axes):
@@ -492,22 +518,23 @@
     )(one, two)
 
 
-def fan_kernel(plan, sums_ref, out_ref):
+def fan_kernel(plan, *refs):
     for place, wanted in enumerate(plan):
-        for kind, at in enumerate(wanted):
-            out_ref[place, :, kind * WIDTH:(kind + 1) * WIDTH] = sums_ref[at]
+        for kind, terms in enumerate(wanted):
+            total = sum(refs[which][at] for which, at in terms)
+            refs[-1][place, :, kind * WIDTH:(kind + 1) * WIDTH] = total
 
 
 def fan_out(sums, plan):
-    rows = sums.shape[1]
+    rows = sums[0].shape[1]
     return pl.pallas_call(
         functools.partial(fan_kernel, plan),
         out_shape=arr(len(plan), rows, WIDTH * len(plan[0])),
-        in_specs=[VMEM],
+        in_specs=[VMEM] * len(sums),
         out_specs=VMEM,
         compiler_params=SMALL,
         cost_estimate=cost(10 ** 6, 10 ** 6),
-    )(sums)
+    )(*sums)
 
 
 def local(sample, probes, skeleton_rows):
@@ -533,23 +560,23 @@
     half, lists = held(half, skeleton_rows)
     half = total_over(half, ("mid", "blk"))
     rest_kept, rest_sent = pick(lists, sample, ((1, 0), (1, 1)), sizes)
-    half = total_over(half, ("n2", "n1"))
     rest = rest_kept + swap(rest_sent, "core")
-    half, rest = held(half, rest)
+    half = half + swap(half, "n2") + swap(half, "n1") + cross_swap(half)
+    half_other, rest = held(swap(half, "core"), rest)
     rest = total_over(rest, ("mid", "blk"))
 
-    skeleton_0, gram, projected_0, kept, sent = level_call(
+    skeleton_0, projected_0, kept, sent = level_call(
         first_kernel,
         [VMEM] * 2 + [ANY, ANY],
-        [wide, square, tall] + outgoing(levels),
+        [wide, tall] + outgoing(levels),
         [s_buf, t_buf(levels), p_buf, sems(2 + levels)],
         3 * 10 ** 9,
-        (half, swap(half, "core"), sample, probes),
-        in_hbm=2,
-    )
+        (half, half_other, sample, probes),
+        in_hbm=1,
+    )
+    sent, rest = held(sent, rest)
     terms = kept + swap(sent, "core")
-    terms, rest = held(terms, rest)
-    inverse_0 = invert(gram)
+    inverse_0 = invert(skeleton_0)
     rows_one = total_over(rest, ("n2",))
     pieces = exchange(to_chunks(terms, chips_of(chips[0])), chips[0])
     pieces, inverse_0 = held(pieces, inverse_0)
@@ -562,7 +589,7 @@
     sums = swap(combine([pieces], inverse_0, plan), "n0")
     sums, lists, rows_one = held(sums, skeleton_rows, rows_one)
     rest_kept, rest_sent = pick(lists, sample, ((2, 0), (2, 1), (2, 2)), sizes)
-    mine = exchange(fan_out(sums, [(0, 2 - one, 4 - two) for one, two in places]), chips[0])
+    mine = exchange(fan_out([sums], [[[(0, at)] for at in (0, 2 - one, 4 - two)] for one, two in places]), chips[0])
     mine = mine.reshape(samples // 2, levels * skel)
     mine, rest_kept, rest_sent = held(mine, rest_kept, rest_sent)
     other = swap(mine, "core")
@@ -570,26 +597,28 @@
     mine, other, rest = held(mine, other, rest)
     rest = total_over(rest, ("mid", "blk"))
 
-    coupling_0, e02, skeleton_1, tilt, gram, projected_1, kept, sent = level_call(
+    low, rows_one = small_call(second_rows_kernel, [square, wide], (rows_one, swap(rows_one, "core"), skeleton_0))
+    coupling_0, back, skeleton_1, tilt, projected_1, kept, sent = level_call(
         second_kernel,
         [VMEM] * 6 + [ANY] * 3,
-        [square, wide, wide, square, square, tall] + outgoing(2),
+        [square, square, wide, square, tall] + outgoing(2),
         [s_buf, t_buf(2), p_buf, p_buf, sems(5)],
         8 * 10 ** 9,
-        (mine, other, inverse_0, rows_one, swap(rows_one, "core"), skeleton_0, projected_0, sample, probes),
-        in_hbm=5,
-    )
-    sent, rest = held(sent, rest)
+        (mine, other, inverse_0, low, rows_one, skeleton_0, projected_0, sample, probes),
+        in_hbm=4,
+    )
     sent, rows_two = held(sent, rest)
-    inverse_1 = invert(gram)
+    rows_two_other = swap(rows_two, "core")
+    inverse_1 = invert(skeleton_1)
+    before = (mine, other)
     if chips_of(chips[2]) == 2:
         kept, sent = add_split(kept, swap(sent, "core"), "blk")
-        terms = kept + swap(sent, "blk")
-        arrived = swap(terms, "n2")
+        arrived = swap(sent, "blk")
         arrived, inverse_1 = held(arrived, inverse_1)
-        plan = [(0, [(0, 0), (1, 0)]), (1, [(1, 0)])]
-        sums = swap(combine([terms[None], arrived[None]], inverse_1, plan), "n1")
-        mine = fan_out(sums, [(0, 1)])[0]
+        sums = combine([kept[None], arrived[None]], inverse_1, [(0, [(0, 0), (1, 0)]), (1, [(0, 0), (1, 0)])])
+        far, beside = cross_swap(sums), swap(sums[:1], "n1")
+        mine = fan_out([far, beside], [[[(0, 0), (1, 0)], [(0, 1)]]])[0]
+        mine, rows_two = held(mine, rows_two)
         beside = swap(mine, "blk")
         parts = (mine, beside, swap(mine, "core"), swap(beside, "core"))
     else:
@@ -601,21 +630,25 @@
         plan = [(0, [(0, at) for at in every])]
         plan += [(1, [(0, at) for at in every if places[at] == two]) for two in range(2)]
         sums = swap(combine([pieces], inverse_1, plan), "n1")
-        mine = exchange(fan_out(sums, [(0, 2 - two) for two in places]), chips[1])
+        mine = exchange(fan_out([sums], [[[(0, at)] for at in (0, 2 - two)] for two in places]), chips[1])
         mine = mine.reshape(samples // 2, 2 * skel)
         parts = (mine, swap(mine, "core"))
 
-    coupling_1, skeleton_2, gram, projected_2, kept, sent = level_call(
+    e02, low, rows_two = small_call(
+        third_rows_kernel,
+        [wide, square, wide],
+        before + (back, rows_two, rows_two_other, skeleton_0, skeleton_1, tilt),
+    )
+    coupling_1, skeleton_2, projected_2, kept, sent = level_call(
         functools.partial(third_kernel, len(parts)),
-        [VMEM] * (len(parts) + 7) + [ANY] * 4,
-        [square, wide, square, tall] + outgoing(1),
+        [VMEM] * (len(parts) + 5) + [ANY] * 4,
+        [square, wide, tall] + outgoing(1),
         [s_buf, pltpu.VMEM((row_count, samples), jnp.float32), p_buf, p_buf, p_buf, sems(5)],
         8 * 10 ** 9,
-        parts + (inverse_1, rows_two, swap(rows_two, "core"), skeleton_0, skeleton_1, tilt, e02,
-                 projected_0, projected_1, sample, probes),
-        in_hbm=3,
-    )
-    inverse_2 = invert(gram)
+        parts + (inverse_1, rows_two, low, e02, skeleton_1, projected_0, projected_1, sample, probes),
+        in_hbm=2,
+    )
+    inverse_2 = invert(skeleton_2)
     terms = kept + swap(sent, "core")
     if chips_of(chips[2]) == 2:
         arrived = swap(terms, "blk")

time: 136 us -> 130 us (0.956)
  waiting for transfers between devices: 49.9 us -> 40.9 us
  starting transfers between devices: 27.1 us -> 29 us
    ppermute x26 -> x25, waiting for transfers between devices: 45.3 us -> 35.1 us  [swap(): return lax.ppermute(block, axis, [(0, 1), (1, 0)])]
    pallas_call x5, Pallas kernels: 33.1 us -> 30.2 us  [level_call(): pl.pallas_call(kernel, out_shape=outs, in_specs=specs, out_specs=[ANY if...]
    pallas_call x6 -> x8, Pallas kernels: 12.2 us -> 14.6 us  [the longest x3 7.74 us: invert_first(): pl.pallas_call(first_half_kernel, out_shape=[square] * 2, in_specs=[VMEM]...]
    ppermute x0 -> x2, waiting for transfers between devices: none -> 1.83 us  [cross_swap(): return lax.ppermute(block, ('n1', 'n2'), [(0, 3), (1, 2), (2, 1), (3, 0)])]
    ppermute x26 -> x25, starting transfers between devices: 18.8 us -> 19.7 us  [swap(): return lax.ppermute(block, axis, [(0, 1), (1, 0)])]
  transfers between devices with their start and end apart: 28 -> 29, of which waited for: 23 -> 21; matrix products, arithmetic and copies ran while one was open for 0% -> 0% of each run, Pallas kernels for 24% -> 30%
where the time goes in v2:
time: 130 us; the launch traced here: 129 us
  Pallas kernels  56.5 us (43%)
  waiting for transfers between devices  40.9 us (31%)
  starting transfers between devices  29 us (22%)
    ppermute x25, waiting for transfers between devices, swap(): return lax.ppermute(block, axis, [(0, 1), (1, 0)])  35.1 us
    pallas_call x5, Pallas kernels, level_call(): pl.pallas_call(kernel, out_shape=outs, in_specs=specs, out_specs=[ANY if...  30.2 us
    ppermute x25, starting transfers between devices, swap(): return lax.ppermute(block, axis, [(0, 1), (1, 0)])  19.7 us
    pallas_call x3, Pallas kernels, pick(): pl.pallas_call(functools.partial(pick_kernel, wanted, sizes), out_shape=[...  10.3 us
    all_to_all x2, starting transfers between devices, exchange(): return lax.all_to_all(pieces, axes, 0, 0, tiled=True)  8.09 us
    pallas_call x3, Pallas kernels, invert_first(): pl.pallas_call(first_half_kernel, out_shape=[square] * 2, in_specs=[VMEM]...  7.74 us
    pallas_call x3, Pallas kernels, invert_second(): pl.pallas_call(second_half_kernel, out_shape=arr(*state.shape), in_specs=...  5.8 us
    all_to_all x2, waiting for transfers between devices, exchange(): return lax.all_to_all(pieces, axes, 0, 0, tiled=True)  3.98 us
  transfers between devices with their start and end apart: 29, of which 21 were waited for; matrix products, arithmetic and copies ran while one was open for 0% of the time, Pallas kernels for 30%

profile of v2, /device:TPU:0, one launch (start us, length us, event | category | flops | bytes accessed | tf_op | source)
XLA Modules:
  0.0 129.1 jit_solution(8746306852840204806)
XLA Ops:
  1.3 2.4 %shard_map.50 = (f32[1,64,512]{2,1,0:T(8,128)S(1)}, f32[1,64,512]{2,1,0:T(8,128)S(1)}) custom-call(s32[14,128]{1,0:T(8,128)S(1)} %copy-done, f32[3,896,512]{2,1,0:T(8,128)} %refs_11_.1), custom_call_target="tpu_custom_call" | custom-call | flops 1000000000 | bytes 1835008 | tf_op jit(solution)/shard_map/pallas_call | solution.py:233
  5.2 2.9 %collective-permute-start.1 = (f32[64,512]{1,0:T(8,128)S(1)}, f32[64,512]{1,0:T(8,128)S(1)}, u32[]{:S(2)}, u32[]{:S(2)}) collective-permute-start(f32[64,512]{1,0:T(8,128)S(1)} %bitcast_add_fusion), channel_id=1, source_target_pairs={{0,1},{1,0},{2,3},{3,2},{4,5},{5,4},{6,7},{7,6},{8,9},{9,8},{10,11... | collective-permute-start | bytes 393224 | tf_op jit(solution)/shard_map/ppermute | solution.py:446
  8.2 3.8 %collective-permute-done.1 = f32[64,512]{1,0:T(8,128)S(1)} collective-permute-done((f32[64,512]{1,0:T(8,128)S(1)}, f32[64,512]{1,0:T(8,128)S(1)}, u32[]{:S(2)}, u32[]{:S(2)}) %collective-permute-start.1) | collective-permute-done | bytes 131104 | tf_op jit(solution)/shard_map/ppermute | solution.py:446
  15.5 3.4 %shard_map.51 = (f32[2,64,512]{2,1,0:T(8,128)S(1)}, f32[2,64,512]{2,1,0:T(8,128)S(1)}) custom-call(s32[14,128]{1,0:T(8,128)S(1)} %copy-done, f32[3,896,512]{2,1,0:T(8,128)} %refs_11_.1, f32[3,896,512]{2,1,0:T(8,128)} %refs_11_.1), custom_call_target="tpu_custom_call" | custom-call | flops 2000000000 | bytes 3670016 | tf_op jit(solution)/shard_map/pallas_call | solution.py:233
  24.5 4.6 %shard_map.52 = (f32[128,512]{1,0:T(8,128)S(1)}, f32[896,128]{1,0:T(8,128)S(1)}, f32[256,384]{1,0:T(8,128)S(1)}, f32[256,384]{1,0:T(8,128)S(1)}) custom-call(f32[64,512]{1,0:T(8,128)S(1)} %add_add_fusion.mine_ref, f32[64,512]{1,0:T(8,128)S(1)} %collective-permute-done.5.other_ref, f32[3,896,512]{2,1,0:T(8,128)} %refs_11_.1, f32[3,896,512]{2,1,0:T(8,128)} %refs_12_.1), custom_call_target="tpu_custom_call" | custom-call | flops 3000000000 | bytes 4000000 | tf_op jit(solution)/shard_map/pallas_call | solution.py:423
  33.7 4.5 %all-to-all-start = ((f32[8,32,384]{2,1,0:T(8,128)}), f32[8,32,384]{2,1,0:T(8,128)S(1)}, u32[]{:S(2)}, u32[]{:S(2)}) async-start(f32[8,32,384]{2,1,0:T(8,128)} %bitcast.2), calls=%async_computation | async-start | bytes 786432 | tf_op jit(solution)/shard_map/all_to_all | solution.py:463
  38.2 2.6 %shard_map.53 = (f32[128,128]{1,0:T(8,128)S(1)}, f32[128,128]{1,0:T(8,128)S(1)}) custom-call(f32[128,512]{1,0:T(8,128)S(1)} %get-tuple-element.75.skel_ref.skel0_ref), custom_call_target="tpu_custom_call" | custom-call | flops 2000000000 | bytes 100000 | tf_op jit(solution)/shard_map/pallas_call | solution.py:164
  40.8 2.1 %collective-permute-start.10 = (f32[2,64,512]{2,1,0:T(8,128)S(1)}, f32[2,64,512]{2,1,0:T(8,128)S(1)}, u32[]{:S(2)}, u32[]{:S(2)}) collective-permute-start(f32[2,64,512]{2,1,0:T(8,128)S(1)} %add.42), channel_id=1, source_target_pairs={{0,4},{4,0},{1,5},{5,1},{2,6},{6,2},{3,7},{7,3},{8,12},{12,8},{9,1... | collective-permute-start | bytes 786440 | tf_op jit(solution)/shard_map/ppermute | solution.py:446
  46.6 2.6 %collective-permute-start.9 = (f32[5,32,128]{2,1,0:T(8,128)S(1)}, f32[5,32,128]{2,1,0:T(8,128)S(1)}, u32[]{:S(2)}, u32[]{:S(2)}) collective-permute-start(f32[5,32,128]{2,1,0:T(8,128)S(1)} %shard_map.55), channel_id=1, source_target_pairs={{0,16},{16,0},{1,17},{17,1},{2,18},{18,2},{3,19},{19,3},{4,20},{20... | collective-permute-start | bytes 245768 | tf_op jit(solution)/shard_map/ppermute | solution.py:446
  53.6 3.6 %all-to-all-start.1 = ((f32[8,32,384]{2,1,0:T(8,128)}), f32[8,32,384]{2,1,0:T(8,128)S(1)}, u32[]{:S(2)}, u32[]{:S(2)}) async-start(f32[8,32,384]{2,1,0:T(8,128)} %shard_map.56), calls=%async_computation.1 | async-start | bytes 786432 | tf_op jit(solution)/shard_map/all_to_all | solution.py:463
  57.3 4.5 %shard_map.57 = (f32[3,64,512]{2,1,0:T(8,128)S(1)}, f32[3,64,512]{2,1,0:T(8,128)S(1)}) custom-call(s32[14,128]{1,0:T(8,128)S(1)} %copy-done.1, f32[3,896,512]{2,1,0:T(8,128)} %refs_11_.1, f32[3,896,512]{2,1,0:T(8,128)} %refs_11_.1, f32[3,896,512]{2,1,0:T(8,128)} %refs_11_.1), custom_call_target="tpu_custom_call" | custom-call | flops 3000000000 | bytes 5505024 | tf_op jit(solution)/shard_map/pallas_call | solution.py:233
  61.8 2.4 %all-to-all-done.1 = f32[8,32,384]{2,1,0:T(8,128)S(1)} async-done(((f32[8,32,384]{2,1,0:T(8,128)}), f32[8,32,384]{2,1,0:T(8,128)S(1)}, u32[]{:S(2)}, u32[]{:S(2)}) %all-to-all-start.1) | async-done | bytes 393248 | tf_op jit(solution)/shard_map/all_to_all | solution.py:463
  64.7 2.1 %collective-permute-done.13.rows_other = f32[2,64,512]{2,1,0:T(8,128)S(1)} collective-permute-done((f32[2,64,512]{2,1,0:T(8,128)S(1)}, f32[2,64,512]{2,1,0:T(8,128)S(1)}, u32[]{:S(2)}, u32[]{:S(2)}) %collective-permute-start.13) | collective-permute-done | bytes 262176 | tf_op jit(solution)/shard_map/ppermute | solution.py:446
  67.5 8.5 %shard_map.59 = (f32[128,128]{1,0:T(8,128)S(1)}, f32[128,128]{1,0:T(8,128)S(1)}, f32[128,512]{1,0:T(8,128)S(1)}, f32[128,128]{1,0:T(8,128)S(1)}, f32[896,128]{1,...) custom-call(f32[256,384]{1,0:T(8,128)S(1)} %bitcast.13, ...), custom_call_target="tpu_custom_call" | custom-call | flops 8000000000 | bytes 4000000 | tf_op jit(solution)/shard_map/pallas_call | solution.py:423
  76.0 2.4 %collective-permute-done.14 = f32[3,64,512]{2,1,0:T(8,128)S(1)} collective-permute-done((f32[3,64,512]{2,1,0:T(8,128)S(1)}, f32[3,64,512]{2,1,0:T(8,128)S(1)}, u32[]{:S(2)}, u32[]{:S(2)}) %collective-permute-start.14) | collective-permute-done | bytes 393248 | tf_op jit(solution)/shard_map/ppermute | solution.py:446
  78.6 2.6 %shard_map.61 = (f32[128,128]{1,0:T(8,128)S(1)}, f32[128,128]{1,0:T(8,128)S(1)}) custom-call(f32[128,512]{1,0:T(8,128)S(1)} %get-tuple-element.100.skel_ref.skel1_ref.refs_8_), custom_call_target="tpu_custom_call" | custom-call | flops 2000000000 | bytes 100000 | tf_op jit(solution)/shard_map/pallas_call | solution.py:164
  84.0 3.2 %collective-permute-done.16 = f32[128,256]{1,0:T(8,128)S(1)} collective-permute-done((f32[128,256]{1,0:T(8,128)S(1)}, f32[128,256]{1,0:T(8,128)S(1)}, u32[]{:S(2)}, u32[]{:S(2)}) %collective-permute-start.16) | collective-permute-done | bytes 131104 | tf_op jit(solution)/shard_map/ppermute | solution.py:446
  89.5 4.0 %collective-permute-done.18.refs_1_ = f32[1,128,128]{2,1,0:T(8,128)S(1)} collective-permute-done((f32[1,128,128]{2,1,0:T(8,128)S(1)}, f32[1,128,128]{2,1,0:T(8,128)S(1)}, u32[]{:S(2)}, u32[]{:S(2)}) %collective-permute-start.18) | collective-permute-done | bytes 65568 | tf_op jit(solution)/shard_map/ppermute | solution.py:446
  94.7 4.1 %collective-permute-done.19.refs_1_ = f32[128,256]{1,0:T(8,128)S(1)} collective-permute-done((f32[128,256]{1,0:T(8,128)S(1)}, f32[128,256]{1,0:T(8,128)S(1)}, u32[]{:S(2)}, u32[]{:S(2)}) %collective-permute-start.19) | collective-permute-done | bytes 131104 | tf_op jit(solution)/shard_map/ppermute | solution.py:446
  100.1 8.5 %shard_map.66 = (f32[128,128]{1,0:T(8,128)S(1)}, f32[128,512]{1,0:T(8,128)S(1)}, f32[896,128]{1,0:T(8,128)S(1)}, f32[256,128]{1,0:T(8,128)S(1)}, f32[256,128]{1,0:T(8,128)S(1)}) custom-call(f32[128,256]{1,0:T(8,128)S(1)} %bitcast.21, f32[128,256]{1,0:T(8,128)S(1)} %collective-permute-done.19.refs_1_, f32[128,256]{1,0:T(8,128)S(1)} %collective-permute-done.20.refs_2_, ...), custom_call_target="tpu_custom_call" | custom-call | flops 8000000000 | bytes 4000000 | tf_op jit(solution)/shard_map/pallas_call | solution.py:423
  108.8 2.6 %shard_map.67 = (f32[128,128]{1,0:T(8,128)S(1)}, f32[128,128]{1,0:T(8,128)S(1)}) custom-call(f32[128,512]{1,0:T(8,128)S(1)} %get-tuple-element.116.skel_ref), custom_call_target="tpu_custom_call" | custom-call | flops 2000000000 | bytes 100000 | tf_op jit(solution)/shard_map/pallas_call | solution.py:164
  114.3 2.9 %collective-permute-done.24 = f32[256,128]{1,0:T(8,128)S(1)} collective-permute-done((f32[256,128]{1,0:T(8,128)S(1)}, f32[256,128]{1,0:T(8,128)S(1)}, u32[]{:S(2)}, u32[]{:S(2)}) %collective-permute-start.24) | collective-permute-done | bytes 131104 | tf_op jit(solution)/shard_map/ppermute | solution.py:446
  118.8 3.2 %shard_map.70 = f32[3,896,128]{2,1,0:T(8,128)} custom-call(f32[896,128]{1,0:T(8,128)S(1)} %get-tuple-element.93.p0_hbm.refs_9_, f32[896,128]{1,0:T(8,128)S(1)} %get-tuple-element.113.refs_10_.p1_hbm, f32[896,128]{1,0:T(8,128)S(1)} %get-tuple-element.121.p2_hbm, f32[128,128]{1,0:T(8,128)S(1)} %shard_map.54.refs_1_.ours_ref.inverse_0, ...), custom_call_target="tpu_custom_call" | custom-call | flops 4000000000 | bytes 4000000 | tf_op jit(solution)/shard_map/pallas_call | solution.py:423
  123.8 5.3 %shard_map.71 = f32[3,1,128,128]{3,2,1,0:T(8,128)} custom-call(f32[256,128]{1,0:T(8,128)S(1)} %collective-permute-done.25.mine_ref, f32[256,128]{1,0:T(8,128)S(1)} %collective-permute-done.26.other_ref, f32[128,512]{1,0:T(8,128)S(1)} %get-tuple-element.116.skel_ref, f32[128,128]{1,0:T(8,128)S(1)} %get-tuple-element.124.c0_ref, ...), custom_call_target="tpu_custom_call" | custom-call | flops 5000000000 | bytes 4000000 | tf_op jit(solution)/shard_map/pallas_call | solution.py:423
  (71 shorter events, 39.3 us)
Async XLA Ops:
  5.2 6.7 %collective-permute-start.1 = (f32[64,512]{1,0:T(8,128)S(1)}, f32[64,512]{1,0:T(8,128)S(1)}, u32[]{:S(2)}, u32[]{:S(2)}) collective-permute-start(f32[64,512]{1,0:T(8,128)S(1)} %bitcast_add_fusion), channel_id=1, source_target_pairs={{0,1},{1,0},{2,3},{3,2},{4,5},{5,4},{6,7},{7,6},{8,9},{9,8},{10,11... | collective-permute-start | bytes 393224 | tf_op jit(solution)/shard_map/ppermute | solution.py:446
  12.0 7.1 %collective-permute-start.2 = (f32[64,512]{1,0:T(8,128)S(1)}, f32[64,512]{1,0:T(8,128)S(1)}, u32[]{:S(2)}, u32[]{:S(2)}) collective-permute-start(f32[64,512]{1,0:T(8,128)S(1)} %add.37), channel_id=1, source_target_pairs={{0,4},{4,0},{1,5},{5,1},{2,6},{6,2},{3,7},{7,3},{8,12},{12,8},{9,1... | collective-permute-start | bytes 393224 | tf_op jit(solution)/shard_map/ppermute | solution.py:446
  13.8 5.8 %collective-permute-start.3 = (f32[64,512]{1,0:T(8,128)S(1)}, f32[64,512]{1,0:T(8,128)S(1)}, u32[]{:S(2)}, u32[]{:S(2)}) collective-permute-start(f32[64,512]{1,0:T(8,128)S(1)} %add.37), channel_id=1, source_target_pairs={{0,8},{8,0},{1,9},{9,1},{2,10},{10,2},{3,11},{11,3},{4,12},{12,4},... | collective-permute-start | bytes 393224 | tf_op jit(solution)/shard_map/ppermute | solution.py:446
  15.4 5.9 %collective-permute-start.4 = (f32[64,512]{1,0:T(8,128)S(1)}, f32[64,512]{1,0:T(8,128)S(1)}, u32[]{:S(2)}, u32[]{:S(2)}) collective-permute-start(f32[64,512]{1,0:T(8,128)S(1)} %add.37), channel_id=1, source_target_pairs={{0,12},{4,8},{8,4},{12,0},{1,13},{5,9},{9,5},{13,1},{2,14},{6,10},... | collective-permute-start | bytes 393224 | tf_op jit(solution)/shard_map/ppermute | solution.py:450
  19.0 2.4 %collective-permute-start.6 = (f32[2,64,512]{2,1,0:T(8,128)S(1)}, f32[2,64,512]{2,1,0:T(8,128)S(1)}, u32[]{:S(2)}, u32[]{:S(2)}) collective-permute-start(f32[2,64,512]{2,1,0:T(8,128)S(1)} %get-tuple-element.69), channel_id=1, source_target_pairs={{0,2},{2,0},{1,3},{3,1},{4,6},{6,4},{5,7},{7,5},{8,10},{10,8},{9,1... | collective-permute-start | bytes 786440 | tf_op jit(solution)/shard_map/ppermute | solution.py:446
  22.7 8.4 %collective-permute-start.7 = (f32[2,64,512]{2,1,0:T(8,128)S(1)}, f32[2,64,512]{2,1,0:T(8,128)S(1)}, u32[]{:S(2)}, u32[]{:S(2)}) collective-permute-start(f32[2,64,512]{2,1,0:T(8,128)S(1)} %add.41), channel_id=1, source_target_pairs={{0,1},{1,0},{2,3},{3,2},{4,5},{5,4},{6,7},{7,6},{8,9},{9,8},{10,11... | collective-permute-start | bytes 786440 | tf_op jit(solution)/shard_map/ppermute | solution.py:446
  33.7 12.7 %all-to-all-start = ((f32[8,32,384]{2,1,0:T(8,128)}), f32[8,32,384]{2,1,0:T(8,128)S(1)}, u32[]{:S(2)}, u32[]{:S(2)}) async-start(f32[8,32,384]{2,1,0:T(8,128)} %bitcast.2), calls=%async_computation | async-start | bytes 786432 | tf_op jit(solution)/shard_map/all_to_all | solution.py:463
  40.8 10.5 %collective-permute-start.10 = (f32[2,64,512]{2,1,0:T(8,128)S(1)}, f32[2,64,512]{2,1,0:T(8,128)S(1)}, u32[]{:S(2)}, u32[]{:S(2)}) collective-permute-start(f32[2,64,512]{2,1,0:T(8,128)S(1)} %add.42), channel_id=1, source_target_pairs={{0,4},{4,0},{1,5},{5,1},{2,6},{6,2},{3,7},{7,3},{8,12},{12,8},{9,1... | collective-permute-start | bytes 786440 | tf_op jit(solution)/shard_map/ppermute | solution.py:446
  46.6 6.3 %collective-permute-start.9 = (f32[5,32,128]{2,1,0:T(8,128)S(1)}, f32[5,32,128]{2,1,0:T(8,128)S(1)}, u32[]{:S(2)}, u32[]{:S(2)}) collective-permute-start(f32[5,32,128]{2,1,0:T(8,128)S(1)} %shard_map.55), channel_id=1, source_target_pairs={{0,16},{16,0},{1,17},{17,1},{2,18},{18,2},{3,19},{19,3},{4,20},{20... | collective-permute-start | bytes 245768 | tf_op jit(solution)/shard_map/ppermute | solution.py:446
  53.6 10.5 %all-to-all-start.1 = ((f32[8,32,384]{2,1,0:T(8,128)}), f32[8,32,384]{2,1,0:T(8,128)S(1)}, u32[]{:S(2)}, u32[]{:S(2)}) async-start(f32[8,32,384]{2,1,0:T(8,128)} %shard_map.56), calls=%async_computation.1 | async-start | bytes 786432 | tf_op jit(solution)/shard_map/all_to_all | solution.py:463
  64.2 3.0 %collective-permute-start.12 = (f32[3,64,512]{2,1,0:T(8,128)S(1)}, f32[3,64,512]{2,1,0:T(8,128)S(1)}, u32[]{:S(2)}, u32[]{:S(2)}) collective-permute-start(f32[3,64,512]{2,1,0:T(8,128)S(1)} %get-tuple-element.87), channel_id=1, source_target_pairs={{0,2},{2,0},{1,3},{3,1},{4,6},{6,4},{5,7},{7,5},{8,10},{10,8},{9,1... | collective-permute-start | bytes 1179656 | tf_op jit(solution)/shard_map/ppermute | solution.py:446
  64.2 3.0 %collective-permute-start.11 = (f32[256,384]{1,0:T(8,128)S(1)}, f32[256,384]{1,0:T(8,128)S(1)}, u32[]{:S(2)}, u32[]{:S(2)}) collective-permute-start(f32[256,384]{1,0:T(8,128)S(1)} %bitcast.12), channel_id=1, source_target_pairs={{0,2},{2,0},{1,3},{3,1},{4,6},{6,4},{5,7},{7,5},{8,10},{10,8},{9,1... | collective-permute-start | bytes 1179656 | tf_op jit(solution)/shard_map/ppermute | solution.py:446
  64.7 2.1 %collective-permute-start.13 = (f32[2,64,512]{2,1,0:T(8,128)S(1)}, f32[2,64,512]{2,1,0:T(8,128)S(1)}, u32[]{:S(2)}, u32[]{:S(2)}) collective-permute-start(f32[2,64,512]{2,1,0:T(8,128)S(1)} %add.44.rows_mine), channel_id=1, source_target_pairs={{0,2},{2,0},{1,3},{3,1},{4,6},{6,4},{5,7},{7,5},{8,10},{10,8},{9,1... | collective-permute-start | bytes 786440 | tf_op jit(solution)/shard_map/ppermute | solution.py:446
  67.2 11.2 %collective-permute-start.14 = (f32[3,64,512]{2,1,0:T(8,128)S(1)}, f32[3,64,512]{2,1,0:T(8,128)S(1)}, u32[]{:S(2)}, u32[]{:S(2)}) collective-permute-start(f32[3,64,512]{2,1,0:T(8,128)S(1)} %add.45), channel_id=1, source_target_pairs={{0,1},{1,0},{2,3},{3,2},{4,5},{5,4},{6,7},{7,6},{8,9},{9,8},{10,11... | collective-permute-start | bytes 1179656 | tf_op jit(solution)/shard_map/ppermute | solution.py:446
  78.5 3.2 %collective-permute-start.15 = (f32[256,256]{1,0:T(8,128)S(1)}, f32[256,256]{1,0:T(8,128)S(1)}, u32[]{:S(2)}, u32[]{:S(2)}) collective-permute-start(f32[256,256]{1,0:T(8,128)S(1)} %get-tuple-element.97), channel_id=1, source_target_pairs={{0,2},{2,0},{1,3},{3,1},{4,6},{6,4},{5,7},{7,5},{8,10},{10,8},{9,1... | collective-permute-start | bytes 786440 | tf_op jit(solution)/shard_map/ppermute | solution.py:446
  81.2 17.6 %collective-permute-start.22 = (f32[3,64,512]{2,1,0:T(8,128)S(1)}, f32[3,64,512]{2,1,0:T(8,128)S(1)}, u32[]{:S(2)}, u32[]{:S(2)}) collective-permute-start(f32[3,64,512]{2,1,0:T(8,128)S(1)} %add.46.rows_mine), channel_id=1, source_target_pairs={{0,2},{2,0},{1,3},{3,1},{4,6},{6,4},{5,7},{7,5},{8,10},{10,8},{9,1... | collective-permute-start | bytes 1179656 | tf_op jit(solution)/shard_map/ppermute | solution.py:446
  81.7 5.5 %collective-permute-start.16 = (f32[128,256]{1,0:T(8,128)S(1)}, f32[128,256]{1,0:T(8,128)S(1)}, u32[]{:S(2)}, u32[]{:S(2)}) collective-permute-start(f32[128,256]{1,0:T(8,128)S(1)} %get-tuple-element.99), channel_id=1, source_target_pairs={{0,1},{1,0},{2,3},{3,2},{4,5},{5,4},{6,7},{7,6},{8,9},{9,8},{10,11... | collective-permute-start | bytes 393224 | tf_op jit(solution)/shard_map/ppermute | solution.py:446
  87.4 6.2 %collective-permute-start.17 = (f32[2,128,128]{2,1,0:T(8,128)S(1)}, f32[2,128,128]{2,1,0:T(8,128)S(1)}, u32[]{:S(2)}, u32[]{:S(2)}) collective-permute-start(f32[2,128,128]{2,1,0:T(8,128)S(1)} %shard_map.63), channel_id=1, source_target_pairs={{0,12},{4,8},{8,4},{12,0},{1,13},{5,9},{9,5},{13,1},{2,14},{6,10},... | collective-permute-start | bytes 393224 | tf_op jit(solution)/shard_map/ppermute | solution.py:450
  88.5 4.9 %collective-permute-start.18 = (f32[1,128,128]{2,1,0:T(8,128)S(1)}, f32[1,128,128]{2,1,0:T(8,128)S(1)}, u32[]{:S(2)}, u32[]{:S(2)}) collective-permute-start(f32[1,128,128]{2,1,0:T(8,128)S(1)} %slice.4), channel_id=1, source_target_pairs={{0,8},{8,0},{1,9},{9,1},{2,10},{10,2},{3,11},{11,3},{4,12},{12,4},... | collective-permute-start | bytes 196616 | tf_op jit(solution)/shard_map/ppermute | solution.py:446
  93.7 5.0 %collective-permute-start.19 = (f32[128,256]{1,0:T(8,128)S(1)}, f32[128,256]{1,0:T(8,128)S(1)}, u32[]{:S(2)}, u32[]{:S(2)}) collective-permute-start(f32[128,256]{1,0:T(8,128)S(1)} %bitcast.19), channel_id=1, source_target_pairs={{0,1},{1,0},{2,3},{3,2},{4,5},{5,4},{6,7},{7,6},{8,9},{9,8},{10,11... | collective-permute-start | bytes 393224 | tf_op jit(solution)/shard_map/ppermute | solution.py:446
  94.7 4.9 %collective-permute-start.20 = (f32[128,256]{1,0:T(8,128)S(1)}, f32[128,256]{1,0:T(8,128)S(1)}, u32[]{:S(2)}, u32[]{:S(2)}) collective-permute-start(f32[128,256]{1,0:T(8,128)S(1)} %bitcast.20), channel_id=1, source_target_pairs={{0,2},{2,0},{1,3},{3,1},{4,6},{6,4},{5,7},{7,5},{8,10},{10,8},{9,1... | collective-permute-start | bytes 393224 | tf_op jit(solution)/shard_map/ppermute | solution.py:446
  108.6 2.8 %collective-permute-start.23 = (f32[256,128]{1,0:T(8,128)S(1)}, f32[256,128]{1,0:T(8,128)S(1)}, u32[]{:S(2)}, u32[]{:S(2)}) collective-permute-start(f32[256,128]{1,0:T(8,128)S(1)} %get-tuple-element.115), channel_id=1, source_target_pairs={{0,2},{2,0},{1,3},{3,1},{4,6},{6,4},{5,7},{7,5},{8,10},{10,8},{9,1... | collective-permute-start | bytes 393224 | tf_op jit(solution)/shard_map/ppermute | solution.py:446
  111.4 5.8 %collective-permute-start.24 = (f32[256,128]{1,0:T(8,128)S(1)}, f32[256,128]{1,0:T(8,128)S(1)}, u32[]{:S(2)}, u32[]{:S(2)}) collective-permute-start(f32[256,128]{1,0:T(8,128)S(1)} %add.47), channel_id=1, source_target_pairs={{0,1},{1,0},{2,3},{3,2},{4,5},{5,4},{6,7},{7,6},{8,9},{9,8},{10,11... | collective-permute-start | bytes 393224 | tf_op jit(solution)/shard_map/ppermute | solution.py:446
  117.4 5.0 %collective-permute-start.25 = (f32[256,128]{1,0:T(8,128)S(1)}, f32[256,128]{1,0:T(8,128)S(1)}, u32[]{:S(2)}, u32[]{:S(2)}) collective-permute-start(f32[256,128]{1,0:T(8,128)S(1)} %bitcast.16), channel_id=1, source_target_pairs={{0,4},{4,0},{1,5},{5,1},{2,6},{6,2},{3,7},{7,3},{8,12},{12,8},{9,1... | collective-permute-start | bytes 393224 | tf_op jit(solution)/shard_map/ppermute | solution.py:446
  (7 other events, 24.6 us)

commit v3 on v2

--- a/solution.py
+++ b/solution.py
@@ -163,14 +163,14 @@
     square = arr(skeleton.shape[0], skeleton.shape[0])
     return pl.pallas_call(
         first_half_kernel, out_shape=[square] * 2, in_specs=[VMEM], out_specs=[VMEM] * 2,
-        compiler_params=SMALL, cost_estimate=cost(2 * 10 ** 9, 10 ** 5),
+        compiler_params=SMALL, cost_estimate=cost(10 ** 8, 10 ** 5),
     )(skeleton)
 
 
 def invert_second(state, scales):
     return pl.pallas_call(
         second_half_kernel, out_shape=arr(*state.shape), in_specs=[VMEM] * 2, out_specs=VMEM,
-        compiler_params=SMALL, cost_estimate=cost(2 * 10 ** 9, 10 ** 5),
+        compiler_params=SMALL, cost_estimate=cost(10 ** 8, 10 ** 5),
     )(state, scales)
 
 
@@ -285,6 +285,16 @@
     return low, high
 
 
+def ordered_pairs(parts, axis):
+    first = lax.axis_index("blk") == 0
+    near, far = [
+        jnp.concatenate([jnp.where(first, one, two), jnp.where(first, two, one)], axis=axis)
+        for one, two in ((parts[0][...], parts[1][...]), (parts[2][...], parts[3][...]))
+    ]
+    here = lax.axis_index("core") == 0
+    return jnp.where(here, near, far), jnp.where(here, far, near)
+
+
 def joined(low, high, kind):
     return jnp.concatenate([half[:, kind * WIDTH:(kind + 1) * WIDTH] for half in (low, high)], axis=0)
 
@@ -324,8 +334,9 @@
     leaving[0].wait()
 
 
-def second_rows_kernel(rows_mine, rows_other, skel0_ref, low_ref, rows_ref):
-    rows_low, rows_high = ordered(rows_mine, rows_other)
+def second_rows_kernel(*refs):
+    parts, (skel0_ref, low_ref, rows_ref) = refs[:-3], refs[-3:]
+    rows_low, rows_high = ordered(*parts) if len(parts) == 2 else ordered_pairs(parts, 1)
     samples = skel0_ref.shape[1]
     low_ref[...] = dot3(whole_rows(rows_low, rows_high, 0), skel0_ref[...], 1, 1) * (1.0 / samples)
     rows_ref[...] = whole_rows(rows_low, rows_high, 1)
@@ -356,8 +367,8 @@
     leaving[0].wait()
 
 
-def third_rows_kernel(mine_ref, other_ref, back_ref, rows_mine, rows_other, skel0_ref, skel1_ref, tilt_ref,
-                      e02_ref, low_ref, rows_ref):
+def third_rows_kernel(mine_ref, other_ref, back_ref, rows_mine, rows_other, last_mine, last_other,
+                      skel0_ref, skel1_ref, tilt_ref, e02_ref, low_ref, rows_ref):
     share = 1.0 / skel0_ref.shape[1]
     low, high = ordered(mine_ref, other_ref)
     rows_low, rows_high = ordered(rows_mine, rows_other)
@@ -367,7 +378,7 @@
     low_ref[...] = (
         dot3(whole_rows(rows_low, rows_high, 1), skel1_ref[...], 1, 1) - dot3(low_0, tilt_ref[...])
     ) * share
-    rows_ref[...] = whole_rows(rows_low, rows_high, 2) - dot3(low_0, e02)
+    rows_ref[...] = whole_rows(*ordered(last_mine, last_other), 0) - dot3(low_0, e02)
 
 
 def third_kernel(pieces, *refs):
@@ -376,17 +387,7 @@
      c1_ref, skel_ref, p_hbm, kept_ref, sent_ref, s_buf, t_buf, p_ref, p0_ref, p1_ref, sems) = refs
     samples = skel1_ref.shape[1]
     running = copies([(s_hbm.at[2], s_buf), (p0_hbm, p0_ref), (p1_hbm, p1_ref), (t_hbm.at[2], t_buf)], sems)
-    if pieces == 2:
-        low, high = ordered(*parts)
-    else:
-        first = lax.axis_index("blk") == 0
-        both = [
-            jnp.concatenate([jnp.where(first, one, two), jnp.where(first, two, one)], axis=0)
-            for one, two in ((parts[0][...], parts[1][...]), (parts[2][...], parts[3][...]))
-        ]
-        here = lax.axis_index("core") == 0
-        low = jnp.where(here, both[0], both[1])
-        high = jnp.where(here, both[1], both[0])
+    low, high = ordered(*parts) if pieces == 2 else ordered_pairs(parts, 0)
     e02 = e02_ref[...]
     coupling = couple(skel1_ref[...], joined(low, high, 0))
     c1_ref[...] = coupling
@@ -499,18 +500,19 @@
 
 
 def add_split_kernel(axis, one_ref, two_ref, kept_ref, sent_ref):
-    total = one_ref[...] + two_ref[...]
-    half = kept_ref.shape[0]
+    half = kept_ref.shape[-2]
     first = lax.axis_index(axis) == 0
-    kept_ref[...] = jnp.where(first, total[:half], total[half:])
-    sent_ref[...] = jnp.where(first, total[half:], total[:half])
+    for at in range(kept_ref.shape[0]):
+        total = one_ref[at] + two_ref[at]
+        kept_ref[at] = jnp.where(first, total[:half], total[half:])
+        sent_ref[at] = jnp.where(first, total[half:], total[:half])
 
 
 def add_split(one, two, axis):
-    rows, width = one.shape
+    count, rows, width = one.shape
     return pl.pallas_call(
         functools.partial(add_split_kernel, axis),
-        out_shape=[arr(rows // 2, width)] * 2,
+        out_shape=[arr(count, rows // 2, width)] * 2,
         in_specs=[VMEM] * 2,
         out_specs=[VMEM] * 2,
         compiler_params=SMALL,
@@ -560,10 +562,16 @@
     half, lists = held(half, skeleton_rows)
     half = total_over(half, ("mid", "blk"))
     rest_kept, rest_sent = pick(lists, sample, ((1, 0), (1, 1)), sizes)
-    rest = rest_kept + swap(rest_sent, "core")
     half = half + swap(half, "n2") + swap(half, "n1") + cross_swap(half)
-    half_other, rest = held(swap(half, "core"), rest)
-    rest = total_over(rest, ("mid", "blk"))
+    pairs = chips_of(chips[2]) == 2
+    if pairs:
+        rest, moved = add_split(rest_kept, swap(rest_sent, "core"), "blk")
+        half_other, rest, moved = held(swap(half, "core"), rest, moved)
+        moved = swap(moved, "blk")
+    else:
+        rest = rest_kept + swap(rest_sent, "core")
+        half_other, rest = held(swap(half, "core"), rest)
+        moved = total_over(rest, ("mid", "blk"))
 
     skeleton_0, projected_0, kept, sent = level_call(
         first_kernel,
@@ -574,10 +582,11 @@
         (half, half_other, sample, probes),
         in_hbm=1,
     )
-    sent, rest = held(sent, rest)
-    terms = kept + swap(sent, "core")
-    inverse_0 = invert(skeleton_0)
-    rows_one = total_over(rest, ("n2",))
+    sent, moved = held(sent, moved)
+    received, skeleton_in = held(swap(sent, "core"), skeleton_0)
+    inverse_0 = invert(skeleton_in)
+    terms = kept + received
+    rows_one = total_over(rest + moved if pairs else moved, ("n2",))
     pieces = exchange(to_chunks(terms, chips_of(chips[0])), chips[0])
     pieces, inverse_0 = held(pieces, inverse_0)
     inner = chips_of(chips[2])
@@ -593,11 +602,14 @@
     mine = mine.reshape(samples // 2, levels * skel)
     mine, rest_kept, rest_sent = held(mine, rest_kept, rest_sent)
     other = swap(mine, "core")
-    rest = rest_kept + swap(rest_sent, "core")
+    rest_sent = swap(rest_sent, "core")
+    rest, last = rest_kept[:2] + rest_sent[:2], rest_kept[2:] + rest_sent[2:]
     mine, other, rest = held(mine, other, rest)
     rest = total_over(rest, ("mid", "blk"))
 
-    low, rows_one = small_call(second_rows_kernel, [square, wide], (rows_one, swap(rows_one, "core"), skeleton_0))
+    row_parts = (rows_one, swap(rows_one, "blk")) if pairs else (rows_one,)
+    row_parts += tuple(swap(part, "core") for part in row_parts)
+    low, rows_one = small_call(second_rows_kernel, [square, wide], row_parts + (skeleton_0,))
     coupling_0, back, skeleton_1, tilt, projected_1, kept, sent = level_call(
         second_kernel,
         [VMEM] * 6 + [ANY] * 3,
@@ -609,21 +621,23 @@
     )
     sent, rows_two = held(sent, rest)
     rows_two_other = swap(rows_two, "core")
-    inverse_1 = invert(skeleton_1)
     before = (mine, other)
-    if chips_of(chips[2]) == 2:
-        kept, sent = add_split(kept, swap(sent, "core"), "blk")
+    received, skeleton_in = held(swap(sent, "core"), skeleton_1)
+    inverse_1 = invert(skeleton_in)
+    if pairs:
+        kept, sent = [part[0] for part in add_split(kept[None], received[None], "blk")]
         arrived = swap(sent, "blk")
-        arrived, inverse_1 = held(arrived, inverse_1)
+        arrived, inverse_1, last = held(arrived, inverse_1, last)
         sums = combine([kept[None], arrived[None]], inverse_1, [(0, [(0, 0), (1, 0)]), (1, [(0, 0), (1, 0)])])
         far, beside = cross_swap(sums), swap(sums[:1], "n1")
         mine = fan_out([far, beside], [[[(0, 0), (1, 0)], [(0, 1)]]])[0]
-        mine, rows_two = held(mine, rows_two)
+        last = total_over(last, ("blk",))
+        mine, rows_two, last = held(mine, rows_two, last)
         beside = swap(mine, "blk")
         parts = (mine, beside, swap(mine, "core"), swap(beside, "core"))
     else:
-        terms = kept + swap(sent, "core")
-        pieces = exchange(to_chunks(terms, chips_of(chips[1])), chips[1])
+        last = total_over(last, ("mid", "blk"))
+        pieces = exchange(to_chunks(kept + received, chips_of(chips[1])), chips[1])
         pieces, inverse_1 = held(pieces, inverse_1)
         places = [two for two in range(2) for _ in range(inner)]
         every = range(len(places))
@@ -637,7 +651,7 @@
     e02, low, rows_two = small_call(
         third_rows_kernel,
         [wide, square, wide],
-        before + (back, rows_two, rows_two_other, skeleton_0, skeleton_1, tilt),
+        before + (back, rows_two, rows_two_other, last, swap(last, "core"), skeleton_0, skeleton_1, tilt),
     )
     coupling_1, skeleton_2, projected_2, kept, sent = level_call(
         functools.partial(third_kernel, len(parts)),
@@ -648,9 +662,10 @@
         parts + (inverse_1, rows_two, low, e02, skeleton_1, projected_0, projected_1, sample, probes),
         in_hbm=2,
     )
-    inverse_2 = invert(skeleton_2)
-    terms = kept + swap(sent, "core")
-    if chips_of(chips[2]) == 2:
+    received, skeleton_in = held(swap(sent, "core"), skeleton_2)
+    inverse_2 = invert(skeleton_in)
+    terms = kept + received
+    if pairs:
         arrived = swap(terms, "blk")
         arrived, inverse_2 = held(arrived, inverse_2)
         mine = combine([terms[None], arrived[None]], inverse_2, [(0, [(0, 0), (1, 0)])])

time: 130 us -> 129 us (level)
  waiting for transfers between devices: 40.9 us -> 37.1 us
  starting transfers between devices: 29 us -> 31.8 us
    ppermute x25 -> x29, starting transfers between devices: 19.7 us -> 23.4 us  [swap(): return lax.ppermute(block, axis, [(0, 1), (1, 0)])]
    ppermute x25 -> x29, waiting for transfers between devices: 35.1 us -> 31.4 us  [swap(): return lax.ppermute(block, axis, [(0, 1), (1, 0)])]
  transfers between devices with their start and end apart: 29 -> 33, of which waited for: 21 -> 20; matrix products, arithmetic and copies ran while one was open for 0% -> 0% of each run, Pallas kernels for 30% -> 31%
where the time goes in v3:
time: 129 us; the launch traced here: 128 us
  Pallas kernels  56.5 us (44%)
  waiting for transfers between devices  37.1 us (29%)
  starting transfers between devices  31.8 us (25%)
    ppermute x29, waiting for transfers between devices, swap(): return lax.ppermute(block, axis, [(0, 1), (1, 0)])  31.4 us
    pallas_call x5, Pallas kernels, level_call(): pl.pallas_call(kernel, out_shape=outs, in_specs=specs, out_specs=[ANY if...  30.1 us
    ppermute x29, starting transfers between devices, swap(): return lax.ppermute(block, axis, [(0, 1), (1, 0)])  23.4 us
    pallas_call x3, Pallas kernels, pick(): pl.pallas_call(functools.partial(pick_kernel, wanted, sizes), out_shape=[...  10.3 us
    pallas_call x3, Pallas kernels, invert_first(): pl.pallas_call(first_half_kernel, out_shape=[square] * 2, in_specs=[VMEM]...  7.74 us
    all_to_all x2, starting transfers between devices, exchange(): return lax.all_to_all(pieces, axes, 0, 0, tiled=True)  7.21 us
    pallas_call x3, Pallas kernels, invert_second(): pl.pallas_call(second_half_kernel, out_shape=arr(*state.shape), in_specs=...  5.88 us
    all_to_all x2, waiting for transfers between devices, exchange(): return lax.all_to_all(pieces, axes, 0, 0, tiled=True)  4.03 us
  transfers between devices with their start and end apart: 33, of which 20 were waited for; matrix products, arithmetic and copies ran while one was open for 0% of the time, Pallas kernels for 31%

profile of v3, /device:TPU:0, one launch (start us, length us, event | category | flops | bytes accessed | tf_op | source)
XLA Modules:
  0.0 128.1 jit_solution(9878368706453116509)
XLA Ops:
  1.3 2.4 %shard_map.50 = (f32[1,64,512]{2,1,0:T(8,128)S(1)}, f32[1,64,512]{2,1,0:T(8,128)S(1)}) custom-call(s32[14,128]{1,0:T(8,128)S(1)} %copy-done, f32[3,896,512]{2,1,0:T(8,128)} %refs_11_.1), custom_call_target="tpu_custom_call" | custom-call | flops 1000000000 | bytes 1835008 | tf_op jit(solution)/shard_map/pallas_call | solution.py:233
  5.2 2.9 %collective-permute-start.1 = (f32[64,512]{1,0:T(8,128)S(1)}, f32[64,512]{1,0:T(8,128)S(1)}, u32[]{:S(2)}, u32[]{:S(2)}) collective-permute-start(f32[64,512]{1,0:T(8,128)S(1)} %bitcast_add_fusion), channel_id=1, source_target_pairs={{0,1},{1,0},{2,3},{3,2},{4,5},{5,4},{6,7},{7,6},{8,9},{9,8},{10,11... | collective-permute-start | bytes 393224 | tf_op jit(solution)/shard_map/ppermute | solution.py:447
  8.2 3.8 %collective-permute-done.1 = f32[64,512]{1,0:T(8,128)S(1)} collective-permute-done((f32[64,512]{1,0:T(8,128)S(1)}, f32[64,512]{1,0:T(8,128)S(1)}, u32[]{:S(2)}, u32[]{:S(2)}) %collective-permute-start.1) | collective-permute-done | bytes 131104 | tf_op jit(solution)/shard_map/ppermute | solution.py:447
  15.5 3.4 %shard_map.51 = (f32[2,64,512]{2,1,0:T(8,128)S(1)}, f32[2,64,512]{2,1,0:T(8,128)S(1)}) custom-call(s32[14,128]{1,0:T(8,128)S(1)} %copy-done, f32[3,896,512]{2,1,0:T(8,128)} %refs_11_.1, f32[3,896,512]{2,1,0:T(8,128)} %refs_11_.1), custom_call_target="tpu_custom_call" | custom-call | flops 2000000000 | bytes 3670016 | tf_op jit(solution)/shard_map/pallas_call | solution.py:233
  24.5 4.6 %shard_map.53 = (f32[128,512]{1,0:T(8,128)S(1)}, f32[896,128]{1,0:T(8,128)S(1)}, f32[256,384]{1,0:T(8,128)S(1)}, f32[256,384]{1,0:T(8,128)S(1)}) custom-call(f32[64,512]{1,0:T(8,128)S(1)} %add_add_fusion.mine_ref, f32[64,512]{1,0:T(8,128)S(1)} %collective-permute-done.5.other_ref, f32[3,896,512]{2,1,0:T(8,128)} %refs_11_.1, f32[3,896,512]{2,1,0:T(8,128)} %refs_12_.1), custom_call_target="tpu_custom_call" | custom-call | flops 3000000000 | bytes 4000000 | tf_op jit(solution)/shard_map/pallas_call | solution.py:424
  31.7 3.6 %all-to-all-start = ((f32[8,32,384]{2,1,0:T(8,128)}), f32[8,32,384]{2,1,0:T(8,128)S(1)}, u32[]{:S(2)}, u32[]{:S(2)}) async-start(f32[8,32,384]{2,1,0:T(8,128)} %bitcast.2), calls=%async_computation | async-start | bytes 786432 | tf_op jit(solution)/shard_map/all_to_all | solution.py:464
  35.3 2.1 %collective-permute-start.10 = (f32[2,32,512]{2,1,0:T(8,128)S(1)}, f32[2,32,512]{2,1,0:T(8,128)S(1)}, u32[]{:S(2)}, u32[]{:S(2)}) collective-permute-start(f32[2,32,512]{2,1,0:T(8,128)S(1)} %add.45), channel_id=1, source_target_pairs={{0,4},{4,0},{1,5},{5,1},{2,6},{6,2},{3,7},{7,3},{8,12},{12,8},{9,1... | collective-permute-start | bytes 393224 | tf_op jit(solution)/shard_map/ppermute | solution.py:447
  37.4 2.6 %shard_map.54 = (f32[128,128]{1,0:T(8,128)S(1)}, f32[128,128]{1,0:T(8,128)S(1)}) custom-call(f32[128,512]{1,0:T(8,128)S(1)} %get-tuple-element.90.skel_ref.refs_4_.skel0_ref), custom_call_target="tpu_custom_call" | custom-call | flops 100000000 | bytes 100000 | tf_op jit(solution)/shard_map/pallas_call | solution.py:164
  40.0 2.0 %shard_map.55.refs_1_.ours_ref.inverse_0 = f32[128,128]{1,0:T(8,128)S(1)} custom-call(f32[128,128]{1,0:T(8,128)S(1)} %get-tuple-element.91.a_ref, f32[128,128]{1,0:T(8,128)S(1)} %get-tuple-element.92.scales_ref), custom_call_target="tpu_custom_call" | custom-call | flops 100000000 | bytes 100000 | tf_op jit(solution)/shard_map/pallas_call | solution.py:171
  43.8 2.6 %collective-permute-start.9 = (f32[5,32,128]{2,1,0:T(8,128)S(1)}, f32[5,32,128]{2,1,0:T(8,128)S(1)}, u32[]{:S(2)}, u32[]{:S(2)}) collective-permute-start(f32[5,32,128]{2,1,0:T(8,128)S(1)} %shard_map.56), channel_id=1, source_target_pairs={{0,16},{16,0},{1,17},{17,1},{2,18},{18,2},{3,19},{19,3},{4,20},{20... | collective-permute-start | bytes 245768 | tf_op jit(solution)/shard_map/ppermute | solution.py:447
  46.4 3.6 %collective-permute-done.9.refs_0_ = f32[5,32,128]{2,1,0:T(8,128)S(1)} collective-permute-done((f32[5,32,128]{2,1,0:T(8,128)S(1)}, f32[5,32,128]{2,1,0:T(8,128)S(1)}, u32[]{:S(2)}, u32[]{:S(2)}) %collective-permute-start.9) | collective-permute-done | bytes 81952 | tf_op jit(solution)/shard_map/ppermute | solution.py:447
  50.8 3.6 %all-to-all-start.1 = ((f32[8,32,384]{2,1,0:T(8,128)}), f32[8,32,384]{2,1,0:T(8,128)S(1)}, u32[]{:S(2)}, u32[]{:S(2)}) async-start(f32[8,32,384]{2,1,0:T(8,128)} %shard_map.57), calls=%async_computation.1 | async-start | bytes 786432 | tf_op jit(solution)/shard_map/all_to_all | solution.py:464
  54.4 4.5 %shard_map.58 = (f32[3,64,512]{2,1,0:T(8,128)S(1)}, f32[3,64,512]{2,1,0:T(8,128)S(1)}) custom-call(s32[14,128]{1,0:T(8,128)S(1)} %copy-done.1, f32[3,896,512]{2,1,0:T(8,128)} %refs_11_.1, f32[3,896,512]{2,1,0:T(8,128)} %refs_11_.1, f32[3,896,512]{2,1,0:T(8,128)} %refs_11_.1), custom_call_target="tpu_custom_call" | custom-call | flops 3000000000 | bytes 5505024 | tf_op jit(solution)/shard_map/pallas_call | solution.py:233
  58.9 2.4 %all-to-all-done.1 = f32[8,32,384]{2,1,0:T(8,128)S(1)} async-done(((f32[8,32,384]{2,1,0:T(8,128)}), f32[8,32,384]{2,1,0:T(8,128)S(1)}, u32[]{:S(2)}, u32[]{:S(2)}) %all-to-all-start.1) | async-done | bytes 393248 | tf_op jit(solution)/shard_map/all_to_all | solution.py:464
  61.9 5.4 %collective-permute-done.13.refs_1_ = f32[2,32,512]{2,1,0:T(8,128)S(1)} collective-permute-done((f32[2,32,512]{2,1,0:T(8,128)S(1)}, f32[2,32,512]{2,1,0:T(8,128)S(1)}, u32[]{:S(2)}, u32[]{:S(2)}) %collective-permute-start.13) | collective-permute-done | bytes 131104 | tf_op jit(solution)/shard_map/ppermute | solution.py:447
  69.4 8.5 %shard_map.60 = (f32[128,128]{1,0:T(8,128)S(1)}, f32[128,128]{1,0:T(8,128)S(1)}, f32[128,512]{1,0:T(8,128)S(1)}, f32[128,128]{1,0:T(8,128)S(1)}, f32[896,128]{1,...) custom-call(f32[256,384]{1,0:T(8,128)S(1)} %bitcast.15, ...), custom_call_target="tpu_custom_call" | custom-call | flops 8000000000 | bytes 4000000 | tf_op jit(solution)/shard_map/pallas_call | solution.py:424
  81.5 2.6 %shard_map.62 = (f32[128,128]{1,0:T(8,128)S(1)}, f32[128,128]{1,0:T(8,128)S(1)}) custom-call(f32[128,512]{1,0:T(8,128)S(1)} %get-tuple-element.118.skel_ref.skel1_ref.refs_8_), custom_call_target="tpu_custom_call" | custom-call | flops 100000000 | bytes 100000 | tf_op jit(solution)/shard_map/pallas_call | solution.py:164
  84.1 2.0 %shard_map.63.refs_2_.refs_4_.inverse_1 = f32[128,128]{1,0:T(8,128)S(1)} custom-call(f32[128,128]{1,0:T(8,128)S(1)} %get-tuple-element.119.a_ref, f32[128,128]{1,0:T(8,128)S(1)} %get-tuple-element.120.scales_ref), custom_call_target="tpu_custom_call" | custom-call | flops 100000000 | bytes 100000 | tf_op jit(solution)/shard_map/pallas_call | solution.py:171
  91.4 2.5 %collective-permute-done.20.refs_1_ = f32[1,128,128]{2,1,0:T(8,128)S(1)} collective-permute-done((f32[1,128,128]{2,1,0:T(8,128)S(1)}, f32[1,128,128]{2,1,0:T(8,128)S(1)}, u32[]{:S(2)}, u32[]{:S(2)}) %collective-permute-start.20) | collective-permute-done | bytes 65568 | tf_op jit(solution)/shard_map/ppermute | solution.py:447
  95.6 3.4 %collective-permute-done.22.refs_1_ = f32[128,256]{1,0:T(8,128)S(1)} collective-permute-done((f32[128,256]{1,0:T(8,128)S(1)}, f32[128,256]{1,0:T(8,128)S(1)}, u32[]{:S(2)}, u32[]{:S(2)}) %collective-permute-start.22) | collective-permute-done | bytes 131104 | tf_op jit(solution)/shard_map/ppermute | solution.py:447
  100.3 8.5 %shard_map.67 = (f32[128,128]{1,0:T(8,128)S(1)}, f32[128,512]{1,0:T(8,128)S(1)}, f32[896,128]{1,0:T(8,128)S(1)}, f32[256,128]{1,0:T(8,128)S(1)}, f32[256,128]{1,0:T(8,128)S(1)}) custom-call(f32[128,256]{1,0:T(8,128)S(1)} %bitcast.24, f32[128,256]{1,0:T(8,128)S(1)} %collective-permute-done.22.refs_1_, f32[128,256]{1,0:T(8,128)S(1)} %collective-permute-done.23.refs_2_, ...), custom_call_target="tpu_custom_call" | custom-call | flops 8000000000 | bytes 4000000 | tf_op jit(solution)/shard_map/pallas_call | solution.py:424
  111.4 2.6 %shard_map.68 = (f32[128,128]{1,0:T(8,128)S(1)}, f32[128,128]{1,0:T(8,128)S(1)}) custom-call(f32[128,512]{1,0:T(8,128)S(1)} %get-tuple-element.138.skel_ref), custom_call_target="tpu_custom_call" | custom-call | flops 100000000 | bytes 100000 | tf_op jit(solution)/shard_map/pallas_call | solution.py:164
  117.5 3.2 %shard_map.71 = f32[3,896,128]{2,1,0:T(8,128)} custom-call(f32[896,128]{1,0:T(8,128)S(1)} %get-tuple-element.109.p0_hbm.refs_9_, f32[896,128]{1,0:T(8,128)S(1)} %get-tuple-element.133.refs_10_.p1_hbm, f32[896,128]{1,0:T(8,128)S(1)} %get-tuple-element.143.p2_hbm, f32[128,128]{1,0:T(8,128)S(1)} %shard_map.55.refs_1_.ours_ref.inverse_0, ...), custom_call_target="tpu_custom_call" | custom-call | flops 4000000000 | bytes 4000000 | tf_op jit(solution)/shard_map/pallas_call | solution.py:424
  122.8 5.3 %shard_map.72 = f32[3,1,128,128]{3,2,1,0:T(8,128)} custom-call(f32[256,128]{1,0:T(8,128)S(1)} %collective-permute-done.29.mine_ref, f32[256,128]{1,0:T(8,128)S(1)} %collective-permute-done.30.other_ref, f32[128,512]{1,0:T(8,128)S(1)} %get-tuple-element.138.skel_ref, f32[128,128]{1,0:T(8,128)S(1)} %get-tuple-element.146.c0_ref, ...), custom_call_target="tpu_custom_call" | custom-call | flops 5000000000 | bytes 4000000 | tf_op jit(solution)/shard_map/pallas_call | solution.py:424
  (81 shorter events, 39.2 us)
Async XLA Ops:
  5.2 6.7 %collective-permute-start.1 = (f32[64,512]{1,0:T(8,128)S(1)}, f32[64,512]{1,0:T(8,128)S(1)}, u32[]{:S(2)}, u32[]{:S(2)}) collective-permute-start(f32[64,512]{1,0:T(8,128)S(1)} %bitcast_add_fusion), channel_id=1, source_target_pairs={{0,1},{1,0},{2,3},{3,2},{4,5},{5,4},{6,7},{7,6},{8,9},{9,8},{10,11... | collective-permute-start | bytes 393224 | tf_op jit(solution)/shard_map/ppermute | solution.py:447
  12.0 7.1 %collective-permute-start.2 = (f32[64,512]{1,0:T(8,128)S(1)}, f32[64,512]{1,0:T(8,128)S(1)}, u32[]{:S(2)}, u32[]{:S(2)}) collective-permute-start(f32[64,512]{1,0:T(8,128)S(1)} %add.40), channel_id=1, source_target_pairs={{0,4},{4,0},{1,5},{5,1},{2,6},{6,2},{3,7},{7,3},{8,12},{12,8},{9,1... | collective-permute-start | bytes 393224 | tf_op jit(solution)/shard_map/ppermute | solution.py:447
  13.8 5.8 %collective-permute-start.3 = (f32[64,512]{1,0:T(8,128)S(1)}, f32[64,512]{1,0:T(8,128)S(1)}, u32[]{:S(2)}, u32[]{:S(2)}) collective-permute-start(f32[64,512]{1,0:T(8,128)S(1)} %add.40), channel_id=1, source_target_pairs={{0,8},{8,0},{1,9},{9,1},{2,10},{10,2},{3,11},{11,3},{4,12},{12,4},... | collective-permute-start | bytes 393224 | tf_op jit(solution)/shard_map/ppermute | solution.py:447
  15.4 5.9 %collective-permute-start.4 = (f32[64,512]{1,0:T(8,128)S(1)}, f32[64,512]{1,0:T(8,128)S(1)}, u32[]{:S(2)}, u32[]{:S(2)}) collective-permute-start(f32[64,512]{1,0:T(8,128)S(1)} %add.40), channel_id=1, source_target_pairs={{0,12},{4,8},{8,4},{12,0},{1,13},{5,9},{9,5},{13,1},{2,14},{6,10},... | collective-permute-start | bytes 393224 | tf_op jit(solution)/shard_map/ppermute | solution.py:451
  19.0 2.4 %collective-permute-start.6 = (f32[2,64,512]{2,1,0:T(8,128)S(1)}, f32[2,64,512]{2,1,0:T(8,128)S(1)}, u32[]{:S(2)}, u32[]{:S(2)}) collective-permute-start(f32[2,64,512]{2,1,0:T(8,128)S(1)} %get-tuple-element.80), channel_id=1, source_target_pairs={{0,2},{2,0},{1,3},{3,1},{4,6},{6,4},{5,7},{7,5},{8,10},{10,8},{9,1... | collective-permute-start | bytes 786440 | tf_op jit(solution)/shard_map/ppermute | solution.py:447
  22.7 6.4 %collective-permute-start.7 = (f32[2,32,512]{2,1,0:T(8,128)S(1)}, f32[2,32,512]{2,1,0:T(8,128)S(1)}, u32[]{:S(2)}, u32[]{:S(2)}) collective-permute-start(f32[2,32,512]{2,1,0:T(8,128)S(1)} %get-tuple-element.86), channel_id=1, source_target_pairs={{0,1},{1,0},{2,3},{3,2},{4,5},{5,4},{6,7},{7,6},{8,9},{9,8},{10,11... | collective-permute-start | bytes 393224 | tf_op jit(solution)/shard_map/ppermute | solution.py:447
  31.7 11.9 %all-to-all-start = ((f32[8,32,384]{2,1,0:T(8,128)}), f32[8,32,384]{2,1,0:T(8,128)S(1)}, u32[]{:S(2)}, u32[]{:S(2)}) async-start(f32[8,32,384]{2,1,0:T(8,128)} %bitcast.2), calls=%async_computation | async-start | bytes 786432 | tf_op jit(solution)/shard_map/all_to_all | solution.py:464
  35.3 11.1 %collective-permute-start.10 = (f32[2,32,512]{2,1,0:T(8,128)S(1)}, f32[2,32,512]{2,1,0:T(8,128)S(1)}, u32[]{:S(2)}, u32[]{:S(2)}) collective-permute-start(f32[2,32,512]{2,1,0:T(8,128)S(1)} %add.45), channel_id=1, source_target_pairs={{0,4},{4,0},{1,5},{5,1},{2,6},{6,2},{3,7},{7,3},{8,12},{12,8},{9,1... | collective-permute-start | bytes 393224 | tf_op jit(solution)/shard_map/ppermute | solution.py:447
  43.8 6.3 %collective-permute-start.9 = (f32[5,32,128]{2,1,0:T(8,128)S(1)}, f32[5,32,128]{2,1,0:T(8,128)S(1)}, u32[]{:S(2)}, u32[]{:S(2)}) collective-permute-start(f32[5,32,128]{2,1,0:T(8,128)S(1)} %shard_map.56), channel_id=1, source_target_pairs={{0,16},{16,0},{1,17},{17,1},{2,18},{18,2},{3,19},{19,3},{4,20},{20... | collective-permute-start | bytes 245768 | tf_op jit(solution)/shard_map/ppermute | solution.py:447
  50.8 10.5 %all-to-all-start.1 = ((f32[8,32,384]{2,1,0:T(8,128)}), f32[8,32,384]{2,1,0:T(8,128)S(1)}, u32[]{:S(2)}, u32[]{:S(2)}) async-start(f32[8,32,384]{2,1,0:T(8,128)} %shard_map.57), calls=%async_computation.1 | async-start | bytes 786432 | tf_op jit(solution)/shard_map/all_to_all | solution.py:464
  61.3 7.6 %collective-permute-start.12 = (f32[3,64,512]{2,1,0:T(8,128)S(1)}, f32[3,64,512]{2,1,0:T(8,128)S(1)}, u32[]{:S(2)}, u32[]{:S(2)}) collective-permute-start(f32[3,64,512]{2,1,0:T(8,128)S(1)} %get-tuple-element.103), channel_id=1, source_target_pairs={{0,2},{2,0},{1,3},{3,1},{4,6},{6,4},{5,7},{7,5},{8,10},{10,8},{9,1... | collective-permute-start | bytes 1179656 | tf_op jit(solution)/shard_map/ppermute | solution.py:447
  61.3 5.9 %collective-permute-start.13 = (f32[2,32,512]{2,1,0:T(8,128)S(1)}, f32[2,32,512]{2,1,0:T(8,128)S(1)}, u32[]{:S(2)}, u32[]{:S(2)}) collective-permute-start(f32[2,32,512]{2,1,0:T(8,128)S(1)} %add.46.refs_0_), channel_id=1, source_target_pairs={{0,1},{1,0},{2,3},{3,2},{4,5},{5,4},{6,7},{7,6},{8,9},{9,8},{10,11... | collective-permute-start | bytes 393224 | tf_op jit(solution)/shard_map/ppermute | solution.py:447
  61.5 6.2 %collective-permute-start.14 = (f32[2,32,512]{2,1,0:T(8,128)S(1)}, f32[2,32,512]{2,1,0:T(8,128)S(1)}, u32[]{:S(2)}, u32[]{:S(2)}) collective-permute-start(f32[2,32,512]{2,1,0:T(8,128)S(1)} %add.46.refs_0_), channel_id=1, source_target_pairs={{0,2},{2,0},{1,3},{3,1},{4,6},{6,4},{5,7},{7,5},{8,10},{10,8},{9,1... | collective-permute-start | bytes 393224 | tf_op jit(solution)/shard_map/ppermute | solution.py:447
  69.2 8.8 %collective-permute-start.16 = (f32[2,64,512]{2,1,0:T(8,128)S(1)}, f32[2,64,512]{2,1,0:T(8,128)S(1)}, u32[]{:S(2)}, u32[]{:S(2)}) collective-permute-start(f32[2,64,512]{2,1,0:T(8,128)S(1)} %slice_add_fusion), channel_id=1, source_target_pairs={{0,1},{1,0},{2,3},{3,2},{4,5},{5,4},{6,7},{7,6},{8,9},{9,8},{10,11... | collective-permute-start | bytes 786440 | tf_op jit(solution)/shard_map/ppermute | solution.py:447
  79.7 6.4 %collective-permute-start.18 = (f32[128,256]{1,0:T(8,128)S(1)}, f32[128,256]{1,0:T(8,128)S(1)}, u32[]{:S(2)}, u32[]{:S(2)}) collective-permute-start(f32[128,256]{1,0:T(8,128)S(1)} %bitcast.25), channel_id=1, source_target_pairs={{0,1},{1,0},{2,3},{3,2},{4,5},{5,4},{6,7},{7,6},{8,9},{9,8},{10,11... | collective-permute-start | bytes 393224 | tf_op jit(solution)/shard_map/ppermute | solution.py:447
  86.1 5.3 %collective-permute-start.21 = (f32[1,64,512]{2,1,0:T(8,128)S(1)}, f32[1,64,512]{2,1,0:T(8,128)S(1)}, u32[]{:S(2)}, u32[]{:S(2)}) collective-permute-start(f32[1,64,512]{2,1,0:T(8,128)S(1)} %slice_add_fusion.1), channel_id=1, source_target_pairs={{0,1},{1,0},{2,3},{3,2},{4,5},{5,4},{6,7},{7,6},{8,9},{9,8},{10,11... | collective-permute-start | bytes 393224 | tf_op jit(solution)/shard_map/ppermute | solution.py:447
  87.2 6.7 %collective-permute-start.19 = (f32[2,128,128]{2,1,0:T(8,128)S(1)}, f32[2,128,128]{2,1,0:T(8,128)S(1)}, u32[]{:S(2)}, u32[]{:S(2)}) collective-permute-start(f32[2,128,128]{2,1,0:T(8,128)S(1)} %shard_map.64), channel_id=1, source_target_pairs={{0,12},{4,8},{8,4},{12,0},{1,13},{5,9},{9,5},{13,1},{2,14},{6,10},... | collective-permute-start | bytes 393224 | tf_op jit(solution)/shard_map/ppermute | solution.py:451
  88.3 10.6 %collective-permute-start.25 = (f32[2,64,512]{2,1,0:T(8,128)S(1)}, f32[2,64,512]{2,1,0:T(8,128)S(1)}, u32[]{:S(2)}, u32[]{:S(2)}) collective-permute-start(f32[2,64,512]{2,1,0:T(8,128)S(1)} %add.48.rows_mine), channel_id=1, source_target_pairs={{0,2},{2,0},{1,3},{3,1},{4,6},{6,4},{5,7},{7,5},{8,10},{10,8},{9,1... | collective-permute-start | bytes 786440 | tf_op jit(solution)/shard_map/ppermute | solution.py:447
  88.3 5.5 %collective-permute-start.20 = (f32[1,128,128]{2,1,0:T(8,128)S(1)}, f32[1,128,128]{2,1,0:T(8,128)S(1)}, u32[]{:S(2)}, u32[]{:S(2)}) collective-permute-start(f32[1,128,128]{2,1,0:T(8,128)S(1)} %slice.22), channel_id=1, source_target_pairs={{0,8},{8,0},{1,9},{9,1},{2,10},{10,2},{3,11},{11,3},{4,12},{12,4},... | collective-permute-start | bytes 196616 | tf_op jit(solution)/shard_map/ppermute | solution.py:447
  93.9 5.0 %collective-permute-start.22 = (f32[128,256]{1,0:T(8,128)S(1)}, f32[128,256]{1,0:T(8,128)S(1)}, u32[]{:S(2)}, u32[]{:S(2)}) collective-permute-start(f32[128,256]{1,0:T(8,128)S(1)} %bitcast.22), channel_id=1, source_target_pairs={{0,1},{1,0},{2,3},{3,2},{4,5},{5,4},{6,7},{7,6},{8,9},{9,8},{10,11... | collective-permute-start | bytes 393224 | tf_op jit(solution)/shard_map/ppermute | solution.py:447
  95.1 3.9 %collective-permute-start.26 = (f32[1,64,512]{2,1,0:T(8,128)S(1)}, f32[1,64,512]{2,1,0:T(8,128)S(1)}, u32[]{:S(2)}, u32[]{:S(2)}) collective-permute-start(f32[1,64,512]{2,1,0:T(8,128)S(1)} %add.50.last_mine), channel_id=1, source_target_pairs={{0,2},{2,0},{1,3},{3,1},{4,6},{6,4},{5,7},{7,5},{8,10},{10,8},{9,1... | collective-permute-start | bytes 393224 | tf_op jit(solution)/shard_map/ppermute | solution.py:447
  95.1 4.7 %collective-permute-start.23 = (f32[128,256]{1,0:T(8,128)S(1)}, f32[128,256]{1,0:T(8,128)S(1)}, u32[]{:S(2)}, u32[]{:S(2)}) collective-permute-start(f32[128,256]{1,0:T(8,128)S(1)} %bitcast.23), channel_id=1, source_target_pairs={{0,2},{2,0},{1,3},{3,1},{4,6},{6,4},{5,7},{7,5},{8,10},{10,8},{9,1... | collective-permute-start | bytes 393224 | tf_op jit(solution)/shard_map/ppermute | solution.py:447
  110.2 5.7 %collective-permute-start.28 = (f32[256,128]{1,0:T(8,128)S(1)}, f32[256,128]{1,0:T(8,128)S(1)}, u32[]{:S(2)}, u32[]{:S(2)}) collective-permute-start(f32[256,128]{1,0:T(8,128)S(1)} %add.51), channel_id=1, source_target_pairs={{0,1},{1,0},{2,3},{3,2},{4,5},{5,4},{6,7},{7,6},{8,9},{9,8},{10,11... | collective-permute-start | bytes 393224 | tf_op jit(solution)/shard_map/ppermute | solution.py:447
  116.1 5.3 %collective-permute-start.29 = (f32[256,128]{1,0:T(8,128)S(1)}, f32[256,128]{1,0:T(8,128)S(1)}, u32[]{:S(2)}, u32[]{:S(2)}) collective-permute-start(f32[256,128]{1,0:T(8,128)S(1)} %bitcast.20), channel_id=1, source_target_pairs={{0,4},{4,0},{1,5},{5,1},{2,6},{6,2},{3,7},{7,3},{8,12},{12,8},{9,1... | collective-permute-start | bytes 393224 | tf_op jit(solution)/shard_map/ppermute | solution.py:447
  (11 other events, 46.1 us)

commit v4 on v3

--- a/solution.py
+++ b/solution.py
@@ -600,16 +600,16 @@
     rest_kept, rest_sent = pick(lists, sample, ((2, 0), (2, 1), (2, 2)), sizes)
     mine = exchange(fan_out([sums], [[[(0, at)] for at in (0, 2 - one, 4 - two)] for one, two in places]), chips[0])
     mine = mine.reshape(samples // 2, levels * skel)
-    mine, rest_kept, rest_sent = held(mine, rest_kept, rest_sent)
+    row_parts = (rows_one, swap(rows_one, "blk")) if pairs else (rows_one,)
+    mine, rest_kept, rest_sent, *row_parts = held(mine, rest_kept, rest_sent, *row_parts)
     other = swap(mine, "core")
     rest_sent = swap(rest_sent, "core")
     rest, last = rest_kept[:2] + rest_sent[:2], rest_kept[2:] + rest_sent[2:]
     mine, other, rest = held(mine, other, rest)
     rest = total_over(rest, ("mid", "blk"))
 
-    row_parts = (rows_one, swap(rows_one, "blk")) if pairs else (rows_one,)
-    row_parts += tuple(swap(part, "core") for part in row_parts)
-    low, rows_one = small_call(second_rows_kernel, [square, wide], row_parts + (skeleton_0,))
+    row_parts += [swap(part, "core") for part in row_parts]
+    low, rows_one = small_call(second_rows_kernel, [square, wide], (*row_parts, skeleton_0))
     coupling_0, back, skeleton_1, tilt, projected_1, kept, sent = level_call(
         second_kernel,
         [VMEM] * 6 + [ANY] * 3,

time: 129 us -> 125 us (0.969)
  waiting for transfers between devices: 37.1 us -> 31.1 us
  starting transfers between devices: 31.8 us -> 33.6 us
    ppermute x29, waiting for transfers between devices: 31.4 us -> 27.8 us  [swap(): return lax.ppermute(block, axis, [(0, 1), (1, 0)])]
    all_to_all x2, waiting for transfers between devices: 4.03 us -> 1.63 us  [exchange(): return lax.all_to_all(pieces, axes, 0, 0, tiled=True)]
    ppermute x2, starting transfers between devices: 1.26 us -> 2.56 us  [cross_swap(): return lax.ppermute(block, ('n1', 'n2'), [(0, 3), (1, 2), (2, 1), (3, 0)])]
  transfers between devices with their start and end apart: 33 -> 33, of which waited for: 20 -> 20; matrix products, arithmetic and copies ran while one was open for 0% -> 0% of each run, Pallas kernels for 31% -> 32%
where the time goes in v4:
time: 125 us; the launch traced here: 124 us
  Pallas kernels  56.6 us (45%)
  starting transfers between devices  33.6 us (27%)
  waiting for transfers between devices  31.1 us (25%)
    pallas_call x5, Pallas kernels, level_call(): pl.pallas_call(kernel, out_shape=outs, in_specs=specs, out_specs=[ANY if...  30.1 us
    ppermute x29, waiting for transfers between devices, swap(): return lax.ppermute(block, axis, [(0, 1), (1, 0)])  27.8 us
    ppermute x29, starting transfers between devices, swap(): return lax.ppermute(block, axis, [(0, 1), (1, 0)])  23.8 us
    pallas_call x3, Pallas kernels, pick(): pl.pallas_call(functools.partial(pick_kernel, wanted, sizes), out_shape=[...  10.3 us
    pallas_call x3, Pallas kernels, invert_first(): pl.pallas_call(first_half_kernel, out_shape=[square] * 2, in_specs=[VMEM]...  7.74 us
    all_to_all x2, starting transfers between devices, exchange(): return lax.all_to_all(pieces, axes, 0, 0, tiled=True)  7.21 us
    pallas_call x3, Pallas kernels, invert_second(): pl.pallas_call(second_half_kernel, out_shape=arr(*state.shape), in_specs=...  5.88 us
    ppermute x2, starting transfers between devices, cross_swap(): return lax.ppermute(block, ('n1', 'n2'), [(0, 3), (1, 2), (2, 1), (3, 0)])  2.56 us
  transfers between devices with their start and end apart: 33, of which 20 were waited for; matrix products, arithmetic and copies ran while one was open for 0% of the time, Pallas kernels for 32%

profile of v4, /device:TPU:0, one launch (start us, length us, event | category | flops | bytes accessed | tf_op | source)
XLA Modules:
  0.0 123.9 jit_solution(15486528042623618674)
XLA Ops:
  1.3 2.4 %shard_map.50 = (f32[1,64,512]{2,1,0:T(8,128)S(1)}, f32[1,64,512]{2,1,0:T(8,128)S(1)}) custom-call(s32[14,128]{1,0:T(8,128)S(1)} %copy-done, f32[3,896,512]{2,1,0:T(8,128)} %refs_11_.1), custom_call_target="tpu_custom_call" | custom-call | flops 1000000000 | bytes 1835008 | tf_op jit(solution)/shard_map/pallas_call | solution.py:233
  5.2 2.9 %collective-permute-start.1 = (f32[64,512]{1,0:T(8,128)S(1)}, f32[64,512]{1,0:T(8,128)S(1)}, u32[]{:S(2)}, u32[]{:S(2)}) collective-permute-start(f32[64,512]{1,0:T(8,128)S(1)} %bitcast_add_fusion), channel_id=1, source_target_pairs={{0,1},{1,0},{2,3},{3,2},{4,5},{5,4},{6,7},{7,6},{8,9},{9,8},{10,11... | collective-permute-start | bytes 393224 | tf_op jit(solution)/shard_map/ppermute | solution.py:447
  8.2 3.8 %collective-permute-done.1 = f32[64,512]{1,0:T(8,128)S(1)} collective-permute-done((f32[64,512]{1,0:T(8,128)S(1)}, f32[64,512]{1,0:T(8,128)S(1)}, u32[]{:S(2)}, u32[]{:S(2)}) %collective-permute-start.1) | collective-permute-done | bytes 131104 | tf_op jit(solution)/shard_map/ppermute | solution.py:447
  15.5 3.4 %shard_map.51 = (f32[2,64,512]{2,1,0:T(8,128)S(1)}, f32[2,64,512]{2,1,0:T(8,128)S(1)}) custom-call(s32[14,128]{1,0:T(8,128)S(1)} %copy-done, f32[3,896,512]{2,1,0:T(8,128)} %refs_11_.1, f32[3,896,512]{2,1,0:T(8,128)} %refs_11_.1), custom_call_target="tpu_custom_call" | custom-call | flops 2000000000 | bytes 3670016 | tf_op jit(solution)/shard_map/pallas_call | solution.py:233
  24.5 4.6 %shard_map.53 = (f32[128,512]{1,0:T(8,128)S(1)}, f32[896,128]{1,0:T(8,128)S(1)}, f32[256,384]{1,0:T(8,128)S(1)}, f32[256,384]{1,0:T(8,128)S(1)}) custom-call(f32[64,512]{1,0:T(8,128)S(1)} %add_add_fusion.mine_ref, f32[64,512]{1,0:T(8,128)S(1)} %collective-permute-done.5.other_ref, f32[3,896,512]{2,1,0:T(8,128)} %refs_11_.1, f32[3,896,512]{2,1,0:T(8,128)} %refs_12_.1), custom_call_target="tpu_custom_call" | custom-call | flops 3000000000 | bytes 4000000 | tf_op jit(solution)/shard_map/pallas_call | solution.py:424
  31.7 3.6 %all-to-all-start = ((f32[8,32,384]{2,1,0:T(8,128)}), f32[8,32,384]{2,1,0:T(8,128)S(1)}, u32[]{:S(2)}, u32[]{:S(2)}) async-start(f32[8,32,384]{2,1,0:T(8,128)} %bitcast.2), calls=%async_computation | async-start | bytes 786432 | tf_op jit(solution)/shard_map/all_to_all | solution.py:464
  35.3 2.1 %collective-permute-start.10 = (f32[2,32,512]{2,1,0:T(8,128)S(1)}, f32[2,32,512]{2,1,0:T(8,128)S(1)}, u32[]{:S(2)}, u32[]{:S(2)}) collective-permute-start(f32[2,32,512]{2,1,0:T(8,128)S(1)} %add.45), channel_id=1, source_target_pairs={{0,4},{4,0},{1,5},{5,1},{2,6},{6,2},{3,7},{7,3},{8,12},{12,8},{9,1... | collective-permute-start | bytes 393224 | tf_op jit(solution)/shard_map/ppermute | solution.py:447
  37.4 2.6 %shard_map.54 = (f32[128,128]{1,0:T(8,128)S(1)}, f32[128,128]{1,0:T(8,128)S(1)}) custom-call(f32[128,512]{1,0:T(8,128)S(1)} %get-tuple-element.92.skel_ref.refs_4_.skel0_ref), custom_call_target="tpu_custom_call" | custom-call | flops 100000000 | bytes 100000 | tf_op jit(solution)/shard_map/pallas_call | solution.py:164
  40.0 2.0 %shard_map.55.refs_1_.ours_ref.inverse_0 = f32[128,128]{1,0:T(8,128)S(1)} custom-call(f32[128,128]{1,0:T(8,128)S(1)} %get-tuple-element.93.a_ref, f32[128,128]{1,0:T(8,128)S(1)} %get-tuple-element.94.scales_ref), custom_call_target="tpu_custom_call" | custom-call | flops 100000000 | bytes 100000 | tf_op jit(solution)/shard_map/pallas_call | solution.py:171
  43.8 2.6 %collective-permute-start.9 = (f32[5,32,128]{2,1,0:T(8,128)S(1)}, f32[5,32,128]{2,1,0:T(8,128)S(1)}, u32[]{:S(2)}, u32[]{:S(2)}) collective-permute-start(f32[5,32,128]{2,1,0:T(8,128)S(1)} %shard_map.56), channel_id=1, source_target_pairs={{0,16},{16,0},{1,17},{17,1},{2,18},{18,2},{3,19},{19,3},{4,20},{20... | collective-permute-start | bytes 245768 | tf_op jit(solution)/shard_map/ppermute | solution.py:447
  46.4 3.6 %collective-permute-done.9.refs_0_ = f32[5,32,128]{2,1,0:T(8,128)S(1)} collective-permute-done((f32[5,32,128]{2,1,0:T(8,128)S(1)}, f32[5,32,128]{2,1,0:T(8,128)S(1)}, u32[]{:S(2)}, u32[]{:S(2)}) %collective-permute-start.9) | collective-permute-done | bytes 81952 | tf_op jit(solution)/shard_map/ppermute | solution.py:447
  50.8 3.6 %all-to-all-start.1 = ((f32[8,32,384]{2,1,0:T(8,128)}), f32[8,32,384]{2,1,0:T(8,128)S(1)}, u32[]{:S(2)}, u32[]{:S(2)}) async-start(f32[8,32,384]{2,1,0:T(8,128)} %shard_map.57), calls=%async_computation.1 | async-start | bytes 786432 | tf_op jit(solution)/shard_map/all_to_all | solution.py:464
  56.2 4.5 %shard_map.58 = (f32[3,64,512]{2,1,0:T(8,128)S(1)}, f32[3,64,512]{2,1,0:T(8,128)S(1)}) custom-call(s32[14,128]{1,0:T(8,128)S(1)} %copy-done.1, f32[3,896,512]{2,1,0:T(8,128)} %refs_11_.1, f32[3,896,512]{2,1,0:T(8,128)} %refs_11_.1, f32[3,896,512]{2,1,0:T(8,128)} %refs_11_.1), custom_call_target="tpu_custom_call" | custom-call | flops 3000000000 | bytes 5505024 | tf_op jit(solution)/shard_map/pallas_call | solution.py:233
  64.5 8.5 %shard_map.60 = (f32[128,128]{1,0:T(8,128)S(1)}, f32[128,128]{1,0:T(8,128)S(1)}, f32[128,512]{1,0:T(8,128)S(1)}, f32[128,128]{1,0:T(8,128)S(1)}, f32[896,128]{1,...) custom-call(f32[256,384]{1,0:T(8,128)S(1)} %bitcast.15, ...), custom_call_target="tpu_custom_call" | custom-call | flops 8000000000 | bytes 4000000 | tf_op jit(solution)/shard_map/pallas_call | solution.py:424
  76.4 2.6 %shard_map.62 = (f32[128,128]{1,0:T(8,128)S(1)}, f32[128,128]{1,0:T(8,128)S(1)}) custom-call(f32[128,512]{1,0:T(8,128)S(1)} %get-tuple-element.122.skel_ref.skel1_ref.refs_8_), custom_call_target="tpu_custom_call" | custom-call | flops 100000000 | bytes 100000 | tf_op jit(solution)/shard_map/pallas_call | solution.py:164
  79.0 2.0 %shard_map.63.refs_2_.refs_4_.inverse_1 = f32[128,128]{1,0:T(8,128)S(1)} custom-call(f32[128,128]{1,0:T(8,128)S(1)} %get-tuple-element.123.a_ref, f32[128,128]{1,0:T(8,128)S(1)} %get-tuple-element.124.scales_ref), custom_call_target="tpu_custom_call" | custom-call | flops 100000000 | bytes 100000 | tf_op jit(solution)/shard_map/pallas_call | solution.py:171
  82.2 2.4 %collective-permute-start.19 = (f32[2,128,128]{2,1,0:T(8,128)S(1)}, f32[2,128,128]{2,1,0:T(8,128)S(1)}, u32[]{:S(2)}, u32[]{:S(2)}) collective-permute-start(f32[2,128,128]{2,1,0:T(8,128)S(1)} %shard_map.64), channel_id=1, source_target_pairs={{0,12},{4,8},{8,4},{12,0},{1,13},{5,9},{9,5},{13,1},{2,14},{6,10},... | collective-permute-start | bytes 393224 | tf_op jit(solution)/shard_map/ppermute | solution.py:451
  86.4 3.2 %collective-permute-done.20.refs_1_ = f32[1,128,128]{2,1,0:T(8,128)S(1)} collective-permute-done((f32[1,128,128]{2,1,0:T(8,128)S(1)}, f32[1,128,128]{2,1,0:T(8,128)S(1)}, u32[]{:S(2)}, u32[]{:S(2)}) %collective-permute-start.20) | collective-permute-done | bytes 65568 | tf_op jit(solution)/shard_map/ppermute | solution.py:447
  91.3 3.4 %collective-permute-done.22.refs_1_ = f32[128,256]{1,0:T(8,128)S(1)} collective-permute-done((f32[128,256]{1,0:T(8,128)S(1)}, f32[128,256]{1,0:T(8,128)S(1)}, u32[]{:S(2)}, u32[]{:S(2)}) %collective-permute-start.22) | collective-permute-done | bytes 131104 | tf_op jit(solution)/shard_map/ppermute | solution.py:447
  96.0 8.5 %shard_map.67 = (f32[128,128]{1,0:T(8,128)S(1)}, f32[128,512]{1,0:T(8,128)S(1)}, f32[896,128]{1,0:T(8,128)S(1)}, f32[256,128]{1,0:T(8,128)S(1)}, f32[256,128]{1,0:T(8,128)S(1)}) custom-call(f32[128,256]{1,0:T(8,128)S(1)} %bitcast.24, f32[128,256]{1,0:T(8,128)S(1)} %collective-permute-done.22.refs_1_, f32[128,256]{1,0:T(8,128)S(1)} %collective-permute-done.23.refs_2_, ...), custom_call_target="tpu_custom_call" | custom-call | flops 8000000000 | bytes 4000000 | tf_op jit(solution)/shard_map/pallas_call | solution.py:424
  107.2 2.6 %shard_map.68 = (f32[128,128]{1,0:T(8,128)S(1)}, f32[128,128]{1,0:T(8,128)S(1)}) custom-call(f32[128,512]{1,0:T(8,128)S(1)} %get-tuple-element.142.skel_ref), custom_call_target="tpu_custom_call" | custom-call | flops 100000000 | bytes 100000 | tf_op jit(solution)/shard_map/pallas_call | solution.py:164
  109.7 2.0 %shard_map.69.refs_2_.inverse_2 = f32[128,128]{1,0:T(8,128)S(1)} custom-call(f32[128,128]{1,0:T(8,128)S(1)} %get-tuple-element.143.a_ref, f32[128,128]{1,0:T(8,128)S(1)} %get-tuple-element.144.scales_ref), custom_call_target="tpu_custom_call" | custom-call | flops 100000000 | bytes 100000 | tf_op jit(solution)/shard_map/pallas_call | solution.py:171
  112.5 3.2 %shard_map.71 = f32[3,896,128]{2,1,0:T(8,128)} custom-call(f32[896,128]{1,0:T(8,128)S(1)} %get-tuple-element.113.p0_hbm.refs_9_, f32[896,128]{1,0:T(8,128)S(1)} %get-tuple-element.137.refs_10_.p1_hbm, f32[896,128]{1,0:T(8,128)S(1)} %get-tuple-element.147.p2_hbm, f32[128,128]{1,0:T(8,128)S(1)} %shard_map.55.refs_1_.ours_ref.inverse_0, ...), custom_call_target="tpu_custom_call" | custom-call | flops 4000000000 | bytes 4000000 | tf_op jit(solution)/shard_map/pallas_call | solution.py:424
  118.6 5.3 %shard_map.72 = f32[3,1,128,128]{3,2,1,0:T(8,128)} custom-call(f32[256,128]{1,0:T(8,128)S(1)} %collective-permute-done.29.mine_ref, f32[256,128]{1,0:T(8,128)S(1)} %collective-permute-done.30.other_ref, f32[128,512]{1,0:T(8,128)S(1)} %get-tuple-element.142.skel_ref, f32[128,128]{1,0:T(8,128)S(1)} %get-tuple-element.150.c0_ref, ...), custom_call_target="tpu_custom_call" | custom-call | flops 5000000000 | bytes 4000000 | tf_op jit(solution)/shard_map/pallas_call | solution.py:424
  (81 shorter events, 37.7 us)
Async XLA Ops:
  5.2 6.7 %collective-permute-start.1 = (f32[64,512]{1,0:T(8,128)S(1)}, f32[64,512]{1,0:T(8,128)S(1)}, u32[]{:S(2)}, u32[]{:S(2)}) collective-permute-start(f32[64,512]{1,0:T(8,128)S(1)} %bitcast_add_fusion), channel_id=1, source_target_pairs={{0,1},{1,0},{2,3},{3,2},{4,5},{5,4},{6,7},{7,6},{8,9},{9,8},{10,11... | collective-permute-start | bytes 393224 | tf_op jit(solution)/shard_map/ppermute | solution.py:447
  12.0 7.1 %collective-permute-start.2 = (f32[64,512]{1,0:T(8,128)S(1)}, f32[64,512]{1,0:T(8,128)S(1)}, u32[]{:S(2)}, u32[]{:S(2)}) collective-permute-start(f32[64,512]{1,0:T(8,128)S(1)} %add.40), channel_id=1, source_target_pairs={{0,4},{4,0},{1,5},{5,1},{2,6},{6,2},{3,7},{7,3},{8,12},{12,8},{9,1... | collective-permute-start | bytes 393224 | tf_op jit(solution)/shard_map/ppermute | solution.py:447
  13.8 5.8 %collective-permute-start.3 = (f32[64,512]{1,0:T(8,128)S(1)}, f32[64,512]{1,0:T(8,128)S(1)}, u32[]{:S(2)}, u32[]{:S(2)}) collective-permute-start(f32[64,512]{1,0:T(8,128)S(1)} %add.40), channel_id=1, source_target_pairs={{0,8},{8,0},{1,9},{9,1},{2,10},{10,2},{3,11},{11,3},{4,12},{12,4},... | collective-permute-start | bytes 393224 | tf_op jit(solution)/shard_map/ppermute | solution.py:447
  15.4 5.9 %collective-permute-start.4 = (f32[64,512]{1,0:T(8,128)S(1)}, f32[64,512]{1,0:T(8,128)S(1)}, u32[]{:S(2)}, u32[]{:S(2)}) collective-permute-start(f32[64,512]{1,0:T(8,128)S(1)} %add.40), channel_id=1, source_target_pairs={{0,12},{4,8},{8,4},{12,0},{1,13},{5,9},{9,5},{13,1},{2,14},{6,10},... | collective-permute-start | bytes 393224 | tf_op jit(solution)/shard_map/ppermute | solution.py:451
  19.0 2.4 %collective-permute-start.6 = (f32[2,64,512]{2,1,0:T(8,128)S(1)}, f32[2,64,512]{2,1,0:T(8,128)S(1)}, u32[]{:S(2)}, u32[]{:S(2)}) collective-permute-start(f32[2,64,512]{2,1,0:T(8,128)S(1)} %get-tuple-element.82), channel_id=1, source_target_pairs={{0,2},{2,0},{1,3},{3,1},{4,6},{6,4},{5,7},{7,5},{8,10},{10,8},{9,1... | collective-permute-start | bytes 786440 | tf_op jit(solution)/shard_map/ppermute | solution.py:447
  22.7 6.4 %collective-permute-start.7 = (f32[2,32,512]{2,1,0:T(8,128)S(1)}, f32[2,32,512]{2,1,0:T(8,128)S(1)}, u32[]{:S(2)}, u32[]{:S(2)}) collective-permute-start(f32[2,32,512]{2,1,0:T(8,128)S(1)} %get-tuple-element.88), channel_id=1, source_target_pairs={{0,1},{1,0},{2,3},{3,2},{4,5},{5,4},{6,7},{7,6},{8,9},{9,8},{10,11... | collective-permute-start | bytes 393224 | tf_op jit(solution)/shard_map/ppermute | solution.py:447
  31.7 11.9 %all-to-all-start = ((f32[8,32,384]{2,1,0:T(8,128)}), f32[8,32,384]{2,1,0:T(8,128)S(1)}, u32[]{:S(2)}, u32[]{:S(2)}) async-start(f32[8,32,384]{2,1,0:T(8,128)} %bitcast.2), calls=%async_computation | async-start | bytes 786432 | tf_op jit(solution)/shard_map/all_to_all | solution.py:464
  35.3 11.1 %collective-permute-start.10 = (f32[2,32,512]{2,1,0:T(8,128)S(1)}, f32[2,32,512]{2,1,0:T(8,128)S(1)}, u32[]{:S(2)}, u32[]{:S(2)}) collective-permute-start(f32[2,32,512]{2,1,0:T(8,128)S(1)} %add.45), channel_id=1, source_target_pairs={{0,4},{4,0},{1,5},{5,1},{2,6},{6,2},{3,7},{7,3},{8,12},{12,8},{9,1... | collective-permute-start | bytes 393224 | tf_op jit(solution)/shard_map/ppermute | solution.py:447
  43.8 6.3 %collective-permute-start.9 = (f32[5,32,128]{2,1,0:T(8,128)S(1)}, f32[5,32,128]{2,1,0:T(8,128)S(1)}, u32[]{:S(2)}, u32[]{:S(2)}) collective-permute-start(f32[5,32,128]{2,1,0:T(8,128)S(1)} %shard_map.56), channel_id=1, source_target_pairs={{0,16},{16,0},{1,17},{17,1},{2,18},{18,2},{3,19},{19,3},{4,20},{20... | collective-permute-start | bytes 245768 | tf_op jit(solution)/shard_map/ppermute | solution.py:447
  50.8 10.6 %all-to-all-start.1 = ((f32[8,32,384]{2,1,0:T(8,128)}), f32[8,32,384]{2,1,0:T(8,128)S(1)}, u32[]{:S(2)}, u32[]{:S(2)}) async-start(f32[8,32,384]{2,1,0:T(8,128)} %shard_map.57), calls=%async_computation.1 | async-start | bytes 786432 | tf_op jit(solution)/shard_map/all_to_all | solution.py:464
  54.4 7.0 %collective-permute-start.11 = (f32[2,32,512]{2,1,0:T(8,128)S(1)}, f32[2,32,512]{2,1,0:T(8,128)S(1)}, u32[]{:S(2)}, u32[]{:S(2)}) collective-permute-start(f32[2,32,512]{2,1,0:T(8,128)S(1)} %add.46.refs_0_), channel_id=1, source_target_pairs={{0,1},{1,0},{2,3},{3,2},{4,5},{5,4},{6,7},{7,6},{8,9},{9,8},{10,11... | collective-permute-start | bytes 393224 | tf_op jit(solution)/shard_map/ppermute | solution.py:447
  61.4 2.4 %collective-permute-start.13 = (f32[3,64,512]{2,1,0:T(8,128)S(1)}, f32[3,64,512]{2,1,0:T(8,128)S(1)}, u32[]{:S(2)}, u32[]{:S(2)}) collective-permute-start(f32[3,64,512]{2,1,0:T(8,128)S(1)} %get-tuple-element.106), channel_id=1, source_target_pairs={{0,2},{2,0},{1,3},{3,1},{4,6},{6,4},{5,7},{7,5},{8,10},{10,8},{9,1... | collective-permute-start | bytes 1179656 | tf_op jit(solution)/shard_map/ppermute | solution.py:447
  61.9 2.1 %collective-permute-start.12 = (f32[256,384]{1,0:T(8,128)S(1)}, f32[256,384]{1,0:T(8,128)S(1)}, u32[]{:S(2)}, u32[]{:S(2)}) collective-permute-start(f32[256,384]{1,0:T(8,128)S(1)} %bitcast.14), channel_id=1, source_target_pairs={{0,2},{2,0},{1,3},{3,1},{4,6},{6,4},{5,7},{7,5},{8,10},{10,8},{9,1... | collective-permute-start | bytes 1179656 | tf_op jit(solution)/shard_map/ppermute | solution.py:447
  64.1 9.0 %collective-permute-start.16 = (f32[2,64,512]{2,1,0:T(8,128)S(1)}, f32[2,64,512]{2,1,0:T(8,128)S(1)}, u32[]{:S(2)}, u32[]{:S(2)}) collective-permute-start(f32[2,64,512]{2,1,0:T(8,128)S(1)} %slice_add_fusion), channel_id=1, source_target_pairs={{0,1},{1,0},{2,3},{3,2},{4,5},{5,4},{6,7},{7,6},{8,9},{9,8},{10,11... | collective-permute-start | bytes 786440 | tf_op jit(solution)/shard_map/ppermute | solution.py:447
  74.8 6.3 %collective-permute-start.18 = (f32[128,256]{1,0:T(8,128)S(1)}, f32[128,256]{1,0:T(8,128)S(1)}, u32[]{:S(2)}, u32[]{:S(2)}) collective-permute-start(f32[128,256]{1,0:T(8,128)S(1)} %bitcast.25), channel_id=1, source_target_pairs={{0,1},{1,0},{2,3},{3,2},{4,5},{5,4},{6,7},{7,6},{8,9},{9,8},{10,11... | collective-permute-start | bytes 393224 | tf_op jit(solution)/shard_map/ppermute | solution.py:447
  81.0 5.3 %collective-permute-start.21 = (f32[1,64,512]{2,1,0:T(8,128)S(1)}, f32[1,64,512]{2,1,0:T(8,128)S(1)}, u32[]{:S(2)}, u32[]{:S(2)}) collective-permute-start(f32[1,64,512]{2,1,0:T(8,128)S(1)} %slice_add_fusion.1), channel_id=1, source_target_pairs={{0,1},{1,0},{2,3},{3,2},{4,5},{5,4},{6,7},{7,6},{8,9},{9,8},{10,11... | collective-permute-start | bytes 393224 | tf_op jit(solution)/shard_map/ppermute | solution.py:447
  82.2 7.4 %collective-permute-start.19 = (f32[2,128,128]{2,1,0:T(8,128)S(1)}, f32[2,128,128]{2,1,0:T(8,128)S(1)}, u32[]{:S(2)}, u32[]{:S(2)}) collective-permute-start(f32[2,128,128]{2,1,0:T(8,128)S(1)} %shard_map.64), channel_id=1, source_target_pairs={{0,12},{4,8},{8,4},{12,0},{1,13},{5,9},{9,5},{13,1},{2,14},{6,10},... | collective-permute-start | bytes 393224 | tf_op jit(solution)/shard_map/ppermute | solution.py:451
  84.6 10.1 %collective-permute-start.25 = (f32[2,64,512]{2,1,0:T(8,128)S(1)}, f32[2,64,512]{2,1,0:T(8,128)S(1)}, u32[]{:S(2)}, u32[]{:S(2)}) collective-permute-start(f32[2,64,512]{2,1,0:T(8,128)S(1)} %add.48.rows_mine), channel_id=1, source_target_pairs={{0,2},{2,0},{1,3},{3,1},{4,6},{6,4},{5,7},{7,5},{8,10},{10,8},{9,1... | collective-permute-start | bytes 786440 | tf_op jit(solution)/shard_map/ppermute | solution.py:447
  84.6 4.9 %collective-permute-start.20 = (f32[1,128,128]{2,1,0:T(8,128)S(1)}, f32[1,128,128]{2,1,0:T(8,128)S(1)}, u32[]{:S(2)}, u32[]{:S(2)}) collective-permute-start(f32[1,128,128]{2,1,0:T(8,128)S(1)} %slice.22), channel_id=1, source_target_pairs={{0,8},{8,0},{1,9},{9,1},{2,10},{10,2},{3,11},{11,3},{4,12},{12,4},... | collective-permute-start | bytes 196616 | tf_op jit(solution)/shard_map/ppermute | solution.py:447
  89.5 5.2 %collective-permute-start.22 = (f32[128,256]{1,0:T(8,128)S(1)}, f32[128,256]{1,0:T(8,128)S(1)}, u32[]{:S(2)}, u32[]{:S(2)}) collective-permute-start(f32[128,256]{1,0:T(8,128)S(1)} %bitcast.22), channel_id=1, source_target_pairs={{0,1},{1,0},{2,3},{3,2},{4,5},{5,4},{6,7},{7,6},{8,9},{9,8},{10,11... | collective-permute-start | bytes 393224 | tf_op jit(solution)/shard_map/ppermute | solution.py:447
  90.7 4.0 %collective-permute-start.26 = (f32[1,64,512]{2,1,0:T(8,128)S(1)}, f32[1,64,512]{2,1,0:T(8,128)S(1)}, u32[]{:S(2)}, u32[]{:S(2)}) collective-permute-start(f32[1,64,512]{2,1,0:T(8,128)S(1)} %add.50.last_mine), channel_id=1, source_target_pairs={{0,2},{2,0},{1,3},{3,1},{4,6},{6,4},{5,7},{7,5},{8,10},{10,8},{9,1... | collective-permute-start | bytes 393224 | tf_op jit(solution)/shard_map/ppermute | solution.py:447
  90.7 4.8 %collective-permute-start.23 = (f32[128,256]{1,0:T(8,128)S(1)}, f32[128,256]{1,0:T(8,128)S(1)}, u32[]{:S(2)}, u32[]{:S(2)}) collective-permute-start(f32[128,256]{1,0:T(8,128)S(1)} %bitcast.23), channel_id=1, source_target_pairs={{0,2},{2,0},{1,3},{3,1},{4,6},{6,4},{5,7},{7,5},{8,10},{10,8},{9,1... | collective-permute-start | bytes 393224 | tf_op jit(solution)/shard_map/ppermute | solution.py:447
  106.0 5.8 %collective-permute-start.28 = (f32[256,128]{1,0:T(8,128)S(1)}, f32[256,128]{1,0:T(8,128)S(1)}, u32[]{:S(2)}, u32[]{:S(2)}) collective-permute-start(f32[256,128]{1,0:T(8,128)S(1)} %add.51), channel_id=1, source_target_pairs={{0,1},{1,0},{2,3},{3,2},{4,5},{5,4},{6,7},{7,6},{8,9},{9,8},{10,11... | collective-permute-start | bytes 393224 | tf_op jit(solution)/shard_map/ppermute | solution.py:447
  111.9 5.3 %collective-permute-start.29 = (f32[256,128]{1,0:T(8,128)S(1)}, f32[256,128]{1,0:T(8,128)S(1)}, u32[]{:S(2)}, u32[]{:S(2)}) collective-permute-start(f32[256,128]{1,0:T(8,128)S(1)} %bitcast.20), channel_id=1, source_target_pairs={{0,4},{4,0},{1,5},{5,1},{2,6},{6,2},{3,7},{7,3},{8,12},{12,8},{9,1... | collective-permute-start | bytes 393224 | tf_op jit(solution)/shard_map/ppermute | solution.py:447
  (11 other events, 48.0 us)

commit v5 on v4

--- a/solution.py
+++ b/solution.py
@@ -499,6 +499,21 @@
     )(*pieces, inverse)
 
 
+def add_kernel(one_ref, two_ref, out_ref):
+    out_ref[...] = one_ref[...] + two_ref[...]
+
+
+def add_blocks(one, two):
+    return pl.pallas_call(
+        add_kernel,
+        out_shape=arr(*one.shape),
+        in_specs=[VMEM] * 2,
+        out_specs=VMEM,
+        compiler_params=SMALL,
+        cost_estimate=cost(10 ** 6, 10 ** 6),
+    )(one, two)
+
+
 def add_split_kernel(axis, one_ref, two_ref, kept_ref, sent_ref):
     half = kept_ref.shape[-2]
     first = lax.axis_index(axis) == 0
@@ -566,7 +581,7 @@
     pairs = chips_of(chips[2]) == 2
     if pairs:
         rest, moved = add_split(rest_kept, swap(rest_sent, "core"), "blk")
-        half_other, rest, moved = held(swap(half, "core"), rest, moved)
+        half_other, rest_kept, rest = held(swap(half, "core"), rest_kept, rest)
         moved = swap(moved, "blk")
     else:
         rest = rest_kept + swap(rest_sent, "core")
@@ -585,7 +600,7 @@
     sent, moved = held(sent, moved)
     received, skeleton_in = held(swap(sent, "core"), skeleton_0)
     inverse_0 = invert(skeleton_in)
-    terms = kept + received
+    terms = add_blocks(kept, received)
     rows_one = total_over(rest + moved if pairs else moved, ("n2",))
     pieces = exchange(to_chunks(terms, chips_of(chips[0])), chips[0])
     pieces, inverse_0 = held(pieces, inverse_0)
@@ -627,8 +642,9 @@
     if pairs:
         kept, sent = [part[0] for part in add_split(kept[None], received[None], "blk")]
         arrived = swap(sent, "blk")
-        arrived, inverse_1, last = held(arrived, inverse_1, last)
+        arrived, inverse_1 = held(arrived, inverse_1)
         sums = combine([kept[None], arrived[None]], inverse_1, [(0, [(0, 0), (1, 0)]), (1, [(0, 0), (1, 0)])])
+        sums, last = held(sums, last)
         far, beside = cross_swap(sums), swap(sums[:1], "n1")
         mine = fan_out([far, beside], [[[(0, 0), (1, 0)], [(0, 1)]]])[0]
         last = total_over(last, ("blk",))

time: 125 us -> 123 us (0.984)
  waiting for transfers between devices: 31.1 us -> 29.7 us
    ppermute x29, waiting for transfers between devices: 27.8 us -> 26.5 us  [swap(): return lax.ppermute(block, axis, [(0, 1), (1, 0)])]
  transfers between devices with their start and end apart: 33 -> 33, of which waited for: 20 -> 19; matrix products, arithmetic and copies ran while one was open for 0% -> 0% of each run, Pallas kernels for 32% -> 32%
where the time goes in v5:
time: 123 us
  Pallas kernels  57.4 us (47%)
  starting transfers between devices  34 us (28%)
  waiting for transfers between devices  29.7 us (24%)
    pallas_call x5, Pallas kernels, level_call(): pl.pallas_call(kernel, out_shape=outs, in_specs=specs, out_specs=[ANY if...  30.2 us
    ppermute x29, waiting for transfers between devices, swap(): return lax.ppermute(block, axis, [(0, 1), (1, 0)])  26.5 us
    ppermute x29, starting transfers between devices, swap(): return lax.ppermute(block, axis, [(0, 1), (1, 0)])  24 us
    pallas_call x3, Pallas kernels, pick(): pl.pallas_call(functools.partial(pick_kernel, wanted, sizes), out_shape=[...  10.3 us
    pallas_call x3, Pallas kernels, invert_first(): pl.pallas_call(first_half_kernel, out_shape=[square] * 2, in_specs=[VMEM]...  7.74 us
    all_to_all x2, starting transfers between devices, exchange(): return lax.all_to_all(pieces, axes, 0, 0, tiled=True)  7.55 us
    pallas_call x3, Pallas kernels, invert_second(): pl.pallas_call(second_half_kernel, out_shape=arr(*state.shape), in_specs=...  5.88 us
    ppermute x2, starting transfers between devices, cross_swap(): return lax.ppermute(block, ('n1', 'n2'), [(0, 3), (1, 2), (2, 1), (3, 0)])  2.52 us
  transfers between devices with their start and end apart: 33, of which 19 were waited for; matrix products, arithmetic and copies ran while one was open for 0% of the time, Pallas kernels for 32%

profile of v5, /device:TPU:0, one launch (start us, length us, event | category | flops | bytes accessed | tf_op | source)
XLA Modules:
  0.0 123.0 jit_solution(3230117827053918569)
XLA Ops:
  1.3 2.4 %shard_map.50 = (f32[1,64,512]{2,1,0:T(8,128)S(1)}, f32[1,64,512]{2,1,0:T(8,128)S(1)}) custom-call(s32[14,128]{1,0:T(8,128)S(1)} %copy-done, f32[3,896,512]{2,1,0:T(8,128)} %refs_11_.1), custom_call_target="tpu_custom_call" | custom-call | flops 1000000000 | bytes 1835008 | tf_op jit(solution)/shard_map/pallas_call | solution.py:233
  5.2 2.9 %collective-permute-start.1 = (f32[64,512]{1,0:T(8,128)S(1)}, f32[64,512]{1,0:T(8,128)S(1)}, u32[]{:S(2)}, u32[]{:S(2)}) collective-permute-start(f32[64,512]{1,0:T(8,128)S(1)} %bitcast_add_fusion), channel_id=1, source_target_pairs={{0,1},{1,0},{2,3},{3,2},{4,5},{5,4},{6,7},{7,6},{8,9},{9,8},{10,11... | collective-permute-start | bytes 393224 | tf_op jit(solution)/shard_map/ppermute | solution.py:447
  8.2 3.8 %collective-permute-done.1 = f32[64,512]{1,0:T(8,128)S(1)} collective-permute-done((f32[64,512]{1,0:T(8,128)S(1)}, f32[64,512]{1,0:T(8,128)S(1)}, u32[]{:S(2)}, u32[]{:S(2)}) %collective-permute-start.1) | collective-permute-done | bytes 131104 | tf_op jit(solution)/shard_map/ppermute | solution.py:447
  15.5 3.4 %shard_map.51 = (f32[2,64,512]{2,1,0:T(8,128)S(1)}, f32[2,64,512]{2,1,0:T(8,128)S(1)}) custom-call(s32[14,128]{1,0:T(8,128)S(1)} %copy-done, f32[3,896,512]{2,1,0:T(8,128)} %refs_11_.1, f32[3,896,512]{2,1,0:T(8,128)} %refs_11_.1), custom_call_target="tpu_custom_call" | custom-call | flops 2000000000 | bytes 3670016 | tf_op jit(solution)/shard_map/pallas_call | solution.py:233
  23.3 4.7 %shard_map.53 = (f32[128,512]{1,0:T(8,128)S(1)}, f32[896,128]{1,0:T(8,128)S(1)}, f32[256,384]{1,0:T(8,128)S(1)}, f32[256,384]{1,0:T(8,128)S(1)}) custom-call(f32[64,512]{1,0:T(8,128)S(1)} %add_add_fusion.mine_ref, f32[64,512]{1,0:T(8,128)S(1)} %collective-permute-done.5.other_ref, f32[3,896,512]{2,1,0:T(8,128)} %refs_11_.1, f32[3,896,512]{2,1,0:T(8,128)} %refs_12_.1), custom_call_target="tpu_custom_call" | custom-call | flops 3000000000 | bytes 4000000 | tf_op jit(solution)/shard_map/pallas_call | solution.py:424
  30.5 3.9 %all-to-all-start = ((f32[8,32,384]{2,1,0:T(8,128)}), f32[8,32,384]{2,1,0:T(8,128)S(1)}, u32[]{:S(2)}, u32[]{:S(2)}) async-start(f32[8,32,384]{2,1,0:T(8,128)} %bitcast.2), calls=%async_computation | async-start | bytes 786432 | tf_op jit(solution)/shard_map/all_to_all | solution.py:464
  34.4 2.1 %collective-permute-start.10 = (f32[2,32,512]{2,1,0:T(8,128)S(1)}, f32[2,32,512]{2,1,0:T(8,128)S(1)}, u32[]{:S(2)}, u32[]{:S(2)}) collective-permute-start(f32[2,32,512]{2,1,0:T(8,128)S(1)} %add.41), channel_id=1, source_target_pairs={{0,4},{4,0},{1,5},{5,1},{2,6},{6,2},{3,7},{7,3},{8,12},{12,8},{9,1... | collective-permute-start | bytes 393224 | tf_op jit(solution)/shard_map/ppermute | solution.py:447
  36.5 2.6 %shard_map.55 = (f32[128,128]{1,0:T(8,128)S(1)}, f32[128,128]{1,0:T(8,128)S(1)}) custom-call(f32[128,512]{1,0:T(8,128)S(1)} %get-tuple-element.91.skel_ref.refs_4_.skel0_ref), custom_call_target="tpu_custom_call" | custom-call | flops 100000000 | bytes 100000 | tf_op jit(solution)/shard_map/pallas_call | solution.py:164
  39.1 2.0 %shard_map.56.refs_1_.ours_ref.inverse_0 = f32[128,128]{1,0:T(8,128)S(1)} custom-call(f32[128,128]{1,0:T(8,128)S(1)} %get-tuple-element.92.a_ref, f32[128,128]{1,0:T(8,128)S(1)} %get-tuple-element.93.scales_ref), custom_call_target="tpu_custom_call" | custom-call | flops 100000000 | bytes 100000 | tf_op jit(solution)/shard_map/pallas_call | solution.py:171
  42.8 2.6 %collective-permute-start.9 = (f32[5,32,128]{2,1,0:T(8,128)S(1)}, f32[5,32,128]{2,1,0:T(8,128)S(1)}, u32[]{:S(2)}, u32[]{:S(2)}) collective-permute-start(f32[5,32,128]{2,1,0:T(8,128)S(1)} %shard_map.57), channel_id=1, source_target_pairs={{0,16},{16,0},{1,17},{17,1},{2,18},{18,2},{3,19},{19,3},{4,20},{20... | collective-permute-start | bytes 245768 | tf_op jit(solution)/shard_map/ppermute | solution.py:447
  45.5 3.6 %collective-permute-done.9.refs_0_ = f32[5,32,128]{2,1,0:T(8,128)S(1)} collective-permute-done((f32[5,32,128]{2,1,0:T(8,128)S(1)}, f32[5,32,128]{2,1,0:T(8,128)S(1)}, u32[]{:S(2)}, u32[]{:S(2)}) %collective-permute-start.9) | collective-permute-done | bytes 81952 | tf_op jit(solution)/shard_map/ppermute | solution.py:447
  49.9 3.6 %all-to-all-start.1 = ((f32[8,32,384]{2,1,0:T(8,128)}), f32[8,32,384]{2,1,0:T(8,128)S(1)}, u32[]{:S(2)}, u32[]{:S(2)}) async-start(f32[8,32,384]{2,1,0:T(8,128)} %shard_map.58), calls=%async_computation.1 | async-start | bytes 786432 | tf_op jit(solution)/shard_map/all_to_all | solution.py:464
  55.3 4.5 %shard_map.59 = (f32[3,64,512]{2,1,0:T(8,128)S(1)}, f32[3,64,512]{2,1,0:T(8,128)S(1)}) custom-call(s32[14,128]{1,0:T(8,128)S(1)} %copy-done.1, f32[3,896,512]{2,1,0:T(8,128)} %refs_11_.1, f32[3,896,512]{2,1,0:T(8,128)} %refs_11_.1, f32[3,896,512]{2,1,0:T(8,128)} %refs_11_.1), custom_call_target="tpu_custom_call" | custom-call | flops 3000000000 | bytes 5505024 | tf_op jit(solution)/shard_map/pallas_call | solution.py:233
  63.6 8.5 %shard_map.61 = (f32[128,128]{1,0:T(8,128)S(1)}, f32[128,128]{1,0:T(8,128)S(1)}, f32[128,512]{1,0:T(8,128)S(1)}, f32[128,128]{1,0:T(8,128)S(1)}, f32[896,128]{1,...) custom-call(f32[256,384]{1,0:T(8,128)S(1)} %bitcast.15, ...), custom_call_target="tpu_custom_call" | custom-call | flops 8000000000 | bytes 4000000 | tf_op jit(solution)/shard_map/pallas_call | solution.py:424
  75.5 2.6 %shard_map.63 = (f32[128,128]{1,0:T(8,128)S(1)}, f32[128,128]{1,0:T(8,128)S(1)}) custom-call(f32[128,512]{1,0:T(8,128)S(1)} %get-tuple-element.121.skel_ref.skel1_ref.refs_8_), custom_call_target="tpu_custom_call" | custom-call | flops 100000000 | bytes 100000 | tf_op jit(solution)/shard_map/pallas_call | solution.py:164
  78.1 2.0 %shard_map.64.refs_2_.refs_4_.inverse_1 = f32[128,128]{1,0:T(8,128)S(1)} custom-call(f32[128,128]{1,0:T(8,128)S(1)} %get-tuple-element.122.a_ref, f32[128,128]{1,0:T(8,128)S(1)} %get-tuple-element.123.scales_ref), custom_call_target="tpu_custom_call" | custom-call | flops 100000000 | bytes 100000 | tf_op jit(solution)/shard_map/pallas_call | solution.py:171
  81.3 2.4 %collective-permute-start.19 = (f32[2,128,128]{2,1,0:T(8,128)S(1)}, f32[2,128,128]{2,1,0:T(8,128)S(1)}, u32[]{:S(2)}, u32[]{:S(2)}) collective-permute-start(f32[2,128,128]{2,1,0:T(8,128)S(1)} %shard_map.65), channel_id=1, source_target_pairs={{0,12},{4,8},{8,4},{12,0},{1,13},{5,9},{9,5},{13,1},{2,14},{6,10},... | collective-permute-start | bytes 393224 | tf_op jit(solution)/shard_map/ppermute | solution.py:451
  85.6 3.0 %collective-permute-done.20.refs_1_ = f32[1,128,128]{2,1,0:T(8,128)S(1)} collective-permute-done((f32[1,128,128]{2,1,0:T(8,128)S(1)}, f32[1,128,128]{2,1,0:T(8,128)S(1)}, u32[]{:S(2)}, u32[]{:S(2)}) %collective-permute-start.20) | collective-permute-done | bytes 65568 | tf_op jit(solution)/shard_map/ppermute | solution.py:447
  90.3 3.5 %collective-permute-done.22.refs_1_ = f32[128,256]{1,0:T(8,128)S(1)} collective-permute-done((f32[128,256]{1,0:T(8,128)S(1)}, f32[128,256]{1,0:T(8,128)S(1)}, u32[]{:S(2)}, u32[]{:S(2)}) %collective-permute-start.22) | collective-permute-done | bytes 131104 | tf_op jit(solution)/shard_map/ppermute | solution.py:447
  95.1 8.5 %shard_map.68 = (f32[128,128]{1,0:T(8,128)S(1)}, f32[128,512]{1,0:T(8,128)S(1)}, f32[896,128]{1,0:T(8,128)S(1)}, f32[256,128]{1,0:T(8,128)S(1)}, f32[256,128]{1,0:T(8,128)S(1)}) custom-call(f32[128,256]{1,0:T(8,128)S(1)} %bitcast.24, f32[128,256]{1,0:T(8,128)S(1)} %collective-permute-done.22.refs_1_, f32[128,256]{1,0:T(8,128)S(1)} %collective-permute-done.23.refs_2_, ...), custom_call_target="tpu_custom_call" | custom-call | flops 8000000000 | bytes 4000000 | tf_op jit(solution)/shard_map/pallas_call | solution.py:424
  106.2 2.6 %shard_map.69 = (f32[128,128]{1,0:T(8,128)S(1)}, f32[128,128]{1,0:T(8,128)S(1)}) custom-call(f32[128,512]{1,0:T(8,128)S(1)} %get-tuple-element.142.skel_ref), custom_call_target="tpu_custom_call" | custom-call | flops 100000000 | bytes 100000 | tf_op jit(solution)/shard_map/pallas_call | solution.py:164
  108.8 2.0 %shard_map.70.refs_2_.inverse_2 = f32[128,128]{1,0:T(8,128)S(1)} custom-call(f32[128,128]{1,0:T(8,128)S(1)} %get-tuple-element.143.a_ref, f32[128,128]{1,0:T(8,128)S(1)} %get-tuple-element.144.scales_ref), custom_call_target="tpu_custom_call" | custom-call | flops 100000000 | bytes 100000 | tf_op jit(solution)/shard_map/pallas_call | solution.py:171
  111.6 3.2 %shard_map.72 = f32[3,896,128]{2,1,0:T(8,128)} custom-call(f32[896,128]{1,0:T(8,128)S(1)} %get-tuple-element.112.p0_hbm.refs_9_, f32[896,128]{1,0:T(8,128)S(1)} %get-tuple-element.137.refs_10_.p1_hbm, f32[896,128]{1,0:T(8,128)S(1)} %get-tuple-element.147.p2_hbm, f32[128,128]{1,0:T(8,128)S(1)} %shard_map.56.refs_1_.ours_ref.inverse_0, ...), custom_call_target="tpu_custom_call" | custom-call | flops 4000000000 | bytes 4000000 | tf_op jit(solution)/shard_map/pallas_call | solution.py:424
  117.6 5.3 %shard_map.73 = f32[3,1,128,128]{3,2,1,0:T(8,128)} custom-call(f32[256,128]{1,0:T(8,128)S(1)} %collective-permute-done.29.mine_ref, f32[256,128]{1,0:T(8,128)S(1)} %collective-permute-done.30.other_ref, f32[128,512]{1,0:T(8,128)S(1)} %get-tuple-element.142.skel_ref, f32[128,128]{1,0:T(8,128)S(1)} %get-tuple-element.150.c0_ref, ...), custom_call_target="tpu_custom_call" | custom-call | flops 5000000000 | bytes 4000000 | tf_op jit(solution)/shard_map/pallas_call | solution.py:424
  (81 shorter events, 36.5 us)
Async XLA Ops:
  5.2 6.7 %collective-permute-start.1 = (f32[64,512]{1,0:T(8,128)S(1)}, f32[64,512]{1,0:T(8,128)S(1)}, u32[]{:S(2)}, u32[]{:S(2)}) collective-permute-start(f32[64,512]{1,0:T(8,128)S(1)} %bitcast_add_fusion), channel_id=1, source_target_pairs={{0,1},{1,0},{2,3},{3,2},{4,5},{5,4},{6,7},{7,6},{8,9},{9,8},{10,11... | collective-permute-start | bytes 393224 | tf_op jit(solution)/shard_map/ppermute | solution.py:447
  12.0 7.1 %collective-permute-start.2 = (f32[64,512]{1,0:T(8,128)S(1)}, f32[64,512]{1,0:T(8,128)S(1)}, u32[]{:S(2)}, u32[]{:S(2)}) collective-permute-start(f32[64,512]{1,0:T(8,128)S(1)} %add.37), channel_id=1, source_target_pairs={{0,4},{4,0},{1,5},{5,1},{2,6},{6,2},{3,7},{7,3},{8,12},{12,8},{9,1... | collective-permute-start | bytes 393224 | tf_op jit(solution)/shard_map/ppermute | solution.py:447
  13.8 5.8 %collective-permute-start.3 = (f32[64,512]{1,0:T(8,128)S(1)}, f32[64,512]{1,0:T(8,128)S(1)}, u32[]{:S(2)}, u32[]{:S(2)}) collective-permute-start(f32[64,512]{1,0:T(8,128)S(1)} %add.37), channel_id=1, source_target_pairs={{0,8},{8,0},{1,9},{9,1},{2,10},{10,2},{3,11},{11,3},{4,12},{12,4},... | collective-permute-start | bytes 393224 | tf_op jit(solution)/shard_map/ppermute | solution.py:447
  15.4 5.9 %collective-permute-start.4 = (f32[64,512]{1,0:T(8,128)S(1)}, f32[64,512]{1,0:T(8,128)S(1)}, u32[]{:S(2)}, u32[]{:S(2)}) collective-permute-start(f32[64,512]{1,0:T(8,128)S(1)} %add.37), channel_id=1, source_target_pairs={{0,12},{4,8},{8,4},{12,0},{1,13},{5,9},{9,5},{13,1},{2,14},{6,10},... | collective-permute-start | bytes 393224 | tf_op jit(solution)/shard_map/ppermute | solution.py:451
  19.0 2.4 %collective-permute-start.6 = (f32[2,64,512]{2,1,0:T(8,128)S(1)}, f32[2,64,512]{2,1,0:T(8,128)S(1)}, u32[]{:S(2)}, u32[]{:S(2)}) collective-permute-start(f32[2,64,512]{2,1,0:T(8,128)S(1)} %get-tuple-element.82), channel_id=1, source_target_pairs={{0,2},{2,0},{1,3},{3,1},{4,6},{6,4},{5,7},{7,5},{8,10},{10,8},{9,1... | collective-permute-start | bytes 786440 | tf_op jit(solution)/shard_map/ppermute | solution.py:447
  21.5 6.5 %collective-permute-start.7 = (f32[2,32,512]{2,1,0:T(8,128)S(1)}, f32[2,32,512]{2,1,0:T(8,128)S(1)}, u32[]{:S(2)}, u32[]{:S(2)}) collective-permute-start(f32[2,32,512]{2,1,0:T(8,128)S(1)} %get-tuple-element.87), channel_id=1, source_target_pairs={{0,1},{1,0},{2,3},{3,2},{4,5},{5,4},{6,7},{7,6},{8,9},{9,8},{10,11... | collective-permute-start | bytes 393224 | tf_op jit(solution)/shard_map/ppermute | solution.py:447
  30.5 12.1 %all-to-all-start = ((f32[8,32,384]{2,1,0:T(8,128)}), f32[8,32,384]{2,1,0:T(8,128)S(1)}, u32[]{:S(2)}, u32[]{:S(2)}) async-start(f32[8,32,384]{2,1,0:T(8,128)} %bitcast.2), calls=%async_computation | async-start | bytes 786432 | tf_op jit(solution)/shard_map/all_to_all | solution.py:464
  34.4 11.0 %collective-permute-start.10 = (f32[2,32,512]{2,1,0:T(8,128)S(1)}, f32[2,32,512]{2,1,0:T(8,128)S(1)}, u32[]{:S(2)}, u32[]{:S(2)}) collective-permute-start(f32[2,32,512]{2,1,0:T(8,128)S(1)} %add.41), channel_id=1, source_target_pairs={{0,4},{4,0},{1,5},{5,1},{2,6},{6,2},{3,7},{7,3},{8,12},{12,8},{9,1... | collective-permute-start | bytes 393224 | tf_op jit(solution)/shard_map/ppermute | solution.py:447
  42.8 6.3 %collective-permute-start.9 = (f32[5,32,128]{2,1,0:T(8,128)S(1)}, f32[5,32,128]{2,1,0:T(8,128)S(1)}, u32[]{:S(2)}, u32[]{:S(2)}) collective-permute-start(f32[5,32,128]{2,1,0:T(8,128)S(1)} %shard_map.57), channel_id=1, source_target_pairs={{0,16},{16,0},{1,17},{17,1},{2,18},{18,2},{3,19},{19,3},{4,20},{20... | collective-permute-start | bytes 245768 | tf_op jit(solution)/shard_map/ppermute | solution.py:447
  49.9 10.6 %all-to-all-start.1 = ((f32[8,32,384]{2,1,0:T(8,128)}), f32[8,32,384]{2,1,0:T(8,128)S(1)}, u32[]{:S(2)}, u32[]{:S(2)}) async-start(f32[8,32,384]{2,1,0:T(8,128)} %shard_map.58), calls=%async_computation.1 | async-start | bytes 786432 | tf_op jit(solution)/shard_map/all_to_all | solution.py:464
  53.5 7.0 %collective-permute-start.11 = (f32[2,32,512]{2,1,0:T(8,128)S(1)}, f32[2,32,512]{2,1,0:T(8,128)S(1)}, u32[]{:S(2)}, u32[]{:S(2)}) collective-permute-start(f32[2,32,512]{2,1,0:T(8,128)S(1)} %add.42.refs_0_), channel_id=1, source_target_pairs={{0,1},{1,0},{2,3},{3,2},{4,5},{5,4},{6,7},{7,6},{8,9},{9,8},{10,11... | collective-permute-start | bytes 393224 | tf_op jit(solution)/shard_map/ppermute | solution.py:447
  60.5 2.4 %collective-permute-start.13 = (f32[3,64,512]{2,1,0:T(8,128)S(1)}, f32[3,64,512]{2,1,0:T(8,128)S(1)}, u32[]{:S(2)}, u32[]{:S(2)}) collective-permute-start(f32[3,64,512]{2,1,0:T(8,128)S(1)} %get-tuple-element.105), channel_id=1, source_target_pairs={{0,2},{2,0},{1,3},{3,1},{4,6},{6,4},{5,7},{7,5},{8,10},{10,8},{9,1... | collective-permute-start | bytes 1179656 | tf_op jit(solution)/shard_map/ppermute | solution.py:447
  61.0 2.1 %collective-permute-start.12 = (f32[256,384]{1,0:T(8,128)S(1)}, f32[256,384]{1,0:T(8,128)S(1)}, u32[]{:S(2)}, u32[]{:S(2)}) collective-permute-start(f32[256,384]{1,0:T(8,128)S(1)} %bitcast.14), channel_id=1, source_target_pairs={{0,2},{2,0},{1,3},{3,1},{4,6},{6,4},{5,7},{7,5},{8,10},{10,8},{9,1... | collective-permute-start | bytes 1179656 | tf_op jit(solution)/shard_map/ppermute | solution.py:447
  63.2 9.0 %collective-permute-start.16 = (f32[2,64,512]{2,1,0:T(8,128)S(1)}, f32[2,64,512]{2,1,0:T(8,128)S(1)}, u32[]{:S(2)}, u32[]{:S(2)}) collective-permute-start(f32[2,64,512]{2,1,0:T(8,128)S(1)} %slice_add_fusion), channel_id=1, source_target_pairs={{0,1},{1,0},{2,3},{3,2},{4,5},{5,4},{6,7},{7,6},{8,9},{9,8},{10,11... | collective-permute-start | bytes 786440 | tf_op jit(solution)/shard_map/ppermute | solution.py:447
  73.8 6.2 %collective-permute-start.18 = (f32[128,256]{1,0:T(8,128)S(1)}, f32[128,256]{1,0:T(8,128)S(1)}, u32[]{:S(2)}, u32[]{:S(2)}) collective-permute-start(f32[128,256]{1,0:T(8,128)S(1)} %bitcast.25), channel_id=1, source_target_pairs={{0,1},{1,0},{2,3},{3,2},{4,5},{5,4},{6,7},{7,6},{8,9},{9,8},{10,11... | collective-permute-start | bytes 393224 | tf_op jit(solution)/shard_map/ppermute | solution.py:447
  80.3 5.3 %collective-permute-start.21 = (f32[1,64,512]{2,1,0:T(8,128)S(1)}, f32[1,64,512]{2,1,0:T(8,128)S(1)}, u32[]{:S(2)}, u32[]{:S(2)}) collective-permute-start(f32[1,64,512]{2,1,0:T(8,128)S(1)} %slice_add_fusion.1), channel_id=1, source_target_pairs={{0,1},{1,0},{2,3},{3,2},{4,5},{5,4},{6,7},{7,6},{8,9},{9,8},{10,11... | collective-permute-start | bytes 393224 | tf_op jit(solution)/shard_map/ppermute | solution.py:447
  81.3 7.3 %collective-permute-start.19 = (f32[2,128,128]{2,1,0:T(8,128)S(1)}, f32[2,128,128]{2,1,0:T(8,128)S(1)}, u32[]{:S(2)}, u32[]{:S(2)}) collective-permute-start(f32[2,128,128]{2,1,0:T(8,128)S(1)} %shard_map.65), channel_id=1, source_target_pairs={{0,12},{4,8},{8,4},{12,0},{1,13},{5,9},{9,5},{13,1},{2,14},{6,10},... | collective-permute-start | bytes 393224 | tf_op jit(solution)/shard_map/ppermute | solution.py:451
  83.7 10.1 %collective-permute-start.25 = (f32[2,64,512]{2,1,0:T(8,128)S(1)}, f32[2,64,512]{2,1,0:T(8,128)S(1)}, u32[]{:S(2)}, u32[]{:S(2)}) collective-permute-start(f32[2,64,512]{2,1,0:T(8,128)S(1)} %add.44.rows_mine), channel_id=1, source_target_pairs={{0,2},{2,0},{1,3},{3,1},{4,6},{6,4},{5,7},{7,5},{8,10},{10,8},{9,1... | collective-permute-start | bytes 786440 | tf_op jit(solution)/shard_map/ppermute | solution.py:447
  83.7 4.9 %collective-permute-start.20 = (f32[1,128,128]{2,1,0:T(8,128)S(1)}, f32[1,128,128]{2,1,0:T(8,128)S(1)}, u32[]{:S(2)}, u32[]{:S(2)}) collective-permute-start(f32[1,128,128]{2,1,0:T(8,128)S(1)} %slice.19), channel_id=1, source_target_pairs={{0,8},{8,0},{1,9},{9,1},{2,10},{10,2},{3,11},{11,3},{4,12},{12,4},... | collective-permute-start | bytes 196616 | tf_op jit(solution)/shard_map/ppermute | solution.py:447
  88.6 5.2 %collective-permute-start.22 = (f32[128,256]{1,0:T(8,128)S(1)}, f32[128,256]{1,0:T(8,128)S(1)}, u32[]{:S(2)}, u32[]{:S(2)}) collective-permute-start(f32[128,256]{1,0:T(8,128)S(1)} %bitcast.22), channel_id=1, source_target_pairs={{0,1},{1,0},{2,3},{3,2},{4,5},{5,4},{6,7},{7,6},{8,9},{9,8},{10,11... | collective-permute-start | bytes 393224 | tf_op jit(solution)/shard_map/ppermute | solution.py:447
  89.7 4.0 %collective-permute-start.26 = (f32[1,64,512]{2,1,0:T(8,128)S(1)}, f32[1,64,512]{2,1,0:T(8,128)S(1)}, u32[]{:S(2)}, u32[]{:S(2)}) collective-permute-start(f32[1,64,512]{2,1,0:T(8,128)S(1)} %add.46.last_mine), channel_id=1, source_target_pairs={{0,2},{2,0},{1,3},{3,1},{4,6},{6,4},{5,7},{7,5},{8,10},{10,8},{9,1... | collective-permute-start | bytes 393224 | tf_op jit(solution)/shard_map/ppermute | solution.py:447
  89.8 4.8 %collective-permute-start.23 = (f32[128,256]{1,0:T(8,128)S(1)}, f32[128,256]{1,0:T(8,128)S(1)}, u32[]{:S(2)}, u32[]{:S(2)}) collective-permute-start(f32[128,256]{1,0:T(8,128)S(1)} %bitcast.23), channel_id=1, source_target_pairs={{0,2},{2,0},{1,3},{3,1},{4,6},{6,4},{5,7},{7,5},{8,10},{10,8},{9,1... | collective-permute-start | bytes 393224 | tf_op jit(solution)/shard_map/ppermute | solution.py:447
  105.0 5.7 %collective-permute-start.28 = (f32[256,128]{1,0:T(8,128)S(1)}, f32[256,128]{1,0:T(8,128)S(1)}, u32[]{:S(2)}, u32[]{:S(2)}) collective-permute-start(f32[256,128]{1,0:T(8,128)S(1)} %add.47), channel_id=1, source_target_pairs={{0,1},{1,0},{2,3},{3,2},{4,5},{5,4},{6,7},{7,6},{8,9},{9,8},{10,11... | collective-permute-start | bytes 393224 | tf_op jit(solution)/shard_map/ppermute | solution.py:447
  111.0 5.3 %collective-permute-start.29 = (f32[256,128]{1,0:T(8,128)S(1)}, f32[256,128]{1,0:T(8,128)S(1)}, u32[]{:S(2)}, u32[]{:S(2)}) collective-permute-start(f32[256,128]{1,0:T(8,128)S(1)} %bitcast.20), channel_id=1, source_target_pairs={{0,4},{4,0},{1,5},{5,1},{2,6},{6,2},{3,7},{7,3},{8,12},{12,8},{9,1... | collective-permute-start | bytes 393224 | tf_op jit(solution)/shard_map/ppermute | solution.py:447
  (11 other events, 47.1 us)
